TPU v7x, 512 devices: a whole 4x4x16 slice. The times are simulated.
512 devices in a mesh: layer: 4 (over y), prow: 16 (over z), pcol: 8 (over x, core).
Axes of the slice: x: 4, y: 4, z: 16, core: 2. Of those that a mesh axis runs over, the one named last changes fastest.
Arguments:
- own_blocks: bfloat16 [4, 21, 16, 128, 2, 8, 128], P('layer', None, 'prow', None, None, 'pcol'), may hold values from -0.046875 to 0.046875
- own_pattern: int32 [4, 21, 16, 2, 8], P('layer', None, 'prow', None, 'pcol'), may hold values 0 or 1
- own_inverse: bfloat16 [4, 3, 16, 128, 2, 8, 128], P('layer', None, 'prow', None, None, 'pcol'), as said below
- pair_blocks: bfloat16 [4, 12, 16, 128, 2, 8, 128], P('layer', None, 'prow', None, None, 'pcol'), as said below
- pair_inverse: bfloat16 [4, 3, 16, 128, 2, 8, 128], P('layer', None, 'prow', None, None, 'pcol'), as said below
- root_blocks: bfloat16 [3, 16, 128, 2, 8, 128], P(None, 'prow', None, None, 'pcol'), may hold values from -0.046875 to 0.046875
- root_inverse: bfloat16 [3, 16, 128, 2, 8, 128], P(None, 'prow', None, None, 'pcol'), as said below
- own_rhs: bfloat16 [4, 3, 16, 128, 256], P('layer', None, 'prow'), may hold values from -6 to 6
- shared_rhs: bfloat16 [4, 6, 16, 128, 256], P('layer', None, 'prow'), may hold values from -3 to 3
Outputs:
- own_solution: bfloat16 [4, 3, 2, 8, 128, 256], P('layer', None, None, 'pcol')
- pair_solution: bfloat16 [4, 3, 2, 8, 128, 256], P('layer', None, None, 'pcol')
- root_solution: bfloat16 [4, 3, 2, 8, 128, 256], P('layer', None, None, 'pcol')
Inputs may be any that keep to these rules, and one draw needn't show every extreme that they name: `pair_blocks`: layers 2m and 2m+1 hold equal copies of their parent's blocks. `pair_inverse`: each panel's inverse is lower triangular; layers 2m and 2m+1 hold equal copies. `own_inverse`: each panel's inverse is lower triangular. `root_inverse`: each panel's inverse is lower triangular.
All inputs are finite; a program needn't handle non-finite values. No bound on the sum of `own_pattern` on one device may be relied on, other than what follows from the above.
Results may differ from a plain program's by a relative error of at most 0.038.
Values may be sent and summed in bfloat16 or wider, within the bound.
No kernel may reach another device: no remote copies, remote signals or barrier semaphores. Data moves between devices by JAX's collectives and lax.ppermute only.
A program may use at most 64 MiB of HBM per device.

v0:
```python
import jax
import jax.numpy as jnp
from jax import lax
from jax.sharding import PartitionSpec as P


def from_partner(array, axis, apart):
    return lax.ppermute(array, axis, [(i, i ^ 1 << apart) for i in range(lax.axis_size(axis))])


def column_product(stacked, solved):
    block_count, row_count, col_width = stacked.shape
    flattened = stacked.reshape(block_count * row_count, col_width)
    product = jnp.dot(flattened, solved, preferred_element_type=jnp.float32)
    return product.reshape(block_count, row_count, solved.shape[1])


def row_total(partial_value):
    return lax.psum(partial_value.astype(jnp.bfloat16), "pcol").astype(jnp.float32)


def panel_solve(residual, inverse):
    rounded = residual.astype(jnp.bfloat16)
    partial_value = lax.dot_general(
        inverse, rounded, (((0,), (0,)), ((), ())), preferred_element_type=jnp.float32
    )
    return lax.psum(partial_value.astype(jnp.bfloat16), "prow")


def forward_solve(
    own_cols, own_inv, pair_cols, pair_inv, root_cols, root_inv, own_rows, shared_rows
):
    panels = own_inv.shape[0]
    chain_length = 3 * panels
    first_col = lax.axis_index("pcol") == 0
    solved = []
    updates_sum = jnp.zeros((chain_length,) + own_rows.shape[1:], jnp.float32)
    offset = 0
    for step_index in range(panels):
        residual = own_rows[step_index].astype(jnp.float32)
        if step_index > 0:
            residual = residual + row_total(-updates_sum[step_index])
        panel_result = panel_solve(residual, own_inv[step_index])
        solved.append(panel_result)
        block_count = chain_length - 1 - step_index
        update = column_product(own_cols[offset : offset + block_count], panel_result)
        updates_sum = updates_sum.at[step_index + 1 :].add(update)
        offset += block_count
    ancestors = jnp.where(first_col, shared_rows.astype(jnp.float32), 0.0) - updates_sum[panels:]
    ancestors = ancestors + from_partner(ancestors.astype(jnp.bfloat16), "layer", 0).astype(
        ancestors.dtype
    )
    parent_part = ancestors[:panels]
    inner_sums = jnp.zeros_like(ancestors)
    offset = 0
    for step_index in range(panels):
        residual = row_total(parent_part[step_index] - inner_sums[step_index])
        panel_result = panel_solve(residual, pair_inv[step_index])
        solved.append(panel_result)
        block_count = 2 * panels - 1 - step_index
        update = column_product(pair_cols[offset : offset + block_count], panel_result)
        inner_sums = inner_sums.at[step_index + 1 :].add(update)
        offset += block_count
    joined = ancestors[panels:] - inner_sums[panels:]
    joined = joined + from_partner(joined.astype(jnp.bfloat16), "layer", 1).astype(joined.dtype)
    root_sums = jnp.zeros_like(joined)
    offset = 0
    for step_index in range(panels):
        residual = row_total(joined[step_index] - root_sums[step_index])
        panel_result = panel_solve(residual, root_inv[step_index])
        solved.append(panel_result)
        block_count = panels - 1 - step_index
        if block_count > 0:
            update = column_product(root_cols[offset : offset + block_count], panel_result)
            root_sums = root_sums.at[step_index + 1 :].add(update)
            offset += block_count
    return solved


def local(
    own_blocks,
    own_pattern,
    own_inverse,
    pair_blocks,
    pair_inverse,
    root_blocks,
    root_inverse,
    own_rhs,
    shared_rhs,
):
    tile_rows = own_blocks.shape[3]
    cycles = own_blocks.shape[4]
    col_width = cycles * tile_rows
    rhs_width = own_rhs.shape[-1]
    own_tiles = own_blocks.reshape(-1, tile_rows, cycles, tile_rows)
    kept_tiles = own_pattern.reshape(-1, 1, cycles, 1) > 0
    own_cols = jnp.where(kept_tiles, own_tiles, jnp.zeros((), own_tiles.dtype)).reshape(
        -1, tile_rows, col_width
    )
    pair_cols = pair_blocks.reshape(-1, tile_rows, col_width)
    root_cols = root_blocks.reshape(-1, tile_rows, col_width)
    own_inv = own_inverse.reshape(-1, tile_rows, col_width)
    pair_inv = pair_inverse.reshape(-1, tile_rows, col_width)
    root_inv = root_inverse.reshape(-1, tile_rows, col_width)
    own_rows = own_rhs.reshape(-1, tile_rows, rhs_width)
    shared_rows = shared_rhs.reshape(-1, tile_rows, rhs_width)
    panels = own_inv.shape[0]
    solved = jnp.stack(
        forward_solve(
            own_cols, own_inv, pair_cols, pair_inv, root_cols, root_inv, own_rows, shared_rows
        )
    )
    solved = solved.reshape(3 * panels, cycles, 1, tile_rows, rhs_width)
    return (solved[:panels][None], solved[panels : 2 * panels][None], solved[2 * panels :][None])


def solution(mesh):
    return jax.shard_map(
        local,
        mesh=mesh,
        in_specs=(
            P("layer", None, "prow", None, None, "pcol", None),
            P("layer", None, "prow", None, "pcol"),
            P("layer", None, "prow", None, None, "pcol", None),
            P("layer", None, "prow", None, None, "pcol", None),
            P("layer", None, "prow", None, None, "pcol", None),
            P(None, "prow", None, None, "pcol", None),
            P(None, "prow", None, None, "pcol", None),
            P("layer", None, "prow", None, None),
            P("layer", None, "prow", None, None),
        ),
        out_specs=(
            P("layer", None, None, "pcol", None, None),
            P("layer", None, None, "pcol", None, None),
            P("layer", None, None, "pcol", None, None),
        ),
        check_vma=False,
    )
```

profile of v0, /device:TPU:2, one launch (start us, length us, event | category | flops | bytes accessed | tf_op | source)
XLA Modules:
  0.0 1858.6 jit_solution(14308534549543791466)
XLA Ops:
  7.2 1.0 fusion.71
  8.3 1.7 convolution_convert_fusion.8
  10.0 0.7 broadcast_compare_fusion
  10.7 0.1 copy.35
  10.8 2.5 broadcast_select_fusion
  13.4 0.4 slice.373
  13.8 0.3 dot_general.68
  14.1 135.7 %all-reduce.18.cloned.1.call-done = bf16[256,256]{1,0:T(8,128)(2,1)} async-done(((bf16[256,256]{1,0:T(8,128)(2,1)}), bf16[256,256]{1,0:T(8,128)(2,1)}) %all-reduce.18.cloned.1.call-update) | async-done | bytes 131088 | tf_op jit(solution)/shard_map/psum | solution.py:27
  149.8 1.2 fusion.32
  151.0 0.6 fusion.36
  151.7 70.0 %all-reduce.20.cloned.1.call-done = bf16[128,256]{1,0:T(8,128)(2,1)} async-done(((bf16[128,256]{1,0:T(8,128)(2,1)}), bf16[128,256]{1,0:T(8,128)(2,1)}) %all-reduce.20.cloned.1.call-update) | async-done | bytes 65552 | tf_op jit(solution)/shard_map/psum | solution.py:19
  221.8 1.7 fusion.3
  223.6 0.3 slice.376
  223.9 1.1 dot_general.71
  225.0 135.4 %all-reduce.22.cloned.1.call-done = bf16[256,256]{0,1:T(8,128)(2,1)} async-done(((bf16[256,256]{0,1:T(8,128)(2,1)}), bf16[256,256]{0,1:T(8,128)(2,1)}) %all-reduce.22.cloned.1.call-update) | async-done | bytes 131088 | tf_op jit(solution)/shard_map/psum | solution.py:27
  360.4 1.4 convolution_add_fusion
  361.8 0.6 fusion.37
  362.5 69.7 %all-reduce.24.cloned.1.call-done = bf16[128,256]{1,0:T(8,128)(2,1)} async-done(((bf16[128,256]{1,0:T(8,128)(2,1)}), bf16[128,256]{1,0:T(8,128)(2,1)}) %all-reduce.24.cloned.1.call-update) | async-done | bytes 65552 | tf_op jit(solution)/shard_map/psum | solution.py:19
  432.2 1.7 fusion.4
  434.0 0.3 slice.379
  434.3 0.3 dot_general.74
  434.5 136.1 %all-reduce.26.cloned.1.call-done = bf16[256,256]{0,1:T(8,128)(2,1)} async-done(((bf16[256,256]{0,1:T(8,128)(2,1)}), bf16[256,256]{0,1:T(8,128)(2,1)}) %all-reduce.26.cloned.1.call-update) | async-done | bytes 131088 | tf_op jit(solution)/shard_map/psum | solution.py:27
  570.6 1.2 fusion.72
  571.9 3.5 collective-permute-start
  575.4 6.3 collective-permute-done
  581.7 0.6 fusion.38
  582.5 0.1 fusion.70
  582.6 68.9 %all-reduce.28.cloned.1.call-done = bf16[128,256]{1,0:T(8,128)(2,1)} async-done(((bf16[128,256]{1,0:T(8,128)(2,1)}), bf16[128,256]{1,0:T(8,128)(2,1)}) %all-reduce.28.cloned.1.call-update) | async-done | bytes 65552 | tf_op jit(solution)/shard_map/psum | solution.py:19
  651.5 1.7 fusion.5
  653.3 136.8 %all-reduce.30.cloned.1.call-done = bf16[256,256]{0,1:T(8,128)(2,1)} async-done(((bf16[256,256]{0,1:T(8,128)(2,1)}), bf16[256,256]{0,1:T(8,128)(2,1)}) %all-reduce.30.cloned.1.call-update) | async-done | bytes 131088 | tf_op jit(solution)/shard_map/psum | solution.py:27
  790.1 1.2 convolution_bitcast_fusion
  791.3 0.6 fusion.25
  792.0 70.0 %all-reduce.32.cloned.1.call-done = bf16[128,256]{1,0:T(8,128)(2,1)} async-done(((bf16[128,256]{1,0:T(8,128)(2,1)}), bf16[128,256]{1,0:T(8,128)(2,1)}) %all-reduce.32.cloned.1.call-update) | async-done | bytes 65552 | tf_op jit(solution)/shard_map/psum | solution.py:19
  862.0 1.7 fusion.6
  863.8 136.8 %all-reduce.34.cloned.1.call-done = bf16[256,256]{0,1:T(8,128)(2,1)} async-done(((bf16[256,256]{0,1:T(8,128)(2,1)}), bf16[256,256]{0,1:T(8,128)(2,1)}) %all-reduce.34.cloned.1.call-update) | async-done | bytes 131088 | tf_op jit(solution)/shard_map/psum | solution.py:27
  1000.6 1.2 fusion.1
  1001.8 0.6 fusion.39
  1002.5 69.9 %all-reduce.36.cloned.1.call-done = bf16[128,256]{1,0:T(8,128)(2,1)} async-done(((bf16[128,256]{1,0:T(8,128)(2,1)}), bf16[128,256]{1,0:T(8,128)(2,1)}) %all-reduce.36.cloned.1.call-update) | async-done | bytes 65552 | tf_op jit(solution)/shard_map/psum | solution.py:19
  1072.4 1.7 fusion.7
  1074.2 136.8 %all-reduce.38.cloned.1.call-done = bf16[256,256]{0,1:T(8,128)(2,1)} async-done(((bf16[256,256]{0,1:T(8,128)(2,1)}), bf16[256,256]{0,1:T(8,128)(2,1)}) %all-reduce.38.cloned.1.call-update) | async-done | bytes 131088 | tf_op jit(solution)/shard_map/psum | solution.py:27
  1211.0 1.1 fusion.2
  1212.3 5.0 collective-permute-start.1
  1217.3 4.1 collective-permute-done.1
  1221.6 0.6 fusion.40
  1222.3 0.1 fusion.69
  1222.5 68.8 %all-reduce.40.cloned.1.call-done = bf16[128,256]{1,0:T(8,128)(2,1)} async-done(((bf16[128,256]{1,0:T(8,128)(2,1)}), bf16[128,256]{1,0:T(8,128)(2,1)}) %all-reduce.40.cloned.1.call-update) | async-done | bytes 65552 | tf_op jit(solution)/shard_map/psum | solution.py:19
  1291.3 1.7 fusion.8
  1293.1 136.8 %all-reduce.42.cloned.1.call-done = bf16[256,256]{0,1:T(8,128)(2,1)} async-done(((bf16[256,256]{0,1:T(8,128)(2,1)}), bf16[256,256]{0,1:T(8,128)(2,1)}) %all-reduce.42.cloned.1.call-update) | async-done | bytes 131088 | tf_op jit(solution)/shard_map/psum | solution.py:27
  1429.9 1.2 convolution_bitcast_fusion.3
  1431.1 0.6 fusion.22
  1431.8 69.9 %all-reduce.44.cloned.1.call-done = bf16[128,256]{1,0:T(8,128)(2,1)} async-done(((bf16[128,256]{1,0:T(8,128)(2,1)}), bf16[128,256]{1,0:T(8,128)(2,1)}) %all-reduce.44.cloned.1.call-update) | async-done | bytes 65552 | tf_op jit(solution)/shard_map/psum | solution.py:19
  1501.7 1.7 fusion.9
  1503.5 136.6 %all-reduce.46.cloned.1.call-done = bf16[256,256]{0,1:T(8,128)(2,1)} async-done(((bf16[256,256]{0,1:T(8,128)(2,1)}), bf16[256,256]{0,1:T(8,128)(2,1)}) %all-reduce.46.cloned.1.call-update) | async-done | bytes 131088 | tf_op jit(solution)/shard_map/psum | solution.py:27
  1640.2 1.8 fusion.21
  1642.0 0.1 copy.36
  1642.1 0.1 copy.38
  1642.2 69.7 %all-reduce.48.cloned.1.call-done = bf16[128,256]{1,0:T(8,128)(2,1)} async-done(((bf16[128,256]{1,0:T(8,128)(2,1)}), bf16[128,256]{1,0:T(8,128)(2,1)}) %all-reduce.48.cloned.1.call-update) | async-done | bytes 65552 | tf_op jit(solution)/shard_map/psum | solution.py:19
  1711.9 1.8 convolution_convert_fusion
  1713.7 0.8 pad_maximum_fusion
  1714.7 0.1 copy.41
  1714.8 0.1 copy.42
  1714.9 0.8 pad_maximum_fusion.1
  1715.9 134.5 %all-reduce.50.cloned.1.call-done = bf16[1,1,2,1,128,256]{5,4,3,2,1,0:T(8,128)(2,1)} async-done(((bf16[1,1,2,1,128,256]{5,4,3,2,1,0:T(8,128)(2,1)}), bf16[1,1,2,1,128,256]{5,4,3,2,1,0:T(8,128)(2,1)}) %all-reduce.50.cloned.1.call-update) | async-done | bytes 131088 | tf_op jit(solution)/shard_map/psum | solution.py:27
  1850.4 1.7 pad_maximum_fusion.2
  (72 shorter events, 1.6 us)
Async XLA Ops:
  7.2 142.7 %all-reduce.18.cloned.1.call-start = ((), (), s32[]{:S(2)}) async-start(), calls=%async_computation | async-start | bytes 262144 | tf_op jit(solution)/shard_map/psum | solution.py:27
  10.0 211.8 %all-reduce.20.cloned.1.call-start = ((), (), s32[]{:S(2)}) async-start(), calls=%async_computation.1 | async-start | bytes 131072 | tf_op jit(solution)/shard_map/psum | solution.py:19
  151.7 208.7 %all-reduce.22.cloned.1.call-start = ((), (), s32[]{:S(2)}) async-start(), calls=%async_computation.2 | async-start | bytes 262144 | tf_op jit(solution)/shard_map/psum | solution.py:27
  223.5 208.6 %all-reduce.24.cloned.1.call-start = ((), (), s32[]{:S(2)}) async-start(), calls=%async_computation.3 | async-start | bytes 131072 | tf_op jit(solution)/shard_map/psum | solution.py:19
  361.7 208.9 %copy-start.8 = (bf16[1,6,1,128,256]{4,3,2,1,0:T(8,128)(2,1)S(1)}, bf16[1,6,1,128,256]{4,3,2,1,0:T(8,128)(2,1)}, u32[]{:S(2)}) copy-start(bf16[1,6,1,128,256]{4,3,2,1,0:T(8,128)(2,1)} %param.33) | copy-start | bytes 1179652
  362.4 208.2 %all-reduce.26.cloned.1.call-start = ((), (), s32[]{:S(2)}) async-start(), calls=%async_computation.4 | async-start | bytes 262144 | tf_op jit(solution)/shard_map/psum | solution.py:27
  433.9 217.5 %all-reduce.28.cloned.1.call-start = ((), (), s32[]{:S(2)}) async-start(), calls=%async_computation.5 | async-start | bytes 131072 | tf_op jit(solution)/shard_map/psum | solution.py:19
  571.8 10.6 copy-start.9
  571.9 9.8 collective-permute-start
  581.7 208.4 %slice-start = ((bf16[1,12,1,128,2,1,128]{6,4,5,3,2,1,0:T(2,128)(2,1)}), bf16[1,5,1,128,2,1,128]{6,4,5,3,2,1,0:T(2,128)(2,1)S(1)}, s32[]{:S(2)}) async-start(bf16[1,12,1,128,2,1,128]{6,4,5,3,2,1,0:T(2,128)(2,1)} %param.28), calls=%async_computation.17 | async-start | bytes 655360 | tf_op jit(solution)/shard_map/slice | solution.py:61
  582.4 207.7 %all-reduce.30.cloned.1.call-start = ((), (), s32[]{:S(2)}) async-start(), calls=%async_computation.6 | async-start | bytes 262144 | tf_op jit(solution)/shard_map/psum | solution.py:27
  653.2 208.8 %all-reduce.32.cloned.1.call-start = ((), (), s32[]{:S(2)}) async-start(), calls=%async_computation.7 | async-start | bytes 131072 | tf_op jit(solution)/shard_map/psum | solution.py:19
  653.2 347.4 %slice-start.1 = ((bf16[1,12,1,128,2,1,128]{6,4,5,3,2,1,0:T(2,128)(2,1)}), bf16[1,4,1,128,2,1,128]{6,4,5,3,2,1,0:T(2,128)(2,1)S(1)}, s32[]{:S(2)}) async-start(bf16[1,12,1,128,2,1,128]{6,4,5,3,2,1,0:T(2,128)(2,1)} %param.28), calls=%async_computation.18 | async-start | bytes 524288 | tf_op jit(solution)/shard_map/slice | solution.py:61
  791.9 208.7 %all-reduce.34.cloned.1.call-start = ((), (), s32[]{:S(2)}) async-start(), calls=%async_computation.8 | async-start | bytes 262144 | tf_op jit(solution)/shard_map/psum | solution.py:27
  863.7 208.7 %all-reduce.36.cloned.1.call-start = ((), (), s32[]{:S(2)}) async-start(), calls=%async_computation.9 | async-start | bytes 131072 | tf_op jit(solution)/shard_map/psum | solution.py:19
  863.8 347.2 %slice-start.2 = ((bf16[1,12,1,128,2,1,128]{6,4,5,3,2,1,0:T(2,128)(2,1)}), bf16[1,3,1,128,2,1,128]{6,4,5,3,2,1,0:T(2,128)(2,1)S(1)}, s32[]{:S(2)}) async-start(bf16[1,12,1,128,2,1,128]{6,4,5,3,2,1,0:T(2,128)(2,1)} %param.28), calls=%async_computation.19 | async-start | bytes 393216 | tf_op jit(solution)/shard_map/slice | solution.py:61
  1002.5 208.6 %all-reduce.38.cloned.1.call-start = ((), (), s32[]{:S(2)}) async-start(), calls=%async_computation.10 | async-start | bytes 262144 | tf_op jit(solution)/shard_map/psum | solution.py:27
  1074.1 217.2 %all-reduce.40.cloned.1.call-start = ((), (), s32[]{:S(2)}) async-start(), calls=%async_computation.11 | async-start | bytes 131072 | tf_op jit(solution)/shard_map/psum | solution.py:19
  1212.2 10.1 copy-start.10
  1212.3 217.6 %slice-start.3 = ((bf16[3,1,128,2,1,128]{5,3,4,2,1,0:T(2,128)(2,1)}), bf16[2,1,128,2,1,128]{5,3,4,2,1,0:T(2,128)(2,1)S(1)}, s32[]{:S(2)}) async-start(bf16[3,1,128,2,1,128]{5,3,4,2,1,0:T(2,128)(2,1)} %param.30), calls=%async_computation.20 | async-start | bytes 262144 | tf_op jit(solution)/shard_map/slice | solution.py:74
  1212.3 9.2 collective-permute-start.1
  1221.6 418.6 %slice-start.4 = ((bf16[3,1,128,2,1,128]{5,3,4,2,1,0:T(2,128)(2,1)}), bf16[1,1,128,2,1,128]{5,3,4,2,1,0:T(2,128)(2,1)S(1)}, s32[]{:S(2)}) async-start(bf16[3,1,128,2,1,128]{5,3,4,2,1,0:T(2,128)(2,1)} %param.30), calls=%async_computation.21 | async-start | bytes 131072 | tf_op jit(solution)/shard_map/slice | solution.py:74
  1222.2 207.7 %all-reduce.42.cloned.1.call-start = ((), (), s32[]{:S(2)}) async-start(), calls=%async_computation.12 | async-start | bytes 262144 | tf_op jit(solution)/shard_map/psum | solution.py:27
  1222.4 419.6 %copy-start = (bf16[256,256]{0,1:T(8,128)(2,1)S(1)}, bf16[256,256]{0,1:T(8,128)(2,1)}, u32[]{:S(2)}) copy-start(bf16[256,256]{0,1:T(8,128)(2,1)} %all-reduce.22.cloned.1.call-done) | copy-start | bytes 393220
  1293.0 349.1 %copy-start.1 = (bf16[256,256]{0,1:T(8,128)(2,1)S(1)}, bf16[256,256]{0,1:T(8,128)(2,1)}, u32[]{:S(2)}) copy-start(bf16[256,256]{0,1:T(8,128)(2,1)} %all-reduce.26.cloned.1.call-done) | copy-start | bytes 393220
  1293.0 208.7 %all-reduce.44.cloned.1.call-start = ((), (), s32[]{:S(2)}) async-start(), calls=%async_computation.13 | async-start | bytes 131072 | tf_op jit(solution)/shard_map/psum | solution.py:19
  1429.9 283.8 %copy-start.7 = (bf16[256,256]{1,0:T(8,128)(2,1)S(1)}, bf16[256,256]{1,0:T(8,128)(2,1)}, u32[]{:S(2)}) copy-start(bf16[256,256]{1,0:T(8,128)(2,1)} %all-reduce.18.cloned.1.call-done) | copy-start | bytes 393220
  1431.7 208.4 %all-reduce.46.cloned.1.call-start = ((), (), s32[]{:S(2)}) async-start(), calls=%async_computation.14 | async-start | bytes 262144 | tf_op jit(solution)/shard_map/psum | solution.py:27
  1501.7 212.8 %copy-start.2 = (bf16[256,256]{0,1:T(8,128)(2,1)S(1)}, bf16[256,256]{0,1:T(8,128)(2,1)}, u32[]{:S(2)}) copy-start(bf16[256,256]{0,1:T(8,128)(2,1)} %all-reduce.30.cloned.1.call-done) | copy-start | bytes 393220
  1503.5 211.2 %copy-start.6 = (bf16[256,256]{0,1:T(8,128)(2,1)S(1)}, bf16[256,256]{0,1:T(8,128)(2,1)}, u32[]{:S(2)}) copy-start(bf16[256,256]{0,1:T(8,128)(2,1)} %all-reduce.34.cloned.1.call-done) | copy-start | bytes 393220
  1503.5 208.5 %all-reduce.48.cloned.1.call-start = ((), (), s32[]{:S(2)}) async-start(), calls=%async_computation.15 | async-start | bytes 131072 | tf_op jit(solution)/shard_map/psum | solution.py:19
  1640.2 74.6 %copy-start.3 = (bf16[256,256]{0,1:T(8,128)(2,1)S(1)}, bf16[256,256]{0,1:T(8,128)(2,1)}, u32[]{:S(2)}) copy-start(bf16[256,256]{0,1:T(8,128)(2,1)} %all-reduce.38.cloned.1.call-done) | copy-start | bytes 393220
  1642.0 208.4 %all-reduce.50.cloned.1.call-start = ((), (), s32[]{:S(2)}) async-start(), calls=%async_computation.16 | async-start | bytes 262144 | tf_op jit(solution)/shard_map/psum | solution.py:27
  1711.9 3.7 copy-start.4
  1713.7 2.1 copy-start.5
Sparse Core Ops, SparseCore 0:
  10.9 138.9 all-reduce.17
  152.8 68.9 all-reduce.19
  224.6 135.6 all-reduce.21
  363.2 68.9 all-reduce.23
  434.9 135.6 all-reduce.25
  582.5 68.8 all-reduce.27
  654.3 135.6 all-reduce.29
  793.1 68.9 all-reduce.31
  864.9 135.6 all-reduce.33
  1003.5 68.9 all-reduce.35
  1075.3 135.6 all-reduce.37
  1222.4 68.8 all-reduce.39
  1294.2 135.6 all-reduce.41
  1432.7 68.9 all-reduce.43
  1504.4 135.6 all-reduce.45
  1643.0 68.9 all-reduce.47
  1714.7 135.6 all-reduce.49
where the time goes:
time: 1860 us
  waiting for transfers between devices  1790 us (96%)
  matrix products  25.7 us (1%)
    psum x9, waiting for transfers between devices, panel_solve(): return lax.psum(partial_value.astype(jnp.bfloat16), 'prow')  1230 us
    psum x8, waiting for transfers between devices, row_total(): lax.psum(partial_value.astype(jnp.bfloat16), 'pcol').astype(jnp.float32)  557 us
  transfers between devices with their start and end apart: 19, of which 19 were waited for; matrix products, arithmetic and copies ran while one was open for 0% of the time, Pallas kernels for 0%

commit v1 on v0

--- a/solution.py
+++ b/solution.py
@@ -15,8 +15,23 @@
     return product.reshape(block_count, row_count, solved.shape[1])
 
 
+def shared_with_all(value, axis):
+    copies = jnp.broadcast_to(value[None], (lax.axis_size(axis),) + value.shape)
+    return lax.all_to_all(copies, axis, 0, 0)
+
+
 def row_total(partial_value):
-    return lax.psum(partial_value.astype(jnp.bfloat16), "pcol").astype(jnp.float32)
+    partials = shared_with_all(partial_value.astype(jnp.bfloat16), "pcol")
+    return jnp.sum(partials.astype(jnp.float32), axis=0)
+
+
+def column_total(partial_value):
+    ways = lax.axis_size("prow")
+    rows, width = partial_value.shape
+    pieces = partial_value.astype(jnp.bfloat16).reshape(ways, rows // ways, width)
+    received = lax.all_to_all(pieces, "prow", 0, 0)
+    piece = jnp.sum(received.astype(jnp.float32), axis=0).astype(jnp.bfloat16)
+    return shared_with_all(piece, "prow").reshape(rows, width)
 
 
 def panel_solve(residual, inverse):
@@ -24,7 +39,7 @@
     partial_value = lax.dot_general(
         inverse, rounded, (((0,), (0,)), ((), ())), preferred_element_type=jnp.float32
     )
-    return lax.psum(partial_value.astype(jnp.bfloat16), "prow")
+    return column_total(partial_value)
 
 
 def forward_solve(

time: 1860 us -> 482 us (0.26)
  the two profiles are of different devices: /device:TPU:2 before, /device:TPU:16 now
where the time goes in v1:
time: 482 us; the launch traced here: 480 us
  blocking collectives  252 us (52%)
  waiting for transfers between devices  154 us (32%)
  starting transfers between devices  48 us (10%)
  local copies, waits for them, and re-layouts  12.7 us (3%)
  matrix products  7.41 us (2%)
    all_to_all x9, blocking collectives, column_total(): received = lax.all_to_all(pieces, 'prow', 0, 0)  173 us
    all_to_all x11, waiting for transfers between devices, shared_with_all(): return lax.all_to_all(copies, axis, 0, 0)  140 us
    all_to_all x6, blocking collectives, shared_with_all(): return lax.all_to_all(copies, axis, 0, 0)  79 us
    all_to_all x11, starting transfers between devices, shared_with_all(): return lax.all_to_all(copies, axis, 0, 0)  42.5 us
    ppermute x2, waiting for transfers between devices, from_partner(): lax.ppermute(array, axis, [(i, i ^ 1 << apart) for i in range(lax.axis_si...  13.3 us
  transfers between devices with their start and end apart: 13, of which 13 were waited for; matrix products, arithmetic and copies ran while one was open for 1% of the time, Pallas kernels for 0%

profile of v1, /device:TPU:16, one launch (start us, length us, event | category | flops | bytes accessed | tf_op | source)
XLA Modules:
  0.0 480.1 jit_solution(13300143541746729746)
XLA Ops:
  0.7 1.8 fusion.65
  2.4 1.0 convolution_convert_fusion.8
  3.5 29.7 %all_to_all.130 = bf16[16,16,256]{2,1,0:T(8,128)(2,1)S(1)} all-to-all(bf16[16,16,256]{2,1,0:T(8,128)(2,1)S(1)} %bitcast.275), channel_id=1, replica_groups=mesh['layer'=4,'prow'=16,'pcol'=8] {'prow'}, dimensions={0} | all-to-all | bytes 262144 | tf_op jit(solution)/shard_map/all_to_all | solution.py:32
  33.2 0.7 broadcast_in_dim.66
  33.9 3.8 all-to-all-start.1
  37.8 1.2 broadcast_select_fusion
  39.1 0.4 slice.379
  39.4 0.3 dot_general.68
  39.8 12.0 %all-to-all-done.1 = bf16[16,16,256]{2,1,0:T(8,128)(2,1)S(1)} async-done(((bf16[16,16,256]{2,1,0:T(8,128)(2,1)}), bf16[16,16,256]{2,1,0:T(8,128)(2,1)S(1)}, u32[]{:S(2)}, u32[]{:S(2)}) %all-to-all-start.1) | async-done | bytes 131104 | tf_op jit(solution)/shard_map/all_to_all | solution.py:20
  52.1 14.5 %all_to_all.131 = bf16[8,128,256]{2,1,0:T(8,128)(2,1)S(1)} all-to-all(bf16[8,128,256]{2,1,0:T(8,128)(2,1)S(1)} %broadcast_in_dim.70), channel_id=1, replica_groups=mesh['layer'=4,'prow'=16,'pcol'=8] {'pcol'}, dimensions={0} | all-to-all | bytes 1048576 | tf_op jit(solution)/shard_map/all_to_all | solution.py:20
  66.7 1.1 convolution_convert_fusion.7
  67.7 17.9 %all_to_all.132 = bf16[16,16,256]{2,1,0:T(8,128)(2,1)S(1)} all-to-all(bf16[16,16,256]{2,1,0:T(8,128)(2,1)S(1)} %bitcast.267), channel_id=1, replica_groups=mesh['layer'=4,'prow'=16,'pcol'=8] {'prow'}, dimensions={0} | all-to-all | bytes 262144 | tf_op jit(solution)/shard_map/all_to_all | solution.py:32
  85.7 0.7 broadcast_in_dim.71
  86.3 4.0 all-to-all-start.4
  90.7 1.1 dot_general.71
  91.7 12.6 %all-to-all-done.4 = bf16[16,16,256]{2,1,0:T(8,128)(2,1)S(1)} async-done(((bf16[16,16,256]{2,1,0:T(8,128)(2,1)}), bf16[16,16,256]{2,1,0:T(8,128)(2,1)S(1)}, u32[]{:S(2)}, u32[]{:S(2)}) %all-to-all-start.4) | async-done | bytes 131104 | tf_op jit(solution)/shard_map/all_to_all | solution.py:20
  104.3 1.3 convolution_add_fusion
  105.7 12.8 %all_to_all.133 = bf16[8,128,256]{2,1,0:T(8,128)(2,1)S(1)} all-to-all(bf16[8,128,256]{2,1,0:T(8,128)(2,1)S(1)} %broadcast_in_dim.73), channel_id=1, replica_groups=mesh['layer'=4,'prow'=16,'pcol'=8] {'pcol'}, dimensions={0} | all-to-all | bytes 1048576 | tf_op jit(solution)/shard_map/all_to_all | solution.py:20
  118.6 1.1 convolution_convert_fusion.6
  119.7 17.7 %all_to_all.134 = bf16[16,16,256]{2,1,0:T(8,128)(2,1)S(1)} all-to-all(bf16[16,16,256]{2,1,0:T(8,128)(2,1)S(1)} %bitcast.268), channel_id=1, replica_groups=mesh['layer'=4,'prow'=16,'pcol'=8] {'prow'}, dimensions={0} | all-to-all | bytes 262144 | tf_op jit(solution)/shard_map/all_to_all | solution.py:32
  137.4 0.7 broadcast_in_dim.74
  138.0 4.0 all-to-all-start.7
  142.6 13.4 %all-to-all-done.7 = bf16[16,16,256]{2,1,0:T(8,128)(2,1)S(1)} async-done(((bf16[16,16,256]{2,1,0:T(8,128)(2,1)}), bf16[16,16,256]{2,1,0:T(8,128)(2,1)S(1)}, u32[]{:S(2)}, u32[]{:S(2)}) %all-to-all-start.7) | async-done | bytes 131104 | tf_op jit(solution)/shard_map/all_to_all | solution.py:20
  156.3 3.2 collective-permute-start
  159.5 6.5 %collective-permute-done = bf16[6,128,256]{2,1,0:T(8,128)(2,1)S(1)} collective-permute-done((bf16[6,128,256]{2,1,0:T(8,128)(2,1)S(1)}, bf16[6,128,256]{2,1,0:T(8,128)(2,1)S(1)}, u32[]{:S(2)}, u32[]{:S(2)}) %collective-permute-start) | collective-permute-done | bytes 393248 | tf_op jit(solution)/shard_map/ppermute | solution.py:8
  166.1 0.8 broadcast_in_dim.77
  166.9 3.5 all-to-all-start.8
  170.5 10.1 %all-to-all-done.8 = bf16[8,128,256]{2,1,0:T(8,128)(2,1)S(1)} async-done(((bf16[8,128,256]{2,1,0:T(8,128)(2,1)}), bf16[8,128,256]{2,1,0:T(8,128)(2,1)S(1)}, u32[]{:S(2)}, u32[]{:S(2)}) %all-to-all-start.8) | async-done | bytes 524320 | tf_op jit(solution)/shard_map/all_to_all | solution.py:20
  180.9 19.6 %all_to_all.135 = bf16[16,16,256]{2,1,0:T(8,128)(2,1)S(1)} all-to-all(bf16[16,16,256]{2,1,0:T(8,128)(2,1)S(1)} %bitcast.269), channel_id=1, replica_groups=mesh['layer'=4,'prow'=16,'pcol'=8] {'prow'}, dimensions={0} | all-to-all | bytes 262144 | tf_op jit(solution)/shard_map/all_to_all | solution.py:32
  200.6 0.7 broadcast_in_dim.78
  201.3 3.9 all-to-all-start.10
  205.2 14.0 %all-to-all-done.10 = bf16[16,16,256]{2,1,0:T(8,128)(2,1)S(1)} async-done(((bf16[16,16,256]{2,1,0:T(8,128)(2,1)}), bf16[16,16,256]{2,1,0:T(8,128)(2,1)S(1)}, u32[]{:S(2)}, u32[]{:S(2)}) %all-to-all-start.10) | async-done | bytes 131104 | tf_op jit(solution)/shard_map/all_to_all | solution.py:20
  219.5 12.9 %all_to_all.136 = bf16[8,128,256]{2,1,0:T(8,128)(2,1)S(1)} all-to-all(bf16[8,128,256]{2,1,0:T(8,128)(2,1)S(1)} %broadcast_in_dim.80), channel_id=1, replica_groups=mesh['layer'=4,'prow'=16,'pcol'=8] {'pcol'}, dimensions={0} | all-to-all | bytes 1048576 | tf_op jit(solution)/shard_map/all_to_all | solution.py:20
  232.8 17.5 %all_to_all.137 = bf16[16,16,256]{2,1,0:T(8,128)(2,1)S(1)} all-to-all(bf16[16,16,256]{2,1,0:T(8,128)(2,1)S(1)} %bitcast.270), channel_id=1, replica_groups=mesh['layer'=4,'prow'=16,'pcol'=8] {'prow'}, dimensions={0} | all-to-all | bytes 262144 | tf_op jit(solution)/shard_map/all_to_all | solution.py:32
  250.3 0.7 broadcast_in_dim.81
  251.0 4.0 all-to-all-start.13
  255.0 14.0 %all-to-all-done.13 = bf16[16,16,256]{2,1,0:T(8,128)(2,1)S(1)} async-done(((bf16[16,16,256]{2,1,0:T(8,128)(2,1)}), bf16[16,16,256]{2,1,0:T(8,128)(2,1)S(1)}, u32[]{:S(2)}, u32[]{:S(2)}) %all-to-all-start.13) | async-done | bytes 131104 | tf_op jit(solution)/shard_map/all_to_all | solution.py:20
  269.3 12.9 %all_to_all.138 = bf16[8,128,256]{2,1,0:T(8,128)(2,1)S(1)} all-to-all(bf16[8,128,256]{2,1,0:T(8,128)(2,1)S(1)} %broadcast_in_dim.83), channel_id=1, replica_groups=mesh['layer'=4,'prow'=16,'pcol'=8] {'pcol'}, dimensions={0} | all-to-all | bytes 1048576 | tf_op jit(solution)/shard_map/all_to_all | solution.py:20
  282.5 17.7 %all_to_all.139 = bf16[16,16,256]{2,1,0:T(8,128)(2,1)S(1)} all-to-all(bf16[16,16,256]{2,1,0:T(8,128)(2,1)S(1)} %bitcast.271), channel_id=1, replica_groups=mesh['layer'=4,'prow'=16,'pcol'=8] {'prow'}, dimensions={0} | all-to-all | bytes 262144 | tf_op jit(solution)/shard_map/all_to_all | solution.py:32
  300.2 0.7 broadcast_in_dim.158
  300.9 4.0 all-to-all-start.16
  304.9 14.0 %all-to-all-done.16 = bf16[16,16,256]{2,1,0:T(8,128)(2,1)S(1)} async-done(((bf16[16,16,256]{2,1,0:T(8,128)(2,1)}), bf16[16,16,256]{2,1,0:T(8,128)(2,1)S(1)}, u32[]{:S(2)}, u32[]{:S(2)}) %all-to-all-start.16) | async-done | bytes 131104 | tf_op jit(solution)/shard_map/all_to_all | solution.py:20
  319.1 2.4 collective-permute-start.1
  321.5 6.8 %collective-permute-done.1 = bf16[3,128,256]{2,1,0:T(8,128)(2,1)S(1)} collective-permute-done((bf16[3,128,256]{2,1,0:T(8,128)(2,1)S(1)}, bf16[3,128,256]{2,1,0:T(8,128)(2,1)S(1)}, u32[]{:S(2)}, u32[]{:S(2)}) %collective-permute-start.1) | collective-permute-done | bytes 196640 | tf_op jit(solution)/shard_map/ppermute | solution.py:8
  328.4 0.8 broadcast_in_dim.160
  329.3 3.5 all-to-all-start.17
  332.9 10.1 %all-to-all-done.17 = bf16[8,128,256]{2,1,0:T(8,128)(2,1)S(1)} async-done(((bf16[8,128,256]{2,1,0:T(8,128)(2,1)}), bf16[8,128,256]{2,1,0:T(8,128)(2,1)S(1)}, u32[]{:S(2)}, u32[]{:S(2)}) %all-to-all-start.17) | async-done | bytes 524320 | tf_op jit(solution)/shard_map/all_to_all | solution.py:20
  343.3 17.9 %all_to_all.140 = bf16[16,16,256]{2,1,0:T(8,128)(2,1)S(1)} all-to-all(bf16[16,16,256]{2,1,0:T(8,128)(2,1)S(1)} %bitcast.272), channel_id=1, replica_groups=mesh['layer'=4,'prow'=16,'pcol'=8] {'prow'}, dimensions={0} | all-to-all | bytes 262144 | tf_op jit(solution)/shard_map/all_to_all | solution.py:32
  361.3 0.7 broadcast_in_dim.161
  361.9 3.9 all-to-all-start.19
  365.8 14.0 %all-to-all-done.19 = bf16[16,16,256]{2,1,0:T(8,128)(2,1)S(1)} async-done(((bf16[16,16,256]{2,1,0:T(8,128)(2,1)}), bf16[16,16,256]{2,1,0:T(8,128)(2,1)S(1)}, u32[]{:S(2)}, u32[]{:S(2)}) %all-to-all-start.19) | async-done | bytes 131104 | tf_op jit(solution)/shard_map/all_to_all | solution.py:20
  380.1 12.9 %all_to_all.141 = bf16[8,128,256]{2,1,0:T(8,128)(2,1)S(1)} all-to-all(bf16[8,128,256]{2,1,0:T(8,128)(2,1)S(1)} %broadcast_in_dim.163), channel_id=1, replica_groups=mesh['layer'=4,'prow'=16,'pcol'=8] {'pcol'}, dimensions={0} | all-to-all | bytes 1048576 | tf_op jit(solution)/shard_map/all_to_all | solution.py:20
  393.3 17.5 %all_to_all.142 = bf16[16,16,256]{2,1,0:T(8,128)(2,1)S(1)} all-to-all(bf16[16,16,256]{2,1,0:T(8,128)(2,1)S(1)} %bitcast.273), channel_id=1, replica_groups=mesh['layer'=4,'prow'=16,'pcol'=8] {'prow'}, dimensions={0} | all-to-all | bytes 262144 | tf_op jit(solution)/shard_map/all_to_all | solution.py:32
  410.9 0.7 broadcast_in_dim.164
  411.6 4.0 all-to-all-start.22
  415.6 14.0 %all-to-all-done.22 = bf16[16,16,256]{2,1,0:T(8,128)(2,1)S(1)} async-done(((bf16[16,16,256]{2,1,0:T(8,128)(2,1)}), bf16[16,16,256]{2,1,0:T(8,128)(2,1)S(1)}, u32[]{:S(2)}, u32[]{:S(2)}) %all-to-all-start.22) | async-done | bytes 131104 | tf_op jit(solution)/shard_map/all_to_all | solution.py:20
  429.8 12.9 %all_to_all.143 = bf16[8,128,256]{2,1,0:T(8,128)(2,1)S(1)} all-to-all(bf16[8,128,256]{2,1,0:T(8,128)(2,1)S(1)} %broadcast_in_dim.166), channel_id=1, replica_groups=mesh['layer'=4,'prow'=16,'pcol'=8] {'pcol'}, dimensions={0} | all-to-all | bytes 1048576 | tf_op jit(solution)/shard_map/all_to_all | solution.py:20
  443.0 17.7 %all_to_all.144 = bf16[16,16,256]{2,1,0:T(8,128)(2,1)S(1)} all-to-all(bf16[16,16,256]{2,1,0:T(8,128)(2,1)S(1)} %bitcast.274), channel_id=1, replica_groups=mesh['layer'=4,'prow'=16,'pcol'=8] {'prow'}, dimensions={0} | all-to-all | bytes 262144 | tf_op jit(solution)/shard_map/all_to_all | solution.py:32
  460.7 0.7 broadcast_in_dim.167
  461.4 4.0 all-to-all-start.25
  465.4 0.8 pad_maximum_fusion
  466.2 0.8 pad_maximum_fusion.1
  466.9 12.4 %all-to-all-done.25 = bf16[16,16,256]{2,1,0:T(8,128)(2,1)S(1)} async-done(((bf16[16,16,256]{2,1,0:T(8,128)(2,1)}), bf16[16,16,256]{2,1,0:T(8,128)(2,1)S(1)}, u32[]{:S(2)}, u32[]{:S(2)}) %all-to-all-start.25) | async-done | bytes 131104 | tf_op jit(solution)/shard_map/all_to_all | solution.py:20
  479.3 0.8 pad_maximum_fusion.2
  (83 shorter events, 5.6 us)
Async XLA Ops:
  0.6 37.1 %copy-start.9 = (s32[1,21,1,2,1]{1,4,3,2,0:T(1,128)S(1)}, s32[1,21,1,2,1]{1,4,3,2,0:T(1,128)}, u32[]{:S(2)}) copy-start(s32[1,21,1,2,1]{1,4,3,2,0:T(1,128)} %param.26) | copy-start | bytes 508
  0.6 37.2 %copy-start = (bf16[1,21,1,128,2,1,128]{6,4,5,3,2,1,0:T(2,128)(2,1)S(1)}, bf16[1,21,1,128,2,1,128]{6,4,5,3,2,1,0:T(2,128)(2,1)}, u32[]{:S(2)}) copy-start(bf16[1,21,1,128,2,1,128]{6,4,5,3,2,1,0:T(2,128)(2,1)} %param.25) | copy-start | bytes 4128772
  33.9 17.9 %all-to-all-start.1 = ((bf16[16,16,256]{2,1,0:T(8,128)(2,1)}), bf16[16,16,256]{2,1,0:T(8,128)(2,1)S(1)}, u32[]{:S(2)}, u32[]{:S(2)}) async-start(bf16[16,16,256]{2,1,0:T(8,128)(2,1)} %broadcast_in_dim.66), calls=%async_computation.1 | async-start | bytes 262144 | tf_op jit(solution)/shard_map/all_to_all | solution.py:20
  51.7 14.9 %copy-start.1 = (bf16[16,16,256]{2,1,0:T(8,128)(2,1)}, bf16[16,16,256]{2,1,0:T(8,128)(2,1)S(1)}, u32[]{:S(2)}) copy-start(bf16[16,16,256]{2,1,0:T(8,128)(2,1)S(1)} %all-to-all-done.1) | copy-start | bytes 393220
  52.0 14.6 %copy-start.6 = (bf16[1,1,1,128,2,1,128]{6,4,5,3,2,1,0:T(2,128)(2,1)S(1)}, bf16[1,1,1,128,2,1,128]{6,4,5,3,2,1,0:T(2,128)(2,1)}, u32[]{:S(2)}) copy-start(bf16[1,1,1,128,2,1,128]{6,4,5,3,2,1,0:T(2,128)(2,1)} %get-tuple-element.107) | copy-start | bytes 196612
  86.3 18.0 %all-to-all-start.4 = ((bf16[16,16,256]{2,1,0:T(8,128)(2,1)}), bf16[16,16,256]{2,1,0:T(8,128)(2,1)S(1)}, u32[]{:S(2)}, u32[]{:S(2)}) async-start(bf16[16,16,256]{2,1,0:T(8,128)(2,1)} %broadcast_in_dim.71), calls=%async_computation.4 | async-start | bytes 262144 | tf_op jit(solution)/shard_map/all_to_all | solution.py:20
  118.5 37.5 %copy-start.5 = (bf16[1,6,1,128,256]{4,3,2,1,0:T(8,128)(2,1)S(1)}, bf16[1,6,1,128,256]{4,3,2,1,0:T(8,128)(2,1)}, u32[]{:S(2)}) copy-start(bf16[1,6,1,128,256]{4,3,2,1,0:T(8,128)(2,1)} %param.33) | copy-start | bytes 1179652
  138.0 18.0 %all-to-all-start.7 = ((bf16[16,16,256]{2,1,0:T(8,128)(2,1)}), bf16[16,16,256]{2,1,0:T(8,128)(2,1)S(1)}, u32[]{:S(2)}, u32[]{:S(2)}) async-start(bf16[16,16,256]{2,1,0:T(8,128)(2,1)} %broadcast_in_dim.74), calls=%async_computation.7 | async-start | bytes 262144 | tf_op jit(solution)/shard_map/all_to_all | solution.py:20
  156.3 9.7 %collective-permute-start = (bf16[6,128,256]{2,1,0:T(8,128)(2,1)S(1)}, bf16[6,128,256]{2,1,0:T(8,128)(2,1)S(1)}, u32[]{:S(2)}, u32[]{:S(2)}) collective-permute-start(bf16[6,128,256]{2,1,0:T(8,128)(2,1)S(1)} %get-tuple-element.108), channel_id=1, source_target_pairs={{0,128},{128,0},{256,384},{384,256},{1,129},{129,1},{257,385},{385... | collective-permute-start | bytes 1179656 | tf_op jit(solution)/shard_map/ppermute | solution.py:8
  166.0 4.4 copy-start.7
  166.9 13.8 %all-to-all-start.8 = ((bf16[8,128,256]{2,1,0:T(8,128)(2,1)}), bf16[8,128,256]{2,1,0:T(8,128)(2,1)S(1)}, u32[]{:S(2)}, u32[]{:S(2)}) async-start(bf16[8,128,256]{2,1,0:T(8,128)(2,1)} %broadcast_in_dim.77), calls=%async_computation.8 | async-start | bytes 1048576 | tf_op jit(solution)/shard_map/all_to_all | solution.py:20
  170.4 48.8 %slice-start = ((bf16[1,12,1,128,2,1,128]{6,4,5,3,2,1,0:T(2,128)(2,1)}), bf16[1,5,1,128,2,1,128]{6,4,5,3,2,1,0:T(2,128)(2,1)S(1)}, s32[]{:S(2)}) async-start(bf16[1,12,1,128,2,1,128]{6,4,5,3,2,1,0:T(2,128)(2,1)} %param.28), calls=%async_computation.26 | async-start | bytes 655360 | tf_op jit(solution)/shard_map/slice | solution.py:76
  201.3 17.9 %all-to-all-start.10 = ((bf16[16,16,256]{2,1,0:T(8,128)(2,1)}), bf16[16,16,256]{2,1,0:T(8,128)(2,1)S(1)}, u32[]{:S(2)}, u32[]{:S(2)}) async-start(bf16[16,16,256]{2,1,0:T(8,128)(2,1)} %broadcast_in_dim.78), calls=%async_computation.10 | async-start | bytes 262144 | tf_op jit(solution)/shard_map/all_to_all | solution.py:20
  219.5 49.5 %slice-start.1 = ((bf16[1,12,1,128,2,1,128]{6,4,5,3,2,1,0:T(2,128)(2,1)}), bf16[1,4,1,128,2,1,128]{6,4,5,3,2,1,0:T(2,128)(2,1)S(1)}, s32[]{:S(2)}) async-start(bf16[1,12,1,128,2,1,128]{6,4,5,3,2,1,0:T(2,128)(2,1)} %param.28), calls=%async_computation.27 | async-start | bytes 524288 | tf_op jit(solution)/shard_map/slice | solution.py:76
  251.0 18.0 %all-to-all-start.13 = ((bf16[16,16,256]{2,1,0:T(8,128)(2,1)}), bf16[16,16,256]{2,1,0:T(8,128)(2,1)S(1)}, u32[]{:S(2)}, u32[]{:S(2)}) async-start(bf16[16,16,256]{2,1,0:T(8,128)(2,1)} %broadcast_in_dim.81), calls=%async_computation.13 | async-start | bytes 262144 | tf_op jit(solution)/shard_map/all_to_all | solution.py:20
  269.0 13.3 %copy-start.3 = (bf16[16,16,256]{2,1,0:T(8,128)(2,1)}, bf16[16,16,256]{2,1,0:T(8,128)(2,1)S(1)}, u32[]{:S(2)}) copy-start(bf16[16,16,256]{2,1,0:T(8,128)(2,1)S(1)} %all-to-all-done.13) | copy-start | bytes 393220
  269.3 49.6 %slice-start.2 = ((bf16[1,12,1,128,2,1,128]{6,4,5,3,2,1,0:T(2,128)(2,1)}), bf16[1,3,1,128,2,1,128]{6,4,5,3,2,1,0:T(2,128)(2,1)S(1)}, s32[]{:S(2)}) async-start(bf16[1,12,1,128,2,1,128]{6,4,5,3,2,1,0:T(2,128)(2,1)} %param.28), calls=%async_computation.28 | async-start | bytes 393216 | tf_op jit(solution)/shard_map/slice | solution.py:76
  300.9 18.0 %all-to-all-start.16 = ((bf16[16,16,256]{2,1,0:T(8,128)(2,1)}), bf16[16,16,256]{2,1,0:T(8,128)(2,1)S(1)}, u32[]{:S(2)}, u32[]{:S(2)}) async-start(bf16[16,16,256]{2,1,0:T(8,128)(2,1)} %broadcast_in_dim.158), calls=%async_computation.16 | async-start | bytes 262144 | tf_op jit(solution)/shard_map/all_to_all | solution.py:20
  319.1 13.6 %copy-start.8 = (bf16[3,1,128,2,1,128]{5,3,4,2,1,0:T(2,128)(2,1)S(1)}, bf16[3,1,128,2,1,128]{5,3,4,2,1,0:T(2,128)(2,1)}, u32[]{:S(2)}) copy-start(bf16[3,1,128,2,1,128]{5,3,4,2,1,0:T(2,128)(2,1)} %param.31) | copy-start | bytes 589828
  319.1 9.2 %collective-permute-start.1 = (bf16[3,128,256]{2,1,0:T(8,128)(2,1)S(1)}, bf16[3,128,256]{2,1,0:T(8,128)(2,1)S(1)}, u32[]{:S(2)}, u32[]{:S(2)}) collective-permute-start(bf16[3,128,256]{2,1,0:T(8,128)(2,1)S(1)} %fusion.11), channel_id=1, source_target_pairs={{0,256},{128,384},{256,0},{384,128},{1,257},{129,385},{257,1},{385... | collective-permute-start | bytes 589832 | tf_op jit(solution)/shard_map/ppermute | solution.py:8
  329.3 13.8 %all-to-all-start.17 = ((bf16[8,128,256]{2,1,0:T(8,128)(2,1)}), bf16[8,128,256]{2,1,0:T(8,128)(2,1)S(1)}, u32[]{:S(2)}, u32[]{:S(2)}) async-start(bf16[8,128,256]{2,1,0:T(8,128)(2,1)} %broadcast_in_dim.160), calls=%async_computation.17 | async-start | bytes 1048576 | tf_op jit(solution)/shard_map/all_to_all | solution.py:20
  332.8 47.1 %slice-start.3 = ((bf16[3,1,128,2,1,128]{5,3,4,2,1,0:T(2,128)(2,1)}), bf16[2,1,128,2,1,128]{5,3,4,2,1,0:T(2,128)(2,1)S(1)}, s32[]{:S(2)}) async-start(bf16[3,1,128,2,1,128]{5,3,4,2,1,0:T(2,128)(2,1)} %param.30), calls=%async_computation.29 | async-start | bytes 262144 | tf_op jit(solution)/shard_map/slice | solution.py:89
  361.9 17.9 %all-to-all-start.19 = ((bf16[16,16,256]{2,1,0:T(8,128)(2,1)}), bf16[16,16,256]{2,1,0:T(8,128)(2,1)S(1)}, u32[]{:S(2)}, u32[]{:S(2)}) async-start(bf16[16,16,256]{2,1,0:T(8,128)(2,1)} %broadcast_in_dim.161), calls=%async_computation.19 | async-start | bytes 262144 | tf_op jit(solution)/shard_map/all_to_all | solution.py:20
  380.1 49.5 %slice-start.4 = ((bf16[3,1,128,2,1,128]{5,3,4,2,1,0:T(2,128)(2,1)}), bf16[1,1,128,2,1,128]{5,3,4,2,1,0:T(2,128)(2,1)S(1)}, s32[]{:S(2)}) async-start(bf16[3,1,128,2,1,128]{5,3,4,2,1,0:T(2,128)(2,1)} %param.30), calls=%async_computation.30 | async-start | bytes 131072 | tf_op jit(solution)/shard_map/slice | solution.py:89
  411.6 18.0 %all-to-all-start.22 = ((bf16[16,16,256]{2,1,0:T(8,128)(2,1)}), bf16[16,16,256]{2,1,0:T(8,128)(2,1)S(1)}, u32[]{:S(2)}, u32[]{:S(2)}) async-start(bf16[16,16,256]{2,1,0:T(8,128)(2,1)} %broadcast_in_dim.164), calls=%async_computation.22 | async-start | bytes 262144 | tf_op jit(solution)/shard_map/all_to_all | solution.py:20
  429.8 35.6 %copy-start.2 = (bf16[16,16,256]{2,1,0:T(8,128)(2,1)S(1)}, bf16[16,16,256]{2,1,0:T(8,128)(2,1)}, u32[]{:S(2)}) copy-start(bf16[16,16,256]{2,1,0:T(8,128)(2,1)} %copy-done.1) | copy-start | bytes 393220
  442.7 23.4 %copy-start.4 = (bf16[16,16,256]{2,1,0:T(8,128)(2,1)S(1)}, bf16[16,16,256]{2,1,0:T(8,128)(2,1)}, u32[]{:S(2)}) copy-start(bf16[16,16,256]{2,1,0:T(8,128)(2,1)} %copy-done.3) | copy-start | bytes 393220
  461.4 18.0 %all-to-all-start.25 = ((bf16[16,16,256]{2,1,0:T(8,128)(2,1)}), bf16[16,16,256]{2,1,0:T(8,128)(2,1)S(1)}, u32[]{:S(2)}, u32[]{:S(2)}) async-start(bf16[16,16,256]{2,1,0:T(8,128)(2,1)} %broadcast_in_dim.167), calls=%async_computation.25 | async-start | bytes 262144 | tf_op jit(solution)/shard_map/all_to_all | solution.py:20

commit v2 on v1

v2 whole, which is shorter than its diff:
```python
import jax
import jax.numpy as jnp
from jax import lax
from jax.sharding import PartitionSpec as P


def shared_with_all(value, axis):
    copies = jnp.broadcast_to(value[None], (lax.axis_size(axis),) + value.shape)
    return lax.all_to_all(copies, axis, 0, 0)


def row_total(partial_value):
    partials = shared_with_all(partial_value.astype(jnp.bfloat16), "pcol")
    return jnp.sum(partials.astype(jnp.float32), axis=0)


def column_total(partial_value):
    ways = lax.axis_size("prow")
    rows, width = partial_value.shape
    pieces = partial_value.astype(jnp.bfloat16).reshape(ways, rows // ways, width)
    received = lax.all_to_all(pieces, "prow", 0, 0)
    piece = jnp.sum(received.astype(jnp.float32), axis=0).astype(jnp.bfloat16)
    return shared_with_all(piece, "prow").reshape(rows, width)


def sibling_groups():
    prows = lax.axis_size("prow")
    return [
        [layer * prows + p for layer in (first, first + 1) for p in range(prows)]
        for first in range(0, lax.axis_size("layer"), 2)
    ]


def among_siblings(pieces):
    return lax.all_to_all(
        pieces, ("layer", "prow"), 0, 0, axis_index_groups=sibling_groups()
    )


def own_solve(own_cols, own_inv, own_rows, shared_turned):
    panels = own_inv.shape[0]
    chain_length = 3 * panels
    solved = []
    within = [None] * panels
    beyond = jnp.where(lax.axis_index("pcol") == 0, shared_turned.astype(jnp.float32), 0.0)
    offset = 0
    for step in range(panels):
        residual = own_rows[step].astype(jnp.float32)
        if within[step] is not None:
            residual = residual - row_total(within[step])
        partial_value = lax.dot_general(
            own_inv[step],
            residual.astype(jnp.bfloat16),
            (((0,), (0,)), ((), ())),
            preferred_element_type=jnp.float32,
        )
        result = column_total(partial_value)
        solved.append(result)
        for target in range(step + 1, panels):
            update = jnp.dot(
                own_cols[offset + target - step - 1], result, preferred_element_type=jnp.float32
            )
            within[target] = update if within[target] is None else within[target] + update
        first = offset + panels - step - 1
        beyond = beyond - lax.dot_general(
            result,
            own_cols[first : first + 2 * panels],
            (((0,), (2,)), ((), ())),
            preferred_element_type=jnp.float32,
        )
        offset += chain_length - 1 - step
    return solved, beyond


def gathered_columns(inverses, blocks):
    tile_rows, cycles = blocks.shape[-4], blocks.shape[-3]
    stacked = jnp.concatenate(
        [part.reshape(-1, tile_rows, cycles * blocks.shape[-1]) for part in (inverses, blocks)]
    )
    return lax.all_gather(stacked, "prow")


def slice_solve(sums, gathered, panels):
    width, prows, targets, tile_rows = sums.shape
    sums = [sums[:, :, t] for t in range(targets)]
    solved = []
    offset = panels
    for step in range(panels):
        residual = row_total(sums[step]).astype(jnp.bfloat16)
        result = lax.dot_general(
            residual,
            gathered[:, step],
            (((1, 2), (0, 1)), ((), ())),
            preferred_element_type=jnp.float32,
        ).astype(jnp.bfloat16)
        solved.append(result)
        for target in range(step + 1, targets):
            sums[target] = sums[target] - lax.dot_general(
                result,
                gathered[:, offset + target - step - 1],
                (((1,), (2,)), ((), ())),
                preferred_element_type=jnp.float32,
            )
        offset += targets - 1 - step
    return jnp.stack(solved), sums[panels:]


def local(
    own_blocks,
    own_pattern,
    own_inverse,
    pair_blocks,
    pair_inverse,
    root_blocks,
    root_inverse,
    own_rhs,
    shared_rhs,
):
    tile_rows = own_blocks.shape[3]
    cycles = own_blocks.shape[4]
    col_width = cycles * tile_rows
    rhs_width = own_rhs.shape[-1]
    prows = lax.axis_size("prow")
    siblings = 2 * prows
    share = rhs_width // siblings
    panels = own_inverse.shape[1]
    pair_all = gathered_columns(pair_inverse, pair_blocks)
    root_all = gathered_columns(root_inverse, root_blocks)
    own_tiles = own_blocks.reshape(-1, tile_rows, cycles, tile_rows)
    kept_tiles = own_pattern.reshape(-1, 1, cycles, 1) > 0
    own_cols = jnp.where(kept_tiles, own_tiles, jnp.zeros((), own_tiles.dtype)).reshape(
        -1, tile_rows, col_width
    )
    own_inv = own_inverse.reshape(-1, tile_rows, col_width)
    own_rows = own_rhs.reshape(-1, tile_rows, rhs_width)
    shared_turned = jnp.transpose(shared_rhs.reshape(-1, tile_rows, rhs_width), (2, 0, 1))

    own_solved, beyond = own_solve(own_cols, own_inv, own_rows, shared_turned)

    pieces = beyond.astype(jnp.bfloat16).reshape(siblings, share, 2 * panels, tile_rows)
    received = among_siblings(pieces).reshape(2, prows, share, 2 * panels, tile_rows)
    sums = jnp.sum(received.astype(jnp.float32), axis=0).transpose(1, 0, 2, 3)
    pair_solved, left = slice_solve(sums, pair_all, panels)

    joined = jnp.stack(left, axis=2)
    swap = [(i, i ^ 2) for i in range(lax.axis_size("layer"))]
    joined = joined + lax.ppermute(joined.astype(jnp.bfloat16), "layer", swap).astype(joined.dtype)
    root_solved, _ = slice_solve(joined, root_all, panels)

    both = jnp.concatenate([pair_solved, root_solved])
    copies = jnp.broadcast_to(both[None], (siblings,) + both.shape)
    whole = among_siblings(copies)
    whole = whole.transpose(1, 3, 0, 2).reshape(2, 1, panels, cycles, 1, tile_rows, rhs_width)
    own_out = jnp.stack(own_solved).reshape(1, panels, cycles, 1, tile_rows, rhs_width)
    return own_out, whole[0], whole[1]


def solution(mesh):
    return jax.shard_map(
        local,
        mesh=mesh,
        in_specs=(
            P("layer", None, "prow", None, None, "pcol", None),
            P("layer", None, "prow", None, "pcol"),
            P("layer", None, "prow", None, None, "pcol", None),
            P("layer", None, "prow", None, None, "pcol", None),
            P("layer", None, "prow", None, None, "pcol", None),
            P(None, "prow", None, None, "pcol", None),
            P(None, "prow", None, None, "pcol", None),
            P("layer", None, "prow", None, None),
            P("layer", None, "prow", None, None),
        ),
        out_specs=(
            P("layer", None, None, "pcol", None, None),
            P("layer", None, None, "pcol", None, None),
            P("layer", None, None, "pcol", None, None),
        ),
        check_vma=False,
    )
```

time: 482 us -> 425 us (0.88)
  the two profiles are of different devices: /device:TPU:16 before, /device:TPU:32 now
where the time goes in v2:
time: 425 us; the launch traced here: 423 us
  waiting for transfers between devices  170 us (40%)
  blocking collectives  114 us (27%)
  starting transfers between devices  61.8 us (15%)
  matrix products  38.9 us (9%)
  local copies, waits for them, and re-layouts  16.9 us (4%)
  between operations  14.4 us (3%)
  other arithmetic  6.43 us (2%)
    all_to_all x5, blocking collectives, shared_with_all(): return lax.all_to_all(copies, axis, 0, 0)  57.1 us
    all_to_all x6, waiting for transfers between devices, shared_with_all(): return lax.all_to_all(copies, axis, 0, 0)  50.6 us
    all_gather x2, waiting for transfers between devices, gathered_columns(): return lax.all_gather(stacked, 'prow')  50.1 us
    all_to_all x1, waiting for transfers between devices, among_siblings(): lax.all_to_all(pieces, ('layer', 'prow'), 0, 0, axis_index_groups=sibling...  42.5 us
    all_to_all x1, blocking collectives, among_siblings(): lax.all_to_all(pieces, ('layer', 'prow'), 0, 0, axis_index_groups=sibling...  37.1 us
    all_to_all x6, starting transfers between devices, shared_with_all(): return lax.all_to_all(copies, axis, 0, 0)  26.9 us
    dot_general x15, matrix products, slice_solve(): lax.dot_general(result, gathered[:, offset + target - step - 1], (((1,),...  24.1 us
    all_to_all x2, waiting for transfers between devices, column_total(): received = lax.all_to_all(pieces, 'prow', 0, 0)  24.1 us
  transfers between devices with their start and end apart: 12, of which 12 were waited for; matrix products, arithmetic and copies ran while one was open for 11% of the time, Pallas kernels for 0%

profile of v2, /device:TPU:32, one launch (start us, length us, event | category | flops | bytes accessed | tf_op | source)
XLA Modules:
  0.0 422.8 jit_solution(11164759933855791767)
XLA Ops:
  7.2 2.5 reshape.131
  9.7 1.1 reshape.130
  10.8 1.1 pad_maximum_fusion
  11.9 1.0 fusion.78
  12.9 1.7 convolution_convert_fusion.2
  14.6 15.2 %all-to-all-start = ((bf16[16,16,256]{2,1,0:T(8,128)(2,1)}), bf16[16,16,256]{2,1,0:T(8,128)(2,1)S(1)}, u32[]{:S(2)}, u32[]{:S(2)}) async-start(bf16[16,16,256]{2,1,0:T(8,128)(2,1)} %bitcast.1), calls=%async_computation | async-start | bytes 262144 | tf_op jit(solution)/shard_map/all_to_all | solution.py:21
  29.9 1.1 reshape.132
  30.9 1.1 reshape.133
  33.6 11.1 %all-to-all-done = bf16[16,16,256]{2,1,0:T(8,128)(2,1)S(1)} async-done(((bf16[16,16,256]{2,1,0:T(8,128)(2,1)}), bf16[16,16,256]{2,1,0:T(8,128)(2,1)S(1)}, u32[]{:S(2)}, u32[]{:S(2)}) %all-to-all-start) | async-done | bytes 131104 | tf_op jit(solution)/shard_map/all_to_all | solution.py:21
  45.4 4.7 %all-to-all-start.1 = ((bf16[16,16,256]{2,1,0:T(8,128)(2,1)}), bf16[16,16,256]{2,1,0:T(8,128)(2,1)S(1)}, u32[]{:S(2)}, u32[]{:S(2)}) async-start(bf16[16,16,256]{2,1,0:T(8,128)(2,1)} %broadcast_in_dim.40), calls=%async_computation.1 | async-start | bytes 262144 | tf_op jit(solution)/shard_map/all_to_all | solution.py:9
  50.1 2.5 broadcast_select_fusion
  52.8 11.8 %all-to-all-done.1 = bf16[16,16,256]{2,1,0:T(8,128)(2,1)S(1)} async-done(((bf16[16,16,256]{2,1,0:T(8,128)(2,1)}), bf16[16,16,256]{2,1,0:T(8,128)(2,1)S(1)}, u32[]{:S(2)}, u32[]{:S(2)}) %all-to-all-start.1) | async-done | bytes 131104 | tf_op jit(solution)/shard_map/all_to_all | solution.py:9
  64.8 14.5 %all_to_all.80 = bf16[8,128,256]{2,1,0:T(8,128)(2,1)S(1)} all-to-all(bf16[8,128,256]{2,1,0:T(8,128)(2,1)S(1)} %broadcast_in_dim.43), channel_id=1, replica_groups=mesh['layer'=4,'prow'=16,'pcol'=8] {'pcol'}, dimensions={0} | all-to-all | bytes 1048576 | tf_op jit(solution)/shard_map/all_to_all | solution.py:9
  79.3 1.1 convolution_convert_fusion.1
  80.4 20.0 %all_to_all.81 = bf16[16,16,256]{2,1,0:T(8,128)(2,1)S(1)} all-to-all(bf16[16,16,256]{2,1,0:T(8,128)(2,1)S(1)} %bitcast.405), channel_id=1, replica_groups=mesh['layer'=4,'prow'=16,'pcol'=8] {'prow'}, dimensions={0} | all-to-all | bytes 262144 | tf_op jit(solution)/shard_map/all_to_all | solution.py:21
  101.1 5.1 %all-to-all-start.4 = ((bf16[16,16,256]{2,1,0:T(8,128)(2,1)}), bf16[16,16,256]{2,1,0:T(8,128)(2,1)S(1)}, u32[]{:S(2)}, u32[]{:S(2)}) async-start(bf16[16,16,256]{2,1,0:T(8,128)(2,1)} %broadcast_in_dim.44), calls=%async_computation.4 | async-start | bytes 262144 | tf_op jit(solution)/shard_map/all_to_all | solution.py:9
  106.3 14.8 %all-to-all-done.4 = bf16[16,16,256]{2,1,0:T(8,128)(2,1)S(1)} async-done(((bf16[16,16,256]{2,1,0:T(8,128)(2,1)}), bf16[16,16,256]{2,1,0:T(8,128)(2,1)S(1)}, u32[]{:S(2)}, u32[]{:S(2)}) %all-to-all-start.4) | async-done | bytes 131104 | tf_op jit(solution)/shard_map/all_to_all | solution.py:9
  121.3 12.8 %all_to_all.82 = bf16[8,128,256]{2,1,0:T(8,128)(2,1)S(1)} all-to-all(bf16[8,128,256]{2,1,0:T(8,128)(2,1)S(1)} %broadcast_in_dim.45), channel_id=1, replica_groups=mesh['layer'=4,'prow'=16,'pcol'=8] {'pcol'}, dimensions={0} | all-to-all | bytes 1048576 | tf_op jit(solution)/shard_map/all_to_all | solution.py:9
  134.2 1.7 convolution_convert_fusion
  135.9 5.0 %all-to-all-start.6 = ((bf16[16,16,256]{2,1,0:T(8,128)(2,1)}), bf16[16,16,256]{2,1,0:T(8,128)(2,1)S(1)}, u32[]{:S(2)}, u32[]{:S(2)}) async-start(bf16[16,16,256]{2,1,0:T(8,128)(2,1)} %bitcast.17), calls=%async_computation.6 | async-start | bytes 262144 | tf_op jit(solution)/shard_map/all_to_all | solution.py:21
  140.9 1.0 fusion.75
  142.9 13.0 %all-to-all-done.6 = bf16[16,16,256]{2,1,0:T(8,128)(2,1)S(1)} async-done(((bf16[16,16,256]{2,1,0:T(8,128)(2,1)}), bf16[16,16,256]{2,1,0:T(8,128)(2,1)S(1)}, u32[]{:S(2)}, u32[]{:S(2)}) %all-to-all-start.6) | async-done | bytes 131104 | tf_op jit(solution)/shard_map/all_to_all | solution.py:21
  156.6 5.0 %all-to-all-start.7 = ((bf16[16,16,256]{2,1,0:T(8,128)(2,1)}), bf16[16,16,256]{2,1,0:T(8,128)(2,1)S(1)}, u32[]{:S(2)}, u32[]{:S(2)}) async-start(bf16[16,16,256]{2,1,0:T(8,128)(2,1)} %broadcast_in_dim.46), calls=%async_computation.7 | async-start | bytes 262144 | tf_op jit(solution)/shard_map/all_to_all | solution.py:9
  162.3 14.3 %all-to-all-done.7 = bf16[16,16,256]{2,1,0:T(8,128)(2,1)S(1)} async-done(((bf16[16,16,256]{2,1,0:T(8,128)(2,1)}), bf16[16,16,256]{2,1,0:T(8,128)(2,1)S(1)}, u32[]{:S(2)}, u32[]{:S(2)}) %all-to-all-start.7) | async-done | bytes 131104 | tf_op jit(solution)/shard_map/all_to_all | solution.py:9
  177.0 37.1 %all_to_all.83 = bf16[32,8,6,128]{3,1,2,0:T(8,128)(2,1)S(1)} all-to-all(bf16[32,8,6,128]{3,1,2,0:T(8,128)(2,1)S(1)} %copy.144), channel_id=1, replica_groups={{0,8,16,24,32,40,48,56,64,72,80,88,96,104,112,120,128,136,144,152,160,1..., dimensions={0} | all-to-all | bytes 786432 | tf_op jit(solution)/shard_map/all_to_all | solution.py:35
  214.3 9.9 %all_to_all.84 = bf16[8,8,16,128]{3,2,1,0:T(8,128)(2,1)S(1)} all-to-all(bf16[8,8,16,128]{3,2,1,0:T(8,128)(2,1)S(1)} %broadcast_in_dim.48), channel_id=1, replica_groups=mesh['layer'=4,'prow'=16,'pcol'=8] {'pcol'}, dimensions={0} | all-to-all | bytes 524288 | tf_op jit(solution)/shard_map/all_to_all | solution.py:9
  224.2 17.3 %all-gather.5.cloned.1.call-done = bf16[240,128,256]{2,1,0:T(8,128)(2,1)} async-done(((bf16[15,128,256]{2,1,0:T(8,128)(2,1)}), bf16[240,128,256]{2,1,0:T(8,128)(2,1)}) %all-gather.5.cloned.1.call-update) | async-done | bytes 15728656 | tf_op jit(solution)/shard_map/all_gather | solution.py:80
  241.6 1.5 constant_dynamic-update-slice_fusion.4
  243.0 1.6 fusion.6
  245.4 4.3 %all-to-all-start.10 = ((bf16[8,8,16,128]{3,2,1,0:T(8,128)(2,1)}), bf16[8,8,16,128]{3,2,1,0:T(8,128)(2,1)S(1)}, u32[]{:S(2)}, u32[]{:S(2)}) async-start(bf16[8,8,16,128]{3,2,1,0:T(8,128)(2,1)} %broadcast_in_dim.49), calls=%async_computation.10 | async-start | bytes 524288 | tf_op jit(solution)/shard_map/all_to_all | solution.py:9
  249.7 1.6 convolution_subtract_fusion.11
  251.3 1.6 convolution_subtract_fusion.13
  252.9 1.6 convolution_subtract_fusion.8
  254.5 1.6 convolution_subtract_fusion.5
  256.1 1.1 all-to-all-done.10
  257.3 1.5 constant_dynamic-update-slice_fusion.3
  258.8 1.6 fusion.7
  261.1 3.7 all-to-all-start.11
  264.9 1.6 convolution_subtract_fusion.10
  266.5 1.6 convolution_subtract_fusion.7
  268.1 1.6 convolution_subtract_fusion.4
  269.7 2.7 all-to-all-done.11
  272.4 1.5 constant_dynamic-update-slice_fusion.2
  273.9 1.6 fusion.5
  275.5 1.6 fusion.4
  277.2 1.6 fusion.3
  278.8 5.1 %collective-permute-start = (bf16[8,16,3,128]{3,0,1,2:T(8,128)(2,1)S(1)}, bf16[8,16,3,128]{3,0,1,2:T(8,128)(2,1)S(1)}, u32[]{:S(2)}, u32[]{:S(2)}) collective-permute-start(bf16[8,16,3,128]{3,0,1,2:T(8,128)(2,1)S(1)} %fusion.19), channel_id=1, source_target_pairs={{0,256},{128,384},{256,0},{384,128},{1,257},{129,385},{257,1},{385... | collective-permute-start | bytes 294920 | tf_op jit(solution)/shard_map/ppermute | solution.py:147
  283.9 2.9 collective-permute-done
  286.9 9.9 %all_to_all.85 = bf16[8,8,16,128]{3,2,1,0:T(8,128)(2,1)S(1)} all-to-all(bf16[8,8,16,128]{3,2,1,0:T(8,128)(2,1)S(1)} %broadcast_in_dim.51), channel_id=1, replica_groups=mesh['layer'=4,'prow'=16,'pcol'=8] {'pcol'}, dimensions={0} | all-to-all | bytes 524288 | tf_op jit(solution)/shard_map/all_to_all | solution.py:9
  296.9 32.8 %all-gather.7.cloned.1.call-done = bf16[96,128,256]{2,1,0:T(8,128)(2,1)} async-done(((bf16[6,128,256]{2,1,0:T(8,128)(2,1)}), bf16[96,128,256]{2,1,0:T(8,128)(2,1)}) %all-gather.7.cloned.1.call-update) | async-done | bytes 6291472 | tf_op jit(solution)/shard_map/all_gather | solution.py:80
  329.7 1.5 constant_dynamic-update-slice_fusion.1
  331.2 1.6 fusion.43
  333.5 4.1 all-to-all-start.13
  337.6 1.6 fusion.17
  339.2 5.9 %all-to-all-done.13 = bf16[8,8,16,128]{3,2,1,0:T(8,128)(2,1)S(1)} async-done(((bf16[8,8,16,128]{3,2,1,0:T(8,128)(2,1)}), bf16[8,8,16,128]{3,2,1,0:T(8,128)(2,1)S(1)}, u32[]{:S(2)}, u32[]{:S(2)}) %all-to-all-start.13) | async-done | bytes 262176 | tf_op jit(solution)/shard_map/all_to_all | solution.py:9
  345.2 1.5 constant_dynamic-update-slice_fusion
  346.7 1.6 fusion.41
  348.4 9.9 %all_to_all.86 = bf16[8,8,16,128]{3,2,1,0:T(8,128)(2,1)S(1)} all-to-all(bf16[8,8,16,128]{3,2,1,0:T(8,128)(2,1)S(1)} %broadcast_in_dim.53), channel_id=1, replica_groups=mesh['layer'=4,'prow'=16,'pcol'=8] {'pcol'}, dimensions={0} | all-to-all | bytes 524288 | tf_op jit(solution)/shard_map/all_to_all | solution.py:9
  358.4 1.5 fusion.15
  359.8 0.9 broadcast_in_dim.54
  360.8 9.5 %all-to-all-start.15 = ((bf16[32,6,8,256]{3,2,1,0:T(8,128)(2,1)}), bf16[32,6,8,256]{3,2,1,0:T(8,128)(2,1)S(1)}, u32[]{:S(2)}, u32[]{:S(2)}) async-start(bf16[32,6,8,256]{3,2,1,0:T(8,128)(2,1)} %broadcast_in_dim.54), calls=%async_computation.15 | async-start | bytes 1572864 | tf_op jit(solution)/shard_map/all_to_all | solution.py:35
  371.1 42.5 %all-to-all-done.15 = bf16[32,6,8,256]{3,2,1,0:T(8,128)(2,1)S(1)} async-done(((bf16[32,6,8,256]{3,2,1,0:T(8,128)(2,1)}), bf16[32,6,8,256]{3,2,1,0:T(8,128)(2,1)S(1)}, u32[]{:S(2)}, u32[]{:S(2)}) %all-to-all-start.15) | async-done | bytes 786464 | tf_op jit(solution)/shard_map/all_to_all | solution.py:35
  413.7 1.0 copy.181
  414.9 1.0 copy.182
  (61 shorter events, 10.5 us)
Async XLA Ops:
  7.2 135.0 %copy-start = (bf16[1,6,1,128,256]{4,3,2,1,0:T(8,128)(2,1)S(1)}, bf16[1,6,1,128,256]{4,3,2,1,0:T(8,128)(2,1)}, u32[]{:S(2)}) copy-start(bf16[1,6,1,128,256]{4,3,2,1,0:T(8,128)(2,1)} %param.17) | copy-start | bytes 1179652
  7.2 234.4 %all-gather.5.cloned.1.call-start = ((), (), s32[]{:S(2)}) async-start(), calls=%async_computation.16 | async-start | bytes 16711680 | tf_op jit(solution)/shard_map/all_gather | solution.py:80
  14.6 30.1 %all-to-all-start = ((bf16[16,16,256]{2,1,0:T(8,128)(2,1)}), bf16[16,16,256]{2,1,0:T(8,128)(2,1)S(1)}, u32[]{:S(2)}, u32[]{:S(2)}) async-start(bf16[16,16,256]{2,1,0:T(8,128)(2,1)} %bitcast.1), calls=%async_computation | async-start | bytes 262144 | tf_op jit(solution)/shard_map/all_to_all | solution.py:21
  29.8 299.9 %all-gather.7.cloned.1.call-start = ((), (), s32[]{:S(2)}) async-start(), calls=%async_computation.17 | async-start | bytes 6684672 | tf_op jit(solution)/shard_map/all_gather | solution.py:80
  45.4 19.2 %all-to-all-start.1 = ((bf16[16,16,256]{2,1,0:T(8,128)(2,1)}), bf16[16,16,256]{2,1,0:T(8,128)(2,1)S(1)}, u32[]{:S(2)}, u32[]{:S(2)}) async-start(bf16[16,16,256]{2,1,0:T(8,128)(2,1)} %broadcast_in_dim.40), calls=%async_computation.1 | async-start | bytes 262144 | tf_op jit(solution)/shard_map/all_to_all | solution.py:9
  101.1 20.0 %all-to-all-start.4 = ((bf16[16,16,256]{2,1,0:T(8,128)(2,1)}), bf16[16,16,256]{2,1,0:T(8,128)(2,1)S(1)}, u32[]{:S(2)}, u32[]{:S(2)}) async-start(bf16[16,16,256]{2,1,0:T(8,128)(2,1)} %broadcast_in_dim.44), calls=%async_computation.4 | async-start | bytes 262144 | tf_op jit(solution)/shard_map/all_to_all | solution.py:9
  135.9 20.0 %all-to-all-start.6 = ((bf16[16,16,256]{2,1,0:T(8,128)(2,1)}), bf16[16,16,256]{2,1,0:T(8,128)(2,1)S(1)}, u32[]{:S(2)}, u32[]{:S(2)}) async-start(bf16[16,16,256]{2,1,0:T(8,128)(2,1)} %bitcast.17), calls=%async_computation.6 | async-start | bytes 262144 | tf_op jit(solution)/shard_map/all_to_all | solution.py:21
  156.6 20.0 %all-to-all-start.7 = ((bf16[16,16,256]{2,1,0:T(8,128)(2,1)}), bf16[16,16,256]{2,1,0:T(8,128)(2,1)S(1)}, u32[]{:S(2)}, u32[]{:S(2)}) async-start(bf16[16,16,256]{2,1,0:T(8,128)(2,1)} %broadcast_in_dim.46), calls=%async_computation.7 | async-start | bytes 262144 | tf_op jit(solution)/shard_map/all_to_all | solution.py:9
  245.4 11.8 %all-to-all-start.10 = ((bf16[8,8,16,128]{3,2,1,0:T(8,128)(2,1)}), bf16[8,8,16,128]{3,2,1,0:T(8,128)(2,1)S(1)}, u32[]{:S(2)}, u32[]{:S(2)}) async-start(bf16[8,8,16,128]{3,2,1,0:T(8,128)(2,1)} %broadcast_in_dim.49), calls=%async_computation.10 | async-start | bytes 524288 | tf_op jit(solution)/shard_map/all_to_all | solution.py:9
  261.1 11.3 %all-to-all-start.11 = ((bf16[8,8,16,128]{3,2,1,0:T(8,128)(2,1)}), bf16[8,8,16,128]{3,2,1,0:T(8,128)(2,1)S(1)}, u32[]{:S(2)}, u32[]{:S(2)}) async-start(bf16[8,8,16,128]{3,2,1,0:T(8,128)(2,1)} %broadcast_in_dim.50), calls=%async_computation.11 | async-start | bytes 524288 | tf_op jit(solution)/shard_map/all_to_all | solution.py:9
  278.8 8.0 %collective-permute-start = (bf16[8,16,3,128]{3,0,1,2:T(8,128)(2,1)S(1)}, bf16[8,16,3,128]{3,0,1,2:T(8,128)(2,1)S(1)}, u32[]{:S(2)}, u32[]{:S(2)}) collective-permute-start(bf16[8,16,3,128]{3,0,1,2:T(8,128)(2,1)S(1)} %fusion.19), channel_id=1, source_target_pairs={{0,256},{128,384},{256,0},{384,128},{1,257},{129,385},{257,1},{385... | collective-permute-start | bytes 294920 | tf_op jit(solution)/shard_map/ppermute | solution.py:147
  333.5 11.6 %all-to-all-start.13 = ((bf16[8,8,16,128]{3,2,1,0:T(8,128)(2,1)}), bf16[8,8,16,128]{3,2,1,0:T(8,128)(2,1)S(1)}, u32[]{:S(2)}, u32[]{:S(2)}) async-start(bf16[8,8,16,128]{3,2,1,0:T(8,128)(2,1)} %broadcast_in_dim.52), calls=%async_computation.13 | async-start | bytes 524288 | tf_op jit(solution)/shard_map/all_to_all | solution.py:9
  360.8 52.8 %all-to-all-start.15 = ((bf16[32,6,8,256]{3,2,1,0:T(8,128)(2,1)}), bf16[32,6,8,256]{3,2,1,0:T(8,128)(2,1)S(1)}, u32[]{:S(2)}, u32[]{:S(2)}) async-start(bf16[32,6,8,256]{3,2,1,0:T(8,128)(2,1)} %broadcast_in_dim.54), calls=%async_computation.15 | async-start | bytes 1572864 | tf_op jit(solution)/shard_map/all_to_all | solution.py:35
Sparse Core Ops, SparseCore 0:
  12.0 229.5 all-gather.4
  244.2 85.4 all-gather.6

commit v3 on v2

--- a/solution.py
+++ b/solution.py
@@ -35,6 +35,10 @@
     return lax.all_to_all(
         pieces, ("layer", "prow"), 0, 0, axis_index_groups=sibling_groups()
     )
+
+
+def among_layers(pieces):
+    return lax.all_to_all(pieces, ("layer", "prow"), 0, 0)
 
 
 def own_solve(own_cols, own_inv, own_rows, shared_turned):
@@ -72,17 +76,13 @@
     return solved, beyond
 
 
-def gathered_columns(inverses, blocks):
-    tile_rows, cycles = blocks.shape[-4], blocks.shape[-3]
-    stacked = jnp.concatenate(
-        [part.reshape(-1, tile_rows, cycles * blocks.shape[-1]) for part in (inverses, blocks)]
-    )
-    return lax.all_gather(stacked, "prow")
+def as_blocks(stored):
+    tile_rows, cycles = stored.shape[-4], stored.shape[-3]
+    return stored.reshape(-1, tile_rows, cycles * stored.shape[-1])
 
 
 def slice_solve(sums, gathered, panels):
-    width, prows, targets, tile_rows = sums.shape
-    sums = [sums[:, :, t] for t in range(targets)]
+    sums = [sums[:, :, t] for t in range(panels)]
     solved = []
     offset = panels
     for step in range(panels):
@@ -94,15 +94,15 @@
             preferred_element_type=jnp.float32,
         ).astype(jnp.bfloat16)
         solved.append(result)
-        for target in range(step + 1, targets):
+        for target in range(step + 1, panels):
             sums[target] = sums[target] - lax.dot_general(
                 result,
                 gathered[:, offset + target - step - 1],
                 (((1,), (2,)), ((), ())),
                 preferred_element_type=jnp.float32,
             )
-        offset += targets - 1 - step
-    return jnp.stack(solved), sums[panels:]
+        offset += panels - 1 - step
+    return jnp.stack(solved)
 
 
 def local(
@@ -120,12 +120,22 @@
     cycles = own_blocks.shape[4]
     col_width = cycles * tile_rows
     rhs_width = own_rhs.shape[-1]
-    prows = lax.axis_size("prow")
-    siblings = 2 * prows
-    share = rhs_width // siblings
     panels = own_inverse.shape[1]
-    pair_all = gathered_columns(pair_inverse, pair_blocks)
-    root_all = gathered_columns(root_inverse, root_blocks)
+    layers, prows = lax.axis_size("layer"), lax.axis_size("prow")
+
+    pair_cols = as_blocks(pair_blocks)
+    inside, outside = [], []
+    offset = 0
+    for step in range(panels):
+        cut = offset + panels - 1 - step
+        inside.append(pair_cols[offset:cut])
+        outside.append(pair_cols[cut : cut + panels])
+        offset = cut + panels
+    pair_all = lax.all_gather(jnp.concatenate([as_blocks(pair_inverse)] + inside), "prow")
+    root_all = lax.all_gather(
+        jnp.concatenate([as_blocks(root_inverse), as_blocks(root_blocks)]), "prow"
+    )
+
     own_tiles = own_blocks.reshape(-1, tile_rows, cycles, tile_rows)
     kept_tiles = own_pattern.reshape(-1, 1, cycles, 1) > 0
     own_cols = jnp.where(kept_tiles, own_tiles, jnp.zeros((), own_tiles.dtype)).reshape(
@@ -137,22 +147,37 @@
 
     own_solved, beyond = own_solve(own_cols, own_inv, own_rows, shared_turned)
 
-    pieces = beyond.astype(jnp.bfloat16).reshape(siblings, share, 2 * panels, tile_rows)
-    received = among_siblings(pieces).reshape(2, prows, share, 2 * panels, tile_rows)
+    share = rhs_width // (2 * prows)
+    pieces = beyond[:, :panels].astype(jnp.bfloat16)
+    received = among_siblings(pieces.reshape(2 * prows, share, panels, tile_rows))
+    received = received.reshape(2, prows, share, panels, tile_rows)
     sums = jnp.sum(received.astype(jnp.float32), axis=0).transpose(1, 0, 2, 3)
-    pair_solved, left = slice_solve(sums, pair_all, panels)
-
-    joined = jnp.stack(left, axis=2)
-    swap = [(i, i ^ 2) for i in range(lax.axis_size("layer"))]
-    joined = joined + lax.ppermute(joined.astype(jnp.bfloat16), "layer", swap).astype(joined.dtype)
-    root_solved, _ = slice_solve(joined, root_all, panels)
-
-    both = jnp.concatenate([pair_solved, root_solved])
-    copies = jnp.broadcast_to(both[None], (siblings,) + both.shape)
-    whole = among_siblings(copies)
-    whole = whole.transpose(1, 3, 0, 2).reshape(2, 1, panels, cycles, 1, tile_rows, rhs_width)
-    own_out = jnp.stack(own_solved).reshape(1, panels, cycles, 1, tile_rows, rhs_width)
-    return own_out, whole[0], whole[1]
+    pair_solved = slice_solve(sums, pair_all, panels)
+    copies = jnp.broadcast_to(pair_solved[None], (2 * prows,) + pair_solved.shape)
+    pair_turned = among_siblings(copies).transpose(1, 0, 2, 3).reshape(panels, rhs_width, col_width)
+
+    left = beyond[:, panels:]
+    for step in range(panels):
+        left = left - 0.5 * lax.dot_general(
+            pair_turned[step],
+            outside[step],
+            (((1,), (2,)), ((), ())),
+            preferred_element_type=jnp.float32,
+        )
+    share = rhs_width // (layers * prows)
+    pieces = left.astype(jnp.bfloat16).reshape(layers * prows, share, panels, tile_rows)
+    received = among_layers(pieces).reshape(layers, prows, share, panels, tile_rows)
+    sums = jnp.sum(received.astype(jnp.float32), axis=0).transpose(1, 0, 2, 3)
+    root_solved = slice_solve(sums, root_all, panels)
+    by_layer = shared_with_all(shared_with_all(root_solved, "prow"), "layer")
+    root_turned = by_layer.transpose(2, 0, 1, 3, 4).reshape(panels, rhs_width, col_width)
+
+    shape = (1, panels, cycles, 1, tile_rows, rhs_width)
+    return (
+        jnp.stack(own_solved).reshape(shape),
+        pair_turned.transpose(0, 2, 1).reshape(shape),
+        root_turned.transpose(0, 2, 1).reshape(shape),
+    )
 
 
 def solution(mesh):

time: 425 us -> 375 us (0.88)
  waiting for transfers between devices: 170 us -> 108 us
  blocking collectives: 114 us -> 153 us
  matrix products: 38.9 us -> 25.2 us
  starting transfers between devices: 61.8 us -> 50.2 us
    all_gather x2, waiting for transfers between devices: 50.1 us -> 0.04 us  [the longest x1 0.02 us: local(): lax.all_gather(jnp.concatenate([as_blocks(pair_inverse)] + inside), 'prow')]
    all_to_all x5 -> x7, blocking collectives: 57.1 us -> 82.2 us  [shared_with_all(): return lax.all_to_all(copies, axis, 0, 0)]
    all_to_all x0 -> x1, blocking collectives: none -> 24.2 us  [among_layers(): return lax.all_to_all(pieces, ('layer', 'prow'), 0, 0)]
    all_to_all x1, waiting for transfers between devices: 42.5 us -> 25.7 us  [among_siblings(): lax.all_to_all(pieces, ('layer', 'prow'), 0, 0, axis_index_groups=sibling...]
    dot_general x15 -> x6, matrix products: 24.1 us -> 9.63 us  [slice_solve(): lax.dot_general(result, gathered[:, offset + target - step - 1], (((1,),...]
    all_to_all x1, blocking collectives: 37.1 us -> 26.6 us  [among_siblings(): lax.all_to_all(pieces, ('layer', 'prow'), 0, 0, axis_index_groups=sibling...]
    all_to_all x6, waiting for transfers between devices: 50.6 us -> 58 us  [shared_with_all(): return lax.all_to_all(copies, axis, 0, 0)]
    ppermute x1 -> x0, starting transfers between devices: 5.11 us -> none  [local(): lax.ppermute(joined.astype(jnp.bfloat16), 'layer', swap)]
  transfers between devices with their start and end apart: 12 -> 11, of which waited for: 12 -> 9; matrix products, arithmetic and copies ran while one was open for 11% -> 9% of each run, Pallas kernels for 0% -> 0%
where the time goes in v3:
time: 375 us; the launch traced here: 373 us
  blocking collectives  153 us (41%)
  waiting for transfers between devices  108 us (29%)
  starting transfers between devices  50.2 us (13%)
  matrix products  25.2 us (7%)
  local copies, waits for them, and re-layouts  17.2 us (5%)
  between operations  14.6 us (4%)
  other arithmetic  4.79 us (1%)
    all_to_all x7, blocking collectives, shared_with_all(): return lax.all_to_all(copies, axis, 0, 0)  82.2 us
    all_to_all x6, waiting for transfers between devices, shared_with_all(): return lax.all_to_all(copies, axis, 0, 0)  58 us
    all_to_all x1, blocking collectives, among_siblings(): lax.all_to_all(pieces, ('layer', 'prow'), 0, 0, axis_index_groups=sibling...  26.6 us
    all_to_all x1, waiting for transfers between devices, among_siblings(): lax.all_to_all(pieces, ('layer', 'prow'), 0, 0, axis_index_groups=sibling...  25.7 us
    all_to_all x6, starting transfers between devices, shared_with_all(): return lax.all_to_all(copies, axis, 0, 0)  25.2 us
    all_to_all x1, blocking collectives, among_layers(): return lax.all_to_all(pieces, ('layer', 'prow'), 0, 0)  24.2 us
    all_to_all x2, waiting for transfers between devices, column_total(): received = lax.all_to_all(pieces, 'prow', 0, 0)  24.1 us
    all_to_all x2, starting transfers between devices, column_total(): received = lax.all_to_all(pieces, 'prow', 0, 0)  20.2 us
  transfers between devices with their start and end apart: 11, of which 9 were waited for; matrix products, arithmetic and copies ran while one was open for 9% of the time, Pallas kernels for 0%

profile of v3, /device:TPU:32, one launch (start us, length us, event | category | flops | bytes accessed | tf_op | source)
XLA Modules:
  0.0 372.7 jit_solution(2604345407770223579)
XLA Ops:
  7.2 1.1 slice.176
  8.3 0.9 slice.178
  9.3 1.1 reshape.154
  10.4 0.8 pad_maximum_fusion.1
  11.2 1.0 fusion.56
  12.3 1.7 convolution_convert_fusion.2
  14.0 15.2 %all-to-all-start = ((bf16[16,16,256]{2,1,0:T(8,128)(2,1)}), bf16[16,16,256]{2,1,0:T(8,128)(2,1)S(1)}, u32[]{:S(2)}, u32[]{:S(2)}) async-start(bf16[16,16,256]{2,1,0:T(8,128)(2,1)} %bitcast.1), calls=%async_computation | async-start | bytes 262144 | tf_op jit(solution)/shard_map/all_to_all | solution.py:21
  29.3 1.1 reshape.158
  30.3 1.1 reshape.159
  31.4 0.8 pad_maximum_fusion.2
  32.2 0.7 broadcast_compare_fusion
  33.0 11.1 %all-to-all-done = bf16[16,16,256]{2,1,0:T(8,128)(2,1)S(1)} async-done(((bf16[16,16,256]{2,1,0:T(8,128)(2,1)}), bf16[16,16,256]{2,1,0:T(8,128)(2,1)S(1)}, u32[]{:S(2)}, u32[]{:S(2)}) %all-to-all-start) | async-done | bytes 131104 | tf_op jit(solution)/shard_map/all_to_all | solution.py:21
  44.1 0.7 broadcast_in_dim.44
  44.8 4.7 %all-to-all-start.1 = ((bf16[16,16,256]{2,1,0:T(8,128)(2,1)}), bf16[16,16,256]{2,1,0:T(8,128)(2,1)S(1)}, u32[]{:S(2)}, u32[]{:S(2)}) async-start(bf16[16,16,256]{2,1,0:T(8,128)(2,1)} %broadcast_in_dim.44), calls=%async_computation.1 | async-start | bytes 262144 | tf_op jit(solution)/shard_map/all_to_all | solution.py:9
  49.5 1.2 broadcast_select_fusion
  50.9 13.0 %all-to-all-done.1 = bf16[16,16,256]{2,1,0:T(8,128)(2,1)S(1)} async-done(((bf16[16,16,256]{2,1,0:T(8,128)(2,1)}), bf16[16,16,256]{2,1,0:T(8,128)(2,1)S(1)}, u32[]{:S(2)}, u32[]{:S(2)}) %all-to-all-start.1) | async-done | bytes 131104 | tf_op jit(solution)/shard_map/all_to_all | solution.py:9
  64.1 14.5 %all_to_all.95 = bf16[8,128,256]{2,1,0:T(8,128)(2,1)S(1)} all-to-all(bf16[8,128,256]{2,1,0:T(8,128)(2,1)S(1)} %broadcast_in_dim.47), channel_id=1, replica_groups=mesh['layer'=4,'prow'=16,'pcol'=8] {'pcol'}, dimensions={0} | all-to-all | bytes 1048576 | tf_op jit(solution)/shard_map/all_to_all | solution.py:9
  78.7 1.1 convolution_convert_fusion.1
  79.8 19.9 %all_to_all.96 = bf16[16,16,256]{2,1,0:T(8,128)(2,1)S(1)} all-to-all(bf16[16,16,256]{2,1,0:T(8,128)(2,1)S(1)} %bitcast.325), channel_id=1, replica_groups=mesh['layer'=4,'prow'=16,'pcol'=8] {'prow'}, dimensions={0} | all-to-all | bytes 262144 | tf_op jit(solution)/shard_map/all_to_all | solution.py:21
  99.6 0.7 broadcast_in_dim.48
  100.3 5.1 %all-to-all-start.4 = ((bf16[16,16,256]{2,1,0:T(8,128)(2,1)}), bf16[16,16,256]{2,1,0:T(8,128)(2,1)S(1)}, u32[]{:S(2)}, u32[]{:S(2)}) async-start(bf16[16,16,256]{2,1,0:T(8,128)(2,1)} %broadcast_in_dim.48), calls=%async_computation.4 | async-start | bytes 262144 | tf_op jit(solution)/shard_map/all_to_all | solution.py:9
  105.6 14.7 %all-to-all-done.4 = bf16[16,16,256]{2,1,0:T(8,128)(2,1)S(1)} async-done(((bf16[16,16,256]{2,1,0:T(8,128)(2,1)}), bf16[16,16,256]{2,1,0:T(8,128)(2,1)S(1)}, u32[]{:S(2)}, u32[]{:S(2)}) %all-to-all-start.4) | async-done | bytes 131104 | tf_op jit(solution)/shard_map/all_to_all | solution.py:9
  120.5 12.8 %all_to_all.97 = bf16[8,128,256]{2,1,0:T(8,128)(2,1)S(1)} all-to-all(bf16[8,128,256]{2,1,0:T(8,128)(2,1)S(1)} %broadcast_in_dim.49), channel_id=1, replica_groups=mesh['layer'=4,'prow'=16,'pcol'=8] {'pcol'}, dimensions={0} | all-to-all | bytes 1048576 | tf_op jit(solution)/shard_map/all_to_all | solution.py:9
  133.4 1.7 convolution_convert_fusion
  135.1 5.0 %all-to-all-start.6 = ((bf16[16,16,256]{2,1,0:T(8,128)(2,1)}), bf16[16,16,256]{2,1,0:T(8,128)(2,1)S(1)}, u32[]{:S(2)}, u32[]{:S(2)}) async-start(bf16[16,16,256]{2,1,0:T(8,128)(2,1)} %bitcast.17), calls=%async_computation.6 | async-start | bytes 262144 | tf_op jit(solution)/shard_map/all_to_all | solution.py:21
  140.1 1.0 fusion.53
  142.2 12.9 %all-to-all-done.6 = bf16[16,16,256]{2,1,0:T(8,128)(2,1)S(1)} async-done(((bf16[16,16,256]{2,1,0:T(8,128)(2,1)}), bf16[16,16,256]{2,1,0:T(8,128)(2,1)S(1)}, u32[]{:S(2)}, u32[]{:S(2)}) %all-to-all-start.6) | async-done | bytes 131104 | tf_op jit(solution)/shard_map/all_to_all | solution.py:21
  155.2 0.7 broadcast_in_dim.50
  155.8 5.1 %all-to-all-start.7 = ((bf16[16,16,256]{2,1,0:T(8,128)(2,1)}), bf16[16,16,256]{2,1,0:T(8,128)(2,1)S(1)}, u32[]{:S(2)}, u32[]{:S(2)}) async-start(bf16[16,16,256]{2,1,0:T(8,128)(2,1)} %broadcast_in_dim.50), calls=%async_computation.7 | async-start | bytes 262144 | tf_op jit(solution)/shard_map/all_to_all | solution.py:9
  161.6 14.3 %all-to-all-done.7 = bf16[16,16,256]{2,1,0:T(8,128)(2,1)S(1)} async-done(((bf16[16,16,256]{2,1,0:T(8,128)(2,1)}), bf16[16,16,256]{2,1,0:T(8,128)(2,1)S(1)}, u32[]{:S(2)}, u32[]{:S(2)}) %all-to-all-start.7) | async-done | bytes 131104 | tf_op jit(solution)/shard_map/all_to_all | solution.py:9
  176.3 26.6 %all_to_all.98 = bf16[32,8,3,128]{3,1,2,0:T(8,128)(2,1)S(1)} all-to-all(bf16[32,8,3,128]{3,1,2,0:T(8,128)(2,1)S(1)} %copy.117), channel_id=1, replica_groups={{0,8,16,24,32,40,48,56,64,72,80,88,96,104,112,120,128,136,144,152,160,1..., dimensions={0} | all-to-all | bytes 393216 | tf_op jit(solution)/shard_map/all_to_all | solution.py:35
  203.1 9.9 %all_to_all.99 = bf16[8,8,16,128]{3,2,1,0:T(8,128)(2,1)S(1)} all-to-all(bf16[8,8,16,128]{3,2,1,0:T(8,128)(2,1)S(1)} %broadcast_in_dim.52), channel_id=1, replica_groups=mesh['layer'=4,'prow'=16,'pcol'=8] {'pcol'}, dimensions={0} | all-to-all | bytes 524288 | tf_op jit(solution)/shard_map/all_to_all | solution.py:9
  213.1 1.5 fusion.9
  214.6 1.6 fusion.5
  216.2 0.7 broadcast_in_dim.53
  217.0 3.4 all-to-all-start.10
  220.4 1.6 convolution_subtract_fusion.4
  222.0 5.8 %all-to-all-done.10 = bf16[8,8,16,128]{3,2,1,0:T(8,128)(2,1)S(1)} async-done(((bf16[8,8,16,128]{3,2,1,0:T(8,128)(2,1)}), bf16[8,8,16,128]{3,2,1,0:T(8,128)(2,1)S(1)}, u32[]{:S(2)}, u32[]{:S(2)}) %all-to-all-start.10) | async-done | bytes 262176 | tf_op jit(solution)/shard_map/all_to_all | solution.py:9
  227.9 1.5 fusion.10
  229.4 1.6 fusion.6
  231.0 9.9 %all_to_all.100 = bf16[8,8,16,128]{3,2,1,0:T(8,128)(2,1)S(1)} all-to-all(bf16[8,8,16,128]{3,2,1,0:T(8,128)(2,1)S(1)} %broadcast_in_dim.54), channel_id=1, replica_groups=mesh['layer'=4,'prow'=16,'pcol'=8] {'pcol'}, dimensions={0} | all-to-all | bytes 524288 | tf_op jit(solution)/shard_map/all_to_all | solution.py:9
  241.0 1.5 fusion.12
  242.5 0.8 broadcast_in_dim.55
  243.3 4.8 %all-to-all-start.12 = ((bf16[32,3,8,256]{3,2,1,0:T(8,128)(2,1)}), bf16[32,3,8,256]{3,2,1,0:T(8,128)(2,1)S(1)}, u32[]{:S(2)}, u32[]{:S(2)}) async-start(bf16[32,3,8,256]{3,2,1,0:T(8,128)(2,1)} %broadcast_in_dim.55), calls=%async_computation.12 | async-start | bytes 786432 | tf_op jit(solution)/shard_map/all_to_all | solution.py:35
  248.9 25.7 %all-to-all-done.12 = bf16[32,3,8,256]{3,2,1,0:T(8,128)(2,1)S(1)} async-done(((bf16[32,3,8,256]{3,2,1,0:T(8,128)(2,1)}), bf16[32,3,8,256]{3,2,1,0:T(8,128)(2,1)S(1)}, u32[]{:S(2)}, u32[]{:S(2)}) %all-to-all-start.12) | async-done | bytes 393248 | tf_op jit(solution)/shard_map/all_to_all | solution.py:35
  275.5 24.2 %all_to_all.101 = bf16[64,4,3,128]{3,1,2,0:T(4,128)(2,1)S(1)} all-to-all(bf16[64,4,3,128]{3,1,2,0:T(4,128)(2,1)S(1)} %copy.132), channel_id=1, replica_groups=mesh['layer'=4,'prow'=16,'pcol'=8] {'layer','prow'}, dimensions={0} | all-to-all | bytes 393216 | tf_op jit(solution)/shard_map/all_to_all | solution.py:41
  299.9 8.5 %all_to_all.102 = bf16[8,4,16,128]{3,2,1,0:T(8,128)(2,1)S(1)} all-to-all(bf16[8,4,16,128]{3,2,1,0:T(8,128)(2,1)S(1)} %broadcast_in_dim.56), channel_id=1, replica_groups=mesh['layer'=4,'prow'=16,'pcol'=8] {'pcol'}, dimensions={0} | all-to-all | bytes 262144 | tf_op jit(solution)/shard_map/all_to_all | solution.py:9
  308.5 1.5 fusion.13
  310.0 1.6 fusion.7
  311.6 0.7 broadcast_in_dim.57
  312.3 3.4 all-to-all-start.15
  315.6 1.6 convolution_subtract_fusion.7
  317.2 4.5 %all-to-all-done.15 = bf16[8,4,16,128]{3,2,1,0:T(8,128)(2,1)S(1)} async-done(((bf16[8,4,16,128]{3,2,1,0:T(8,128)(2,1)}), bf16[8,4,16,128]{3,2,1,0:T(8,128)(2,1)S(1)}, u32[]{:S(2)}, u32[]{:S(2)}) %all-to-all-start.15) | async-done | bytes 131104 | tf_op jit(solution)/shard_map/all_to_all | solution.py:9
  321.7 1.5 fusion.14
  323.2 1.6 fusion.8
  324.9 8.5 %all_to_all.103 = bf16[8,4,16,128]{3,2,1,0:T(8,128)(2,1)S(1)} all-to-all(bf16[8,4,16,128]{3,2,1,0:T(8,128)(2,1)S(1)} %broadcast_in_dim.58), channel_id=1, replica_groups=mesh['layer'=4,'prow'=16,'pcol'=8] {'pcol'}, dimensions={0} | all-to-all | bytes 262144 | tf_op jit(solution)/shard_map/all_to_all | solution.py:9
  333.4 1.5 fusion.16
  334.9 18.0 %all_to_all.104 = bf16[16,3,4,256]{3,2,1,0:T(4,128)(2,1)S(1)} all-to-all(bf16[16,3,4,256]{3,2,1,0:T(4,128)(2,1)S(1)} %broadcast_in_dim.59), channel_id=1, replica_groups=mesh['layer'=4,'prow'=16,'pcol'=8] {'prow'}, dimensions={0} | all-to-all | bytes 196608 | tf_op jit(solution)/shard_map/all_to_all | solution.py:9
  353.0 0.9 broadcast_in_dim.60
  353.9 3.5 all-to-all-start.18
  357.4 0.8 pad_maximum_fusion
  358.1 0.9 copy.157
  359.1 5.6 %all-to-all-done.18 = bf16[4,16,3,4,256]{4,3,1,2,0:T(4,128)(2,1)S(1)} async-done(((bf16[4,16,3,4,256]{4,3,1,2,0:T(4,128)(2,1)}), bf16[4,16,3,4,256]{4,3,1,2,0:T(4,128)(2,1)S(1)}, u32[]{:S(2)}, u32[]{:S(2)}) %all-to-all-start.18) | async-done | bytes 393248 | tf_op jit(solution)/shard_map/all_to_all | solution.py:9
  365.0 0.9 copy.158
  (72 shorter events, 5.8 us)
Async XLA Ops:
  7.2 42.3 %copy-start = (bf16[1,21,1,128,2,1,128]{6,4,5,3,2,1,0:T(2,128)(2,1)S(1)}, bf16[1,21,1,128,2,1,128]{6,4,5,3,2,1,0:T(2,128)(2,1)}, u32[]{:S(2)}) copy-start(bf16[1,21,1,128,2,1,128]{6,4,5,3,2,1,0:T(2,128)(2,1)} %param.9) | copy-start | bytes 4128772
  7.2 205.9 %all-gather.5.cloned.1.call-start = ((), (), s32[]{:S(2)}) async-start(), calls=%async_computation.19 | async-start | bytes 6684672 | tf_op jit(solution)/shard_map/all_gather | solution.py:134
  14.0 30.1 %all-to-all-start = ((bf16[16,16,256]{2,1,0:T(8,128)(2,1)}), bf16[16,16,256]{2,1,0:T(8,128)(2,1)S(1)}, u32[]{:S(2)}, u32[]{:S(2)}) async-start(bf16[16,16,256]{2,1,0:T(8,128)(2,1)} %bitcast.1), calls=%async_computation | async-start | bytes 262144 | tf_op jit(solution)/shard_map/all_to_all | solution.py:21
  29.2 279.3 %all-gather.7.cloned.1.call-start = ((), (), s32[]{:S(2)}) async-start(), calls=%async_computation.20 | async-start | bytes 6684672 | tf_op jit(solution)/shard_map/all_gather | solution.py:135
  44.8 19.1 %all-to-all-start.1 = ((bf16[16,16,256]{2,1,0:T(8,128)(2,1)}), bf16[16,16,256]{2,1,0:T(8,128)(2,1)S(1)}, u32[]{:S(2)}, u32[]{:S(2)}) async-start(bf16[16,16,256]{2,1,0:T(8,128)(2,1)} %broadcast_in_dim.44), calls=%async_computation.1 | async-start | bytes 262144 | tf_op jit(solution)/shard_map/all_to_all | solution.py:9
  49.5 91.9 %copy-start.2 = (bf16[1,6,1,128,256]{4,3,2,1,0:T(8,128)(2,1)S(1)}, bf16[1,6,1,128,256]{4,3,2,1,0:T(8,128)(2,1)}, u32[]{:S(2)}) copy-start(bf16[1,6,1,128,256]{4,3,2,1,0:T(8,128)(2,1)} %param.17) | copy-start | bytes 1179652
  100.3 20.0 %all-to-all-start.4 = ((bf16[16,16,256]{2,1,0:T(8,128)(2,1)}), bf16[16,16,256]{2,1,0:T(8,128)(2,1)S(1)}, u32[]{:S(2)}, u32[]{:S(2)}) async-start(bf16[16,16,256]{2,1,0:T(8,128)(2,1)} %broadcast_in_dim.48), calls=%async_computation.4 | async-start | bytes 262144 | tf_op jit(solution)/shard_map/all_to_all | solution.py:9
  135.1 20.0 %all-to-all-start.6 = ((bf16[16,16,256]{2,1,0:T(8,128)(2,1)}), bf16[16,16,256]{2,1,0:T(8,128)(2,1)S(1)}, u32[]{:S(2)}, u32[]{:S(2)}) async-start(bf16[16,16,256]{2,1,0:T(8,128)(2,1)} %bitcast.17), calls=%async_computation.6 | async-start | bytes 262144 | tf_op jit(solution)/shard_map/all_to_all | solution.py:21
  155.8 20.1 %all-to-all-start.7 = ((bf16[16,16,256]{2,1,0:T(8,128)(2,1)}), bf16[16,16,256]{2,1,0:T(8,128)(2,1)S(1)}, u32[]{:S(2)}, u32[]{:S(2)}) async-start(bf16[16,16,256]{2,1,0:T(8,128)(2,1)} %broadcast_in_dim.50), calls=%async_computation.7 | async-start | bytes 262144 | tf_op jit(solution)/shard_map/all_to_all | solution.py:9
  176.3 71.7 %copy-start.1 = (bf16[1,12,1,128,2,1,128]{6,4,5,3,2,1,0:T(2,128)(2,1)S(1)}, bf16[1,12,1,128,2,1,128]{6,4,5,3,2,1,0:T(2,128)(2,1)}, u32[]{:S(2)}) copy-start(bf16[1,12,1,128,2,1,128]{6,4,5,3,2,1,0:T(2,128)(2,1)} %param.12) | copy-start | bytes 2359300
  217.0 10.9 %all-to-all-start.10 = ((bf16[8,8,16,128]{3,2,1,0:T(8,128)(2,1)}), bf16[8,8,16,128]{3,2,1,0:T(8,128)(2,1)S(1)}, u32[]{:S(2)}, u32[]{:S(2)}) async-start(bf16[8,8,16,128]{3,2,1,0:T(8,128)(2,1)} %broadcast_in_dim.53), calls=%async_computation.10 | async-start | bytes 524288 | tf_op jit(solution)/shard_map/all_to_all | solution.py:9
  243.3 31.3 %all-to-all-start.12 = ((bf16[32,3,8,256]{3,2,1,0:T(8,128)(2,1)}), bf16[32,3,8,256]{3,2,1,0:T(8,128)(2,1)S(1)}, u32[]{:S(2)}, u32[]{:S(2)}) async-start(bf16[32,3,8,256]{3,2,1,0:T(8,128)(2,1)} %broadcast_in_dim.55), calls=%async_computation.12 | async-start | bytes 786432 | tf_op jit(solution)/shard_map/all_to_all | solution.py:35
  312.3 9.4 %all-to-all-start.15 = ((bf16[8,4,16,128]{3,2,1,0:T(8,128)(2,1)}), bf16[8,4,16,128]{3,2,1,0:T(8,128)(2,1)S(1)}, u32[]{:S(2)}, u32[]{:S(2)}) async-start(bf16[8,4,16,128]{3,2,1,0:T(8,128)(2,1)} %broadcast_in_dim.57), calls=%async_computation.15 | async-start | bytes 262144 | tf_op jit(solution)/shard_map/all_to_all | solution.py:9
  353.9 10.8 %all-to-all-start.18 = ((bf16[4,16,3,4,256]{4,3,1,2,0:T(4,128)(2,1)}), bf16[4,16,3,4,256]{4,3,1,2,0:T(4,128)(2,1)S(1)}, u32[]{:S(2)}, u32[]{:S(2)}) async-start(bf16[4,16,3,4,256]{4,3,1,2,0:T(4,128)(2,1)} %broadcast_in_dim.60), calls=%async_computation.18 | async-start | bytes 786432 | tf_op jit(solution)/shard_map/all_to_all | solution.py:9
Sparse Core Ops, SparseCore 0:
  11.4 107.3 all-gather.4
  121.4 104.0 all-gather.6

commit v4 on v3

v4 whole, which is shorter than its diff:
```python
import jax
import jax.numpy as jnp
from jax import lax
from jax.sharding import PartitionSpec as P


def shared_with_all(value, axis):
    copies = jnp.broadcast_to(value[None], (lax.axis_size(axis),) + value.shape)
    return lax.all_to_all(copies, axis, 0, 0)


def row_total(partial_value):
    partials = shared_with_all(partial_value.astype(jnp.bfloat16), "pcol")
    return jnp.sum(partials.astype(jnp.float32), axis=0)


def transposed_product(solved, blocks):
    return lax.dot_general(
        solved,
        blocks,
        (((solved.ndim - 1,), (blocks.ndim - 1,)), ((), ())),
        preferred_element_type=jnp.float32,
    )


def column_total(partial_value):
    ways = lax.axis_size("prow")
    rows, width = partial_value.shape
    pieces = partial_value.reshape(ways, rows // ways, width)
    received = lax.all_to_all(pieces, "prow", 0, 0)
    piece = jnp.sum(received.astype(jnp.float32), axis=0).astype(jnp.bfloat16)
    return shared_with_all(piece, "prow").reshape(rows, width)


def inverse_product(inverse, residual):
    return lax.dot_general(
        inverse,
        residual.astype(jnp.bfloat16),
        (((0,), (0,)), ((), ())),
        preferred_element_type=jnp.float32,
    ).astype(jnp.bfloat16)


def layer_swap(value, apart):
    return lax.ppermute(value, "layer", [(i, i ^ apart) for i in range(lax.axis_size("layer"))])


def as_blocks(stored):
    tile_rows, cycles = stored.shape[-4], stored.shape[-3]
    return stored.reshape(-1, tile_rows, cycles * stored.shape[-1])


def by_column(cols, panels, chain_length):
    inside, outside = [], []
    offset = 0
    for step in range(panels):
        cut = offset + panels - 1 - step
        inside.append(cols[offset:cut])
        offset += chain_length - 1 - step
        outside.append(cols[cut:offset])
    return inside, outside


def slice_solve(sums, gathered, panels):
    sums = [sums[:, :, t] for t in range(panels)]
    solved = []
    offset = panels
    for step in range(panels):
        residual = row_total(sums[step]).astype(jnp.bfloat16)
        result = lax.dot_general(
            residual,
            gathered[:, step],
            (((1, 2), (0, 1)), ((), ())),
            preferred_element_type=jnp.float32,
        ).astype(jnp.bfloat16)
        solved.append(result)
        for target in range(step + 1, panels):
            sums[target] = sums[target] - transposed_product(
                result, gathered[:, offset + target - step - 1]
            )
        offset += panels - 1 - step
    return jnp.stack(solved)


def local(
    own_blocks,
    own_pattern,
    own_inverse,
    pair_blocks,
    pair_inverse,
    root_blocks,
    root_inverse,
    own_rhs,
    shared_rhs,
):
    tile_rows = own_blocks.shape[3]
    cycles = own_blocks.shape[4]
    col_width = cycles * tile_rows
    rhs_width = own_rhs.shape[-1]
    panels = own_inverse.shape[1]
    layers, prows = lax.axis_size("layer"), lax.axis_size("prow")
    second = lax.axis_index("layer") % 2
    wide = rhs_width // prows
    half = wide // 2
    narrow = wide // layers

    own_inv = own_inverse.reshape(-1, tile_rows, col_width)
    own_rows = own_rhs.reshape(-1, tile_rows, rhs_width)
    first_partial = inverse_product(own_inv[0], own_rows[0])
    (
        first_partial,
        own_blocks,
        own_pattern,
        pair_blocks,
        pair_inverse,
        root_blocks,
        root_inverse,
        shared_rhs,
    ) = lax.optimization_barrier(
        (
            first_partial,
            own_blocks,
            own_pattern,
            pair_blocks,
            pair_inverse,
            root_blocks,
            root_inverse,
            shared_rhs,
        )
    )

    own_tiles = own_blocks.reshape(-1, tile_rows, cycles, tile_rows)
    kept_tiles = own_pattern.reshape(-1, 1, cycles, 1) > 0
    own_cols = jnp.where(kept_tiles, own_tiles, jnp.zeros((), own_tiles.dtype)).reshape(
        -1, tile_rows, col_width
    )
    own_in, own_out = by_column(own_cols, panels, 3 * panels)
    pair_in, pair_out = by_column(as_blocks(pair_blocks), panels, 2 * panels)
    pair_all = lax.all_gather(
        jnp.concatenate([as_blocks(pair_inverse)] + pair_in + [own_out[-1][:panels]]), "prow"
    )
    root_all = lax.all_gather(
        jnp.concatenate([as_blocks(root_inverse), as_blocks(root_blocks)]), "prow"
    )

    shared_turned = jnp.transpose(shared_rhs.reshape(-1, tile_rows, rhs_width), (2, 0, 1))
    beyond = jnp.where(lax.axis_index("pcol") == 0, shared_turned.astype(jnp.float32), 0.0)
    within = [None] * panels
    own_solved = []
    for step in range(panels - 1):
        if step == 0:
            partial_value = first_partial
        else:
            residual = own_rows[step].astype(jnp.float32) - row_total(within[step])
            partial_value = inverse_product(own_inv[step], residual)
        result = column_total(partial_value)
        own_solved.append(result)
        for target in range(step + 1, panels):
            block = own_in[step][target - step - 1]
            update = jnp.dot(block, result, preferred_element_type=jnp.float32)
            within[target] = update if within[target] is None else within[target] + update
        beyond = beyond - lax.dot_general(
            result, own_out[step], (((0,), (2,)), ((), ())), preferred_element_type=jnp.float32
        )

    residual = own_rows[-1].astype(jnp.float32) - row_total(within[-1])
    partial_turned = lax.dot_general(
        residual.astype(jnp.bfloat16),
        own_inv[-1],
        (((0,), (0,)), ((), ())),
        preferred_element_type=jnp.float32,
    ).astype(jnp.bfloat16)
    pieces = jnp.concatenate(
        [
            partial_turned.reshape(prows, wide, col_width),
            beyond[:, :panels].astype(jnp.bfloat16).reshape(prows, wide, panels * tile_rows),
        ],
        axis=-1,
    )
    received = lax.all_to_all(pieces, "prow", 0, 0).astype(jnp.float32)
    last_own = jnp.sum(received[:, :, :col_width], axis=0).astype(jnp.bfloat16)
    ancestors = received[:, :, col_width:].reshape(prows, wide, panels, tile_rows)
    ancestors = ancestors.transpose(1, 0, 2, 3)
    ancestors = ancestors - transposed_product(last_own, pair_all[:, -panels:])

    low, high = ancestors[:half], ancestors[half:]
    kept = jnp.where(second == 0, low, high)
    given = jnp.where(second == 0, high, low)
    sums = kept + layer_swap(given.astype(jnp.bfloat16), 1).astype(jnp.float32)
    pair_solved = slice_solve(sums, pair_all, panels)
    payload = jnp.concatenate([pair_solved.reshape(panels * half, col_width), last_own])
    everywhere = shared_with_all(payload, "prow")
    last_turned = everywhere[:, panels * half :].reshape(rhs_width, col_width)
    mine = everywhere[:, : panels * half]
    theirs = layer_swap(mine, 1)
    pair_turned = jnp.where(
        second == 0, jnp.stack([mine, theirs], axis=1), jnp.stack([theirs, mine], axis=1)
    )
    pair_turned = pair_turned.reshape(prows, 2, panels, half, col_width).transpose(2, 0, 1, 3, 4)

    left = beyond[:, panels:] - transposed_product(last_turned, own_out[-1][panels:])
    mine = mine.reshape(prows, panels, half, col_width).transpose(1, 0, 2, 3)
    mine = mine.reshape(panels, prows * half, col_width)
    taken = sum(transposed_product(mine[step], pair_out[step]) for step in range(panels))
    taken = taken.reshape(prows, 1, half, panels, tile_rows)
    is_mine = jnp.arange(2).reshape(1, 2, 1, 1, 1) == second
    left = left.reshape(prows, 2, half, panels, tile_rows) - jnp.where(is_mine, taken, 0.0)
    pieces = left.astype(jnp.bfloat16).reshape(prows, layers, narrow, panels, tile_rows)
    pieces = pieces.transpose(1, 0, 2, 3, 4).reshape(layers * prows, narrow, panels, tile_rows)
    received = lax.all_to_all(pieces, ("layer", "prow"), 0, 0)
    received = received.reshape(layers, prows, narrow, panels, tile_rows)
    sums = jnp.sum(received.astype(jnp.float32), axis=0).transpose(1, 0, 2, 3)
    root_solved = slice_solve(sums, root_all, panels)
    by_layer = shared_with_all(shared_with_all(root_solved, "prow"), "layer")
    root_turned = by_layer.transpose(2, 1, 0, 3, 4).reshape(panels, rhs_width, col_width)

    shape = (1, panels, cycles, 1, tile_rows, rhs_width)
    own_solved.append(last_turned.T)
    return (
        jnp.stack(own_solved).reshape(shape),
        pair_turned.reshape(panels, rhs_width, col_width).transpose(0, 2, 1).reshape(shape),
        root_turned.transpose(0, 2, 1).reshape(shape),
    )


def solution(mesh):
    return jax.shard_map(
        local,
        mesh=mesh,
        in_specs=(
            P("layer", None, "prow", None, None, "pcol", None),
            P("layer", None, "prow", None, "pcol"),
            P("layer", None, "prow", None, None, "pcol", None),
            P("layer", None, "prow", None, None, "pcol", None),
            P("layer", None, "prow", None, None, "pcol", None),
            P(None, "prow", None, None, "pcol", None),
            P(None, "prow", None, None, "pcol", None),
            P("layer", None, "prow", None, None),
            P("layer", None, "prow", None, None),
        ),
        out_specs=(
            P("layer", None, None, "pcol", None, None),
            P("layer", None, None, "pcol", None, None),
            P("layer", None, None, "pcol", None, None),
        ),
        check_vma=False,
    )
```

time: 375 us -> 360 us (0.960)
  blocking collectives: 153 us -> 130 us
  waiting for transfers between devices: 108 us -> 114 us
    all_to_all x1 -> x2, blocking collectives: 19.9 us -> 49.1 us  [column_total(): received = lax.all_to_all(pieces, 'prow', 0, 0)]
    all_to_all x7 -> x5, blocking collectives: 82.2 us -> 54.6 us  [shared_with_all(): return lax.all_to_all(copies, axis, 0, 0)]
    all_to_all x6 -> x8, waiting for transfers between devices: 58 us -> 85.4 us  [shared_with_all(): return lax.all_to_all(copies, axis, 0, 0)]
    all_to_all x3 -> x1, waiting for transfers between devices: 49.8 us -> 24.4 us  [local(): received = lax.all_to_all(pieces, 'prow', 0, 0).astype(jnp.float32)]
    all_to_all x2 -> x1, blocking collectives: 50.9 us -> 26.3 us  [local(): received = lax.all_to_all(pieces, ('layer', 'prow'), 0, 0)]
    all_to_all x3 -> x1, starting transfers between devices: 25 us -> 4.99 us  [local(): received = lax.all_to_all(pieces, 'prow', 0, 0).astype(jnp.float32)]
    all_to_all x6 -> x8, starting transfers between devices: 25.2 us -> 39.5 us  [shared_with_all(): return lax.all_to_all(copies, axis, 0, 0)]
    ppermute x0 -> x2, starting transfers between devices: none -> 6 us  [layer_swap(): lax.ppermute(value, 'layer', [(i, i ^ apart) for i in range(lax.axis_size...]
  transfers between devices with their start and end apart: 11 -> 13, of which waited for: 9 -> 11; matrix products, arithmetic and copies ran while one was open for 9% -> 8% of each run, Pallas kernels for 0% -> 0%
where the time goes in v4:
time: 360 us; the launch traced here: 358 us
  blocking collectives  130 us (36%)
  waiting for transfers between devices  114 us (32%)
  starting transfers between devices  50.6 us (14%)
  matrix products  24.8 us (7%)
  local copies, waits for them, and re-layouts  16.7 us (5%)
  between operations  14.7 us (4%)
  other arithmetic  7.31 us (2%)
    all_to_all x8, waiting for transfers between devices, shared_with_all(): return lax.all_to_all(copies, axis, 0, 0)  85.4 us
    all_to_all x5, blocking collectives, shared_with_all(): return lax.all_to_all(copies, axis, 0, 0)  54.6 us
    all_to_all x2, blocking collectives, column_total(): received = lax.all_to_all(pieces, 'prow', 0, 0)  49.1 us
    all_to_all x8, starting transfers between devices, shared_with_all(): return lax.all_to_all(copies, axis, 0, 0)  39.5 us
    all_to_all x1, blocking collectives, local(): received = lax.all_to_all(pieces, ('layer', 'prow'), 0, 0)  26.3 us
    all_to_all x1, waiting for transfers between devices, local(): received = lax.all_to_all(pieces, 'prow', 0, 0).astype(jnp.float32)  24.4 us
    dot_general x11, matrix products, transposed_product(): lax.dot_general(solved, blocks, (((solved.ndim - 1,), (blocks.ndim - 1,))...  13.4 us
    dot_general x6, matrix products, slice_solve(): lax.dot_general(residual, gathered[:, step], (((1, 2), (0, 1)), ((), ()))...  8.89 us
  transfers between devices with their start and end apart: 13, of which 11 were waited for; matrix products, arithmetic and copies ran while one was open for 8% of the time, Pallas kernels for 0%

profile of v4, /device:TPU:32, one launch (start us, length us, event | category | flops | bytes accessed | tf_op | source)
XLA Modules:
  0.0 357.7 jit_solution(14622383722186520540)
XLA Ops:
  7.2 1.1 fusion.74
  8.3 1.0 convolution_convert_fusion.2
  9.4 1.0 slice.210
  10.5 0.9 slice.212
  11.3 0.7 broadcast_compare_fusion
  12.1 2.5 broadcast_select_fusion
  15.3 1.1 reshape.187
  16.3 0.9 pad_maximum_fusion
  17.2 29.3 %all_to_all.85 = bf16[16,16,256]{2,1,0:T(8,128)(2,1)S(1)} all-to-all(bf16[16,16,256]{2,1,0:T(8,128)(2,1)S(1)} %bitcast.347), channel_id=1, replica_groups=mesh['layer'=4,'prow'=16,'pcol'=8] {'prow'}, dimensions={0} | all-to-all | bytes 262144 | tf_op jit(solution)/shard_map/all_to_all | solution.py:30
  46.5 0.7 broadcast_in_dim.70
  47.2 4.3 %all-to-all-start.1 = ((bf16[16,16,256]{2,1,0:T(8,128)(2,1)}), bf16[16,16,256]{2,1,0:T(8,128)(2,1)S(1)}, u32[]{:S(2)}, u32[]{:S(2)}) async-start(bf16[16,16,256]{2,1,0:T(8,128)(2,1)} %broadcast_in_dim.70), calls=%async_computation.1 | async-start | bytes 262144 | tf_op jit(solution)/shard_map/all_to_all | solution.py:9
  51.9 0.8 pad_maximum_fusion.2
  52.8 13.7 %all-to-all-done.1 = bf16[16,16,256]{2,1,0:T(8,128)(2,1)S(1)} async-done(((bf16[16,16,256]{2,1,0:T(8,128)(2,1)}), bf16[16,16,256]{2,1,0:T(8,128)(2,1)S(1)}, u32[]{:S(2)}, u32[]{:S(2)}) %all-to-all-start.1) | async-done | bytes 131104 | tf_op jit(solution)/shard_map/all_to_all | solution.py:9
  66.7 14.5 %all_to_all.86 = bf16[8,128,256]{2,1,0:T(8,128)(2,1)S(1)} all-to-all(bf16[8,128,256]{2,1,0:T(8,128)(2,1)S(1)} %broadcast_in_dim.73), channel_id=1, replica_groups=mesh['layer'=4,'prow'=16,'pcol'=8] {'pcol'}, dimensions={0} | all-to-all | bytes 1048576 | tf_op jit(solution)/shard_map/all_to_all | solution.py:9
  81.5 19.8 %all_to_all.87 = bf16[16,16,256]{2,1,0:T(8,128)(2,1)S(1)} all-to-all(bf16[16,16,256]{2,1,0:T(8,128)(2,1)S(1)} %bitcast.346), channel_id=1, replica_groups=mesh['layer'=4,'prow'=16,'pcol'=8] {'prow'}, dimensions={0} | all-to-all | bytes 262144 | tf_op jit(solution)/shard_map/all_to_all | solution.py:30
  101.3 0.7 broadcast_in_dim.74
  102.0 5.1 %all-to-all-start.4 = ((bf16[16,16,256]{2,1,0:T(8,128)(2,1)}), bf16[16,16,256]{2,1,0:T(8,128)(2,1)S(1)}, u32[]{:S(2)}, u32[]{:S(2)}) async-start(bf16[16,16,256]{2,1,0:T(8,128)(2,1)} %broadcast_in_dim.74), calls=%async_computation.4 | async-start | bytes 262144 | tf_op jit(solution)/shard_map/all_to_all | solution.py:9
  107.1 0.7 fusion.72
  108.7 13.3 %all-to-all-done.4 = bf16[16,16,256]{2,1,0:T(8,128)(2,1)S(1)} async-done(((bf16[16,16,256]{2,1,0:T(8,128)(2,1)}), bf16[16,16,256]{2,1,0:T(8,128)(2,1)S(1)}, u32[]{:S(2)}, u32[]{:S(2)}) %all-to-all-start.4) | async-done | bytes 131104 | tf_op jit(solution)/shard_map/all_to_all | solution.py:9
  122.2 0.8 broadcast_in_dim.75
  123.0 3.5 all-to-all-start.5
  127.5 9.2 %all-to-all-done.5 = bf16[8,128,256]{2,1,0:T(8,128)(2,1)S(1)} async-done(((bf16[8,128,256]{2,1,0:T(8,128)(2,1)}), bf16[8,128,256]{2,1,0:T(8,128)(2,1)S(1)}, u32[]{:S(2)}, u32[]{:S(2)}) %all-to-all-start.5) | async-done | bytes 524320 | tf_op jit(solution)/shard_map/all_to_all | solution.py:9
  137.1 0.8 pad_maximum_fusion.3
  137.8 5.0 %all-to-all-start.6 = ((bf16[16,16,640]{2,1,0:T(8,128)(2,1)}), bf16[16,16,640]{2,1,0:T(8,128)(2,1)S(1)}, u32[]{:S(2)}, u32[]{:S(2)}) async-start(bf16[16,16,640]{2,1,0:T(8,128)(2,1)} %pad_maximum_fusion.3), calls=%async_computation.6 | async-start | bytes 655360 | tf_op jit(solution)/shard_map/all_to_all | solution.py:180
  142.8 24.4 %all-to-all-done.6 = bf16[16,16,640]{2,1,0:T(8,128)(2,1)S(1)} async-done(((bf16[16,16,640]{2,1,0:T(8,128)(2,1)}), bf16[16,16,640]{2,1,0:T(8,128)(2,1)S(1)}, u32[]{:S(2)}, u32[]{:S(2)}) %all-to-all-start.6) | async-done | bytes 327712 | tf_op jit(solution)/shard_map/all_to_all | solution.py:180
  167.8 2.8 fusion.2
  170.7 3.5 collective-permute-start
  174.2 3.2 collective-permute-done
  177.6 11.6 %all_to_all.88 = bf16[8,8,16,128]{3,2,1,0:T(8,128)(2,1)S(1)} all-to-all(bf16[8,8,16,128]{3,2,1,0:T(8,128)(2,1)S(1)} %broadcast_in_dim.129), channel_id=1, replica_groups=mesh['layer'=4,'prow'=16,'pcol'=8] {'pcol'}, dimensions={0} | all-to-all | bytes 524288 | tf_op jit(solution)/shard_map/all_to_all | solution.py:9
  189.2 1.5 fusion.9
  190.7 1.6 fusion.47
  192.3 0.7 broadcast_in_dim.130
  193.1 3.4 all-to-all-start.8
  196.5 1.6 fusion.18
  198.1 5.8 %all-to-all-done.8 = bf16[8,8,16,128]{3,2,1,0:T(8,128)(2,1)S(1)} async-done(((bf16[8,8,16,128]{3,2,1,0:T(8,128)(2,1)}), bf16[8,8,16,128]{3,2,1,0:T(8,128)(2,1)S(1)}, u32[]{:S(2)}, u32[]{:S(2)}) %all-to-all-start.8) | async-done | bytes 262176 | tf_op jit(solution)/shard_map/all_to_all | solution.py:9
  204.0 1.5 fusion.10
  205.5 1.6 fusion.45
  207.2 9.9 %all_to_all.89 = bf16[8,8,16,128]{3,2,1,0:T(8,128)(2,1)S(1)} all-to-all(bf16[8,8,16,128]{3,2,1,0:T(8,128)(2,1)S(1)} %broadcast_in_dim.131), channel_id=1, replica_groups=mesh['layer'=4,'prow'=16,'pcol'=8] {'pcol'}, dimensions={0} | all-to-all | bytes 524288 | tf_op jit(solution)/shard_map/all_to_all | solution.py:9
  217.2 1.5 fusion.12
  218.7 0.8 broadcast_in_dim.132
  219.4 10.1 %all-to-all-start.10 = ((bf16[16,40,256]{2,1,0:T(8,128)(2,1)}), bf16[16,40,256]{2,1,0:T(8,128)(2,1)S(1)}, u32[]{:S(2)}, u32[]{:S(2)}) async-start(bf16[16,40,256]{2,1,0:T(8,128)(2,1)} %broadcast_in_dim.132), calls=%async_computation.10 | async-start | bytes 655360 | tf_op jit(solution)/shard_map/all_to_all | solution.py:9
  230.7 23.2 %all-to-all-done.10 = bf16[16,40,256]{2,1,0:T(8,128)(2,1)S(1)} async-done(((bf16[16,40,256]{2,1,0:T(8,128)(2,1)}), bf16[16,40,256]{2,1,0:T(8,128)(2,1)S(1)}, u32[]{:S(2)}, u32[]{:S(2)}) %all-to-all-start.10) | async-done | bytes 327712 | tf_op jit(solution)/shard_map/all_to_all | solution.py:9
  255.4 26.3 %all_to_all.90 = bf16[64,4,3,128]{3,1,2,0:T(4,128)(2,1)S(1)} all-to-all(bf16[64,4,3,128]{3,1,2,0:T(4,128)(2,1)S(1)} %copy.160), channel_id=1, replica_groups=mesh['layer'=4,'prow'=16,'pcol'=8] {'layer','prow'}, dimensions={0} | all-to-all | bytes 393216 | tf_op jit(solution)/shard_map/all_to_all | solution.py:210
  281.9 10.1 %all_to_all.91 = bf16[8,4,16,128]{3,2,1,0:T(8,128)(2,1)S(1)} all-to-all(bf16[8,4,16,128]{3,2,1,0:T(8,128)(2,1)S(1)} %broadcast_in_dim.140), channel_id=1, replica_groups=mesh['layer'=4,'prow'=16,'pcol'=8] {'pcol'}, dimensions={0} | all-to-all | bytes 262144 | tf_op jit(solution)/shard_map/all_to_all | solution.py:9
  292.0 1.5 fusion.13
  293.5 1.6 fusion.7
  295.1 0.7 broadcast_in_dim.141
  295.8 3.4 all-to-all-start.13
  299.1 1.6 convolution_subtract_fusion.4
  300.7 4.5 %all-to-all-done.13 = bf16[8,4,16,128]{3,2,1,0:T(8,128)(2,1)S(1)} async-done(((bf16[8,4,16,128]{3,2,1,0:T(8,128)(2,1)}), bf16[8,4,16,128]{3,2,1,0:T(8,128)(2,1)S(1)}, u32[]{:S(2)}, u32[]{:S(2)}) %all-to-all-start.13) | async-done | bytes 131104 | tf_op jit(solution)/shard_map/all_to_all | solution.py:9
  305.2 1.5 fusion.14
  306.7 1.6 fusion.8
  308.4 8.5 %all_to_all.92 = bf16[8,4,16,128]{3,2,1,0:T(8,128)(2,1)S(1)} all-to-all(bf16[8,4,16,128]{3,2,1,0:T(8,128)(2,1)S(1)} %broadcast_in_dim.142), channel_id=1, replica_groups=mesh['layer'=4,'prow'=16,'pcol'=8] {'pcol'}, dimensions={0} | all-to-all | bytes 262144 | tf_op jit(solution)/shard_map/all_to_all | solution.py:9
  316.9 1.5 fusion.16
  318.4 0.7 broadcast_in_dim.143
  319.1 5.8 %all-to-all-start.15 = ((bf16[16,3,4,256]{3,2,1,0:T(4,128)(2,1)}), bf16[16,3,4,256]{3,2,1,0:T(4,128)(2,1)S(1)}, u32[]{:S(2)}, u32[]{:S(2)}) async-start(bf16[16,3,4,256]{3,2,1,0:T(4,128)(2,1)} %broadcast_in_dim.143), calls=%async_computation.15 | async-start | bytes 196608 | tf_op jit(solution)/shard_map/all_to_all | solution.py:9
  324.9 2.5 collective-permute-start.1
  327.4 10.2 %all-to-all-done.15 = bf16[16,3,4,256]{3,2,1,0:T(4,128)(2,1)S(1)} async-done(((bf16[16,3,4,256]{3,2,1,0:T(4,128)(2,1)}), bf16[16,3,4,256]{3,2,1,0:T(4,128)(2,1)S(1)}, u32[]{:S(2)}, u32[]{:S(2)}) %all-to-all-start.15) | async-done | bytes 98336 | tf_op jit(solution)/shard_map/all_to_all | solution.py:9
  337.6 0.9 broadcast_in_dim.144
  338.5 3.9 %all-to-all-start.16 = ((bf16[4,16,3,4,256]{4,3,1,2,0:T(4,128)(2,1)}), bf16[4,16,3,4,256]{4,3,1,2,0:T(4,128)(2,1)S(1)}, u32[]{:S(2)}, u32[]{:S(2)}) async-start(bf16[4,16,3,4,256]{4,3,1,2,0:T(4,128)(2,1)} %broadcast_in_dim.144), calls=%async_computation.16 | async-start | bytes 786432 | tf_op jit(solution)/shard_map/all_to_all | solution.py:9
  342.5 0.8 pad_maximum_fusion.1
  343.3 0.9 copy.186
  344.3 5.5 %all-to-all-done.16 = bf16[4,16,3,4,256]{4,3,1,2,0:T(4,128)(2,1)S(1)} async-done(((bf16[4,16,3,4,256]{4,3,1,2,0:T(4,128)(2,1)}), bf16[4,16,3,4,256]{4,3,1,2,0:T(4,128)(2,1)S(1)}, u32[]{:S(2)}, u32[]{:S(2)}) %all-to-all-start.16) | async-done | bytes 393248 | tf_op jit(solution)/shard_map/all_to_all | solution.py:9
  350.0 0.9 copy.187
  (96 shorter events, 8.2 us)
Async XLA Ops:
  7.2 44.6 %copy-start.3 = (bf16[3,1,128,2,1,128]{5,3,4,2,1,0:T(2,128)(2,1)S(1)}, bf16[3,1,128,2,1,128]{5,3,4,2,1,0:T(2,128)(2,1)}, u32[]{:S(2)}) copy-start(bf16[3,1,128,2,1,128]{5,3,4,2,1,0:T(2,128)(2,1)} %param.14) | copy-start | bytes 589828
  7.2 44.4 %copy-start.2 = (bf16[3,1,128,2,1,128]{5,3,4,2,1,0:T(2,128)(2,1)S(1)}, bf16[3,1,128,2,1,128]{5,3,4,2,1,0:T(2,128)(2,1)}, u32[]{:S(2)}) copy-start(bf16[3,1,128,2,1,128]{5,3,4,2,1,0:T(2,128)(2,1)} %param.15) | copy-start | bytes 589828
  7.2 160.6 %all-gather.5.cloned.1.call-start = ((), (), s32[]{:S(2)}) async-start(), calls=%async_computation.17 | async-start | bytes 10027008 | tf_op jit(solution)/shard_map/all_gather | solution.py:139
  9.4 71.9 %copy-start.4 = (bf16[1,3,1,128,256]{4,3,2,1,0:T(8,128)(2,1)S(1)}, bf16[1,3,1,128,256]{4,3,2,1,0:T(8,128)(2,1)}, u32[]{:S(2)}) copy-start(bf16[1,3,1,128,256]{4,3,2,1,0:T(8,128)(2,1)} %param.16) | copy-start | bytes 589828
  15.0 93.0 %copy-start.1 = (bf16[1,6,1,128,256]{4,3,2,1,0:T(8,128)(2,1)S(1)}, bf16[1,6,1,128,256]{4,3,2,1,0:T(8,128)(2,1)}, u32[]{:S(2)}) copy-start(bf16[1,6,1,128,256]{4,3,2,1,0:T(8,128)(2,1)} %param.17) | copy-start | bytes 1179652
  47.2 19.3 %all-to-all-start.1 = ((bf16[16,16,256]{2,1,0:T(8,128)(2,1)}), bf16[16,16,256]{2,1,0:T(8,128)(2,1)S(1)}, u32[]{:S(2)}, u32[]{:S(2)}) async-start(bf16[16,16,256]{2,1,0:T(8,128)(2,1)} %broadcast_in_dim.70), calls=%async_computation.1 | async-start | bytes 262144 | tf_op jit(solution)/shard_map/all_to_all | solution.py:9
  51.5 240.4 %all-gather.7.cloned.1.call-start = ((), (), s32[]{:S(2)}) async-start(), calls=%async_computation.18 | async-start | bytes 6684672 | tf_op jit(solution)/shard_map/all_gather | solution.py:142
  102.0 20.0 %all-to-all-start.4 = ((bf16[16,16,256]{2,1,0:T(8,128)(2,1)}), bf16[16,16,256]{2,1,0:T(8,128)(2,1)S(1)}, u32[]{:S(2)}, u32[]{:S(2)}) async-start(bf16[16,16,256]{2,1,0:T(8,128)(2,1)} %broadcast_in_dim.74), calls=%async_computation.4 | async-start | bytes 262144 | tf_op jit(solution)/shard_map/all_to_all | solution.py:9
  123.0 13.8 %all-to-all-start.5 = ((bf16[8,128,256]{2,1,0:T(8,128)(2,1)}), bf16[8,128,256]{2,1,0:T(8,128)(2,1)S(1)}, u32[]{:S(2)}, u32[]{:S(2)}) async-start(bf16[8,128,256]{2,1,0:T(8,128)(2,1)} %broadcast_in_dim.75), calls=%async_computation.5 | async-start | bytes 1048576 | tf_op jit(solution)/shard_map/all_to_all | solution.py:9
  137.8 29.4 %all-to-all-start.6 = ((bf16[16,16,640]{2,1,0:T(8,128)(2,1)}), bf16[16,16,640]{2,1,0:T(8,128)(2,1)S(1)}, u32[]{:S(2)}, u32[]{:S(2)}) async-start(bf16[16,16,640]{2,1,0:T(8,128)(2,1)} %pad_maximum_fusion.3), calls=%async_computation.6 | async-start | bytes 655360 | tf_op jit(solution)/shard_map/all_to_all | solution.py:180
  170.7 59.0 %copy-start = (bf16[1,12,1,128,2,1,128]{6,4,5,3,2,1,0:T(2,128)(2,1)S(1)}, bf16[1,12,1,128,2,1,128]{6,4,5,3,2,1,0:T(2,128)(2,1)}, u32[]{:S(2)}) copy-start(bf16[1,12,1,128,2,1,128]{6,4,5,3,2,1,0:T(2,128)(2,1)} %param.12) | copy-start | bytes 2359300
  170.7 6.8 %collective-permute-start = (bf16[8,16,3,128]{3,0,2,1:T(8,128)(2,1)S(1)}, bf16[8,16,3,128]{3,0,2,1:T(8,128)(2,1)S(1)}, u32[]{:S(2)}, u32[]{:S(2)}) collective-permute-start(bf16[8,16,3,128]{3,0,2,1:T(8,128)(2,1)S(1)} %select_convert_fusion), channel_id=1, source_target_pairs={{0,128},{128,0},{256,384},{384,256},{1,129},{129,1},{257,385},{385... | collective-permute-start | bytes 294920 | tf_op jit(solution)/shard_map/ppermute | solution.py:45
  193.1 10.9 %all-to-all-start.8 = ((bf16[8,8,16,128]{3,2,1,0:T(8,128)(2,1)}), bf16[8,8,16,128]{3,2,1,0:T(8,128)(2,1)S(1)}, u32[]{:S(2)}, u32[]{:S(2)}) async-start(bf16[8,8,16,128]{3,2,1,0:T(8,128)(2,1)} %broadcast_in_dim.130), calls=%async_computation.8 | async-start | bytes 524288 | tf_op jit(solution)/shard_map/all_to_all | solution.py:9
  219.4 34.5 %all-to-all-start.10 = ((bf16[16,40,256]{2,1,0:T(8,128)(2,1)}), bf16[16,40,256]{2,1,0:T(8,128)(2,1)S(1)}, u32[]{:S(2)}, u32[]{:S(2)}) async-start(bf16[16,40,256]{2,1,0:T(8,128)(2,1)} %broadcast_in_dim.132), calls=%async_computation.10 | async-start | bytes 655360 | tf_op jit(solution)/shard_map/all_to_all | solution.py:9
  295.8 9.4 %all-to-all-start.13 = ((bf16[8,4,16,128]{3,2,1,0:T(8,128)(2,1)}), bf16[8,4,16,128]{3,2,1,0:T(8,128)(2,1)S(1)}, u32[]{:S(2)}, u32[]{:S(2)}) async-start(bf16[8,4,16,128]{3,2,1,0:T(8,128)(2,1)} %broadcast_in_dim.141), calls=%async_computation.13 | async-start | bytes 262144 | tf_op jit(solution)/shard_map/all_to_all | solution.py:9
  319.1 18.5 %all-to-all-start.15 = ((bf16[16,3,4,256]{3,2,1,0:T(4,128)(2,1)}), bf16[16,3,4,256]{3,2,1,0:T(4,128)(2,1)S(1)}, u32[]{:S(2)}, u32[]{:S(2)}) async-start(bf16[16,3,4,256]{3,2,1,0:T(4,128)(2,1)} %broadcast_in_dim.143), calls=%async_computation.15 | async-start | bytes 196608 | tf_op jit(solution)/shard_map/all_to_all | solution.py:9
  324.9 18.4 %collective-permute-start.1 = (bf16[16,24,256]{2,1,0:T(8,128)(2,1)S(1)}, bf16[16,24,256]{2,1,0:T(8,128)(2,1)S(1)}, u32[]{:S(2)}, u32[]{:S(2)}) collective-permute-start(bf16[16,24,256]{2,1,0:T(8,128)(2,1)S(1)} %get-tuple-element.46), channel_id=1, source_target_pairs={{0,128},{128,0},{256,384},{384,256},{1,129},{129,1},{257,385},{385... | collective-permute-start | bytes 589832 | tf_op jit(solution)/shard_map/ppermute | solution.py:45
  338.5 11.3 %all-to-all-start.16 = ((bf16[4,16,3,4,256]{4,3,1,2,0:T(4,128)(2,1)}), bf16[4,16,3,4,256]{4,3,1,2,0:T(4,128)(2,1)S(1)}, u32[]{:S(2)}, u32[]{:S(2)}) async-start(bf16[4,16,3,4,256]{4,3,1,2,0:T(4,128)(2,1)} %broadcast_in_dim.144), calls=%async_computation.16 | async-start | bytes 786432 | tf_op jit(solution)/shard_map/all_to_all | solution.py:9
Sparse Core Ops, SparseCore 0:
  17.4 150.4 all-gather.4
  170.5 103.4 all-gather.6

commit v5 on v4

--- a/solution.py
+++ b/solution.py
@@ -61,12 +61,12 @@
     return inside, outside
 
 
-def slice_solve(sums, gathered, panels):
-    sums = [sums[:, :, t] for t in range(panels)]
+def slice_solve(first, sums, gathered, panels):
+    sums = [first] + sums
     solved = []
     offset = panels
     for step in range(panels):
-        residual = row_total(sums[step]).astype(jnp.bfloat16)
+        residual = (first if step == 0 else row_total(sums[step])).astype(jnp.bfloat16)
         result = lax.dot_general(
             residual,
             gathered[:, step],
@@ -104,13 +104,14 @@
     half = wide // 2
     narrow = wide // layers
 
-    own_inv = own_inverse.reshape(-1, tile_rows, col_width)
     own_rows = own_rhs.reshape(-1, tile_rows, rhs_width)
-    first_partial = inverse_product(own_inv[0], own_rows[0])
+    first_inv = own_inverse[0, 0, 0].reshape(tile_rows, col_width)
+    first_partial = inverse_product(first_inv, own_rows[0])
     (
         first_partial,
         own_blocks,
         own_pattern,
+        own_inverse,
         pair_blocks,
         pair_inverse,
         root_blocks,
@@ -121,6 +122,7 @@
             first_partial,
             own_blocks,
             own_pattern,
+            own_inverse,
             pair_blocks,
             pair_inverse,
             root_blocks,
@@ -129,15 +131,22 @@
         )
     )
 
+    own_inv = own_inverse.reshape(-1, tile_rows, col_width)
     own_tiles = own_blocks.reshape(-1, tile_rows, cycles, tile_rows)
     kept_tiles = own_pattern.reshape(-1, 1, cycles, 1) > 0
     own_cols = jnp.where(kept_tiles, own_tiles, jnp.zeros((), own_tiles.dtype)).reshape(
         -1, tile_rows, col_width
     )
     own_in, own_out = by_column(own_cols, panels, 3 * panels)
+    ahead = slice(own_tiles.shape[0] - 2 * panels, own_tiles.shape[0] - panels)
+    early_tiles = own_blocks[0, ahead, 0].reshape(-1, tile_rows, cycles, tile_rows)
+    early_kept = own_pattern[0, ahead].reshape(-1, 1, cycles, 1) > 0
+    early_cols = jnp.where(early_kept, early_tiles, jnp.zeros((), own_tiles.dtype)).reshape(
+        -1, tile_rows, col_width
+    )
     pair_in, pair_out = by_column(as_blocks(pair_blocks), panels, 2 * panels)
     pair_all = lax.all_gather(
-        jnp.concatenate([as_blocks(pair_inverse)] + pair_in + [own_out[-1][:panels]]), "prow"
+        jnp.concatenate([as_blocks(pair_inverse)] + pair_in + [early_cols]), "prow"
     )
     root_all = lax.all_gather(
         jnp.concatenate([as_blocks(root_inverse), as_blocks(root_blocks)]), "prow"
@@ -179,15 +188,34 @@
     )
     received = lax.all_to_all(pieces, "prow", 0, 0).astype(jnp.float32)
     last_own = jnp.sum(received[:, :, :col_width], axis=0).astype(jnp.bfloat16)
-    ancestors = received[:, :, col_width:].reshape(prows, wide, panels, tile_rows)
-    ancestors = ancestors.transpose(1, 0, 2, 3)
-    ancestors = ancestors - transposed_product(last_own, pair_all[:, -panels:])
-
-    low, high = ancestors[:half], ancestors[half:]
+    parts = received[:, :, col_width:].reshape(prows, wide, panels, tile_rows)
+    ancestors = [
+        parts[:, :, t].transpose(1, 0, 2)
+        - transposed_product(last_own, pair_all[:, t - panels])
+        for t in range(panels)
+    ]
+
+    pcols = lax.axis_size("pcol")
+    halves = ancestors[0].astype(jnp.bfloat16).reshape(2, 1, half, prows, tile_rows)
+    pieces = jnp.broadcast_to(halves, (2, pcols, half, prows, tile_rows))
+    groups = [
+        [layer * pcols + c for layer in (low, low + 1) for c in range(pcols)]
+        for low in range(0, layers, 2)
+    ]
+    partials = lax.all_to_all(
+        pieces.reshape((2 * pcols,) + halves.shape[2:]),
+        ("layer", "pcol"),
+        0,
+        0,
+        axis_index_groups=groups,
+    )
+    first = jnp.sum(partials.astype(jnp.float32), axis=0)
+    later = jnp.stack(ancestors[1:])
+    low, high = later[:, :half], later[:, half:]
     kept = jnp.where(second == 0, low, high)
     given = jnp.where(second == 0, high, low)
-    sums = kept + layer_swap(given.astype(jnp.bfloat16), 1).astype(jnp.float32)
-    pair_solved = slice_solve(sums, pair_all, panels)
+    later = kept + layer_swap(given.astype(jnp.bfloat16), 1).astype(jnp.float32)
+    pair_solved = slice_solve(first, list(later), pair_all, panels)
     payload = jnp.concatenate([pair_solved.reshape(panels * half, col_width), last_own])
     everywhere = shared_with_all(payload, "prow")
     last_turned = everywhere[:, panels * half :].reshape(rhs_width, col_width)
@@ -210,7 +238,8 @@
     received = lax.all_to_all(pieces, ("layer", "prow"), 0, 0)
     received = received.reshape(layers, prows, narrow, panels, tile_rows)
     sums = jnp.sum(received.astype(jnp.float32), axis=0).transpose(1, 0, 2, 3)
-    root_solved = slice_solve(sums, root_all, panels)
+    sums = [sums[:, :, t] for t in range(panels)]
+    root_solved = slice_solve(row_total(sums[0]), sums[1:], root_all, panels)
     by_layer = shared_with_all(shared_with_all(root_solved, "prow"), "layer")
     root_turned = by_layer.transpose(2, 1, 0, 3, 4).reshape(panels, rhs_width, col_width)
 

time: 360 us -> 359 us (level)
  blocking collectives: 130 us -> 73.7 us
  starting transfers between devices: 50.6 us -> 70.9 us
  waiting for transfers between devices: 114 us -> 131 us
  local copies, waits for them, and re-layouts: 16.7 us -> 27.3 us
  matrix products: 24.8 us -> 30.2 us
    all_to_all x2 -> x1, blocking collectives: 49.1 us -> 19.8 us  [column_total(): received = lax.all_to_all(pieces, 'prow', 0, 0)]
    all_to_all x5 -> x3, blocking collectives: 54.6 us -> 27.4 us  [shared_with_all(): return lax.all_to_all(copies, axis, 0, 0)]
    all_to_all x0 -> x2, starting transfers between devices: none -> 18.8 us  [the longest x1 15.2 us: column_total(): received = lax.all_to_all(pieces, 'prow', 0, 0)]
    all_to_all x0 -> x2, waiting for transfers between devices: none -> 11.2 us  [the longest x1 11.2 us: column_total(): received = lax.all_to_all(pieces, 'prow', 0, 0)]
    all_to_all x8 -> x9, waiting for transfers between devices: 85.4 us -> 91.5 us  [shared_with_all(): return lax.all_to_all(copies, axis, 0, 0)]
    dot_general x11 -> x13, matrix products: 13.4 us -> 16.3 us  [transposed_product(): lax.dot_general(solved, blocks, (((solved.ndim - 1,), (blocks.ndim - 1,))...]
    all_to_all x8 -> x9, starting transfers between devices: 39.5 us -> 40.5 us  [shared_with_all(): return lax.all_to_all(copies, axis, 0, 0)]
  transfers between devices with their start and end apart: 13 -> 16, of which waited for: 11 -> 12; matrix products, arithmetic and copies ran while one was open for 8% -> 13% of each run, Pallas kernels for 0% -> 0%
where the time goes in v5:
time: 359 us; the launch traced here: 356 us
  waiting for transfers between devices  131 us (36%)
  blocking collectives  73.7 us (21%)
  starting transfers between devices  70.9 us (20%)
  matrix products  30.2 us (8%)
  local copies, waits for them, and re-layouts  27.3 us (8%)
  between operations  14.7 us (4%)
  other arithmetic  7.98 us (2%)
    all_to_all x9, waiting for transfers between devices, shared_with_all(): return lax.all_to_all(copies, axis, 0, 0)  91.5 us
    all_to_all x9, starting transfers between devices, shared_with_all(): return lax.all_to_all(copies, axis, 0, 0)  40.5 us
    all_to_all x3, blocking collectives, shared_with_all(): return lax.all_to_all(copies, axis, 0, 0)  27.4 us
    all_to_all x1, blocking collectives, local(): received = lax.all_to_all(pieces, ('layer', 'prow'), 0, 0)  26.4 us
    all_to_all x1, waiting for transfers between devices, local(): received = lax.all_to_all(pieces, 'prow', 0, 0).astype(jnp.float32)  24.5 us
    all_to_all x1, blocking collectives, column_total(): received = lax.all_to_all(pieces, 'prow', 0, 0)  19.8 us
    dot_general x13, matrix products, transposed_product(): lax.dot_general(solved, blocks, (((solved.ndim - 1,), (blocks.ndim - 1,))...  16.3 us
    all_to_all x1, starting transfers between devices, column_total(): received = lax.all_to_all(pieces, 'prow', 0, 0)  15.2 us
  transfers between devices with their start and end apart: 16, of which 12 were waited for; matrix products, arithmetic and copies ran while one was open for 13% of the time, Pallas kernels for 0%

profile of v5, /device:TPU:32, one launch (start us, length us, event | category | flops | bytes accessed | tf_op | source)
XLA Modules:
  0.0 356.2 jit_solution(5203392150888609946)
XLA Ops:
  7.2 1.0 slice.197
  8.2 1.7 convolution_convert_fusion.2
  10.0 1.0 slice.214
  11.8 1.1 slice.219
  14.0 1.1 reshape.195
  15.1 0.9 pad_maximum_fusion
  16.1 15.2 %all-to-all-start = ((bf16[16,16,256]{2,1,0:T(8,128)(2,1)}), bf16[16,16,256]{2,1,0:T(8,128)(2,1)S(1)}, u32[]{:S(2)}, u32[]{:S(2)}) async-start(bf16[16,16,256]{2,1,0:T(8,128)(2,1)} %bitcast.1), calls=%async_computation | async-start | bytes 262144 | tf_op jit(solution)/shard_map/all_to_all | solution.py:30
  31.3 1.1 reshape.204
  32.4 1.1 reshape.205
  34.4 11.2 %all-to-all-done = bf16[16,16,256]{2,1,0:T(8,128)(2,1)S(1)} async-done(((bf16[16,16,256]{2,1,0:T(8,128)(2,1)}), bf16[16,16,256]{2,1,0:T(8,128)(2,1)S(1)}, u32[]{:S(2)}, u32[]{:S(2)}) %all-to-all-start) | async-done | bytes 131104 | tf_op jit(solution)/shard_map/all_to_all | solution.py:30
  46.3 4.3 %all-to-all-start.1 = ((bf16[16,16,256]{2,1,0:T(8,128)(2,1)}), bf16[16,16,256]{2,1,0:T(8,128)(2,1)S(1)}, u32[]{:S(2)}, u32[]{:S(2)}) async-start(bf16[16,16,256]{2,1,0:T(8,128)(2,1)} %broadcast_in_dim.139), calls=%async_computation.1 | async-start | bytes 262144 | tf_op jit(solution)/shard_map/all_to_all | solution.py:9
  50.6 1.2 broadcast_select_fusion
  51.9 13.6 %all-to-all-done.1 = bf16[16,16,256]{2,1,0:T(8,128)(2,1)S(1)} async-done(((bf16[16,16,256]{2,1,0:T(8,128)(2,1)}), bf16[16,16,256]{2,1,0:T(8,128)(2,1)S(1)}, u32[]{:S(2)}, u32[]{:S(2)}) %all-to-all-start.1) | async-done | bytes 131104 | tf_op jit(solution)/shard_map/all_to_all | solution.py:9
  66.6 4.3 %all-to-all-start.2 = ((bf16[8,128,256]{2,1,0:T(8,128)(2,1)}), bf16[8,128,256]{2,1,0:T(8,128)(2,1)S(1)}, u32[]{:S(2)}, u32[]{:S(2)}) async-start(bf16[8,128,256]{2,1,0:T(8,128)(2,1)} %broadcast_in_dim.142), calls=%async_computation.2 | async-start | bytes 1048576 | tf_op jit(solution)/shard_map/all_to_all | solution.py:9
  71.6 9.6 %all-to-all-done.2 = bf16[8,128,256]{2,1,0:T(8,128)(2,1)S(1)} async-done(((bf16[8,128,256]{2,1,0:T(8,128)(2,1)}), bf16[8,128,256]{2,1,0:T(8,128)(2,1)S(1)}, u32[]{:S(2)}, u32[]{:S(2)}) %all-to-all-start.2) | async-done | bytes 524320 | tf_op jit(solution)/shard_map/all_to_all | solution.py:9
  81.3 1.0 convolution_convert_fusion.1
  82.3 19.8 %all_to_all.85 = bf16[16,16,256]{2,1,0:T(8,128)(2,1)S(1)} all-to-all(bf16[16,16,256]{2,1,0:T(8,128)(2,1)S(1)} %bitcast.392), channel_id=1, replica_groups=mesh['layer'=4,'prow'=16,'pcol'=8] {'prow'}, dimensions={0} | all-to-all | bytes 262144 | tf_op jit(solution)/shard_map/all_to_all | solution.py:30
  102.9 5.1 %all-to-all-start.4 = ((bf16[16,16,256]{2,1,0:T(8,128)(2,1)}), bf16[16,16,256]{2,1,0:T(8,128)(2,1)S(1)}, u32[]{:S(2)}, u32[]{:S(2)}) async-start(bf16[16,16,256]{2,1,0:T(8,128)(2,1)} %broadcast_in_dim.143), calls=%async_computation.4 | async-start | bytes 262144 | tf_op jit(solution)/shard_map/all_to_all | solution.py:9
  108.9 1.2 copy.191
  110.6 12.4 %all-to-all-done.4 = bf16[16,16,256]{2,1,0:T(8,128)(2,1)S(1)} async-done(((bf16[16,16,256]{2,1,0:T(8,128)(2,1)}), bf16[16,16,256]{2,1,0:T(8,128)(2,1)S(1)}, u32[]{:S(2)}, u32[]{:S(2)}) %all-to-all-start.4) | async-done | bytes 131104 | tf_op jit(solution)/shard_map/all_to_all | solution.py:9
  124.0 3.5 all-to-all-start.5
  128.5 9.2 %all-to-all-done.5 = bf16[8,128,256]{2,1,0:T(8,128)(2,1)S(1)} async-done(((bf16[8,128,256]{2,1,0:T(8,128)(2,1)}), bf16[8,128,256]{2,1,0:T(8,128)(2,1)S(1)}, u32[]{:S(2)}, u32[]{:S(2)}) %all-to-all-start.5) | async-done | bytes 524320 | tf_op jit(solution)/shard_map/all_to_all | solution.py:9
  137.9 1.1 convolution_convert_fusion
  139.7 5.0 %all-to-all-start.6 = ((bf16[16,16,640]{2,1,0:T(8,128)(2,1)}), bf16[16,16,640]{2,1,0:T(8,128)(2,1)S(1)}, u32[]{:S(2)}, u32[]{:S(2)}) async-start(bf16[16,16,640]{2,1,0:T(8,128)(2,1)} %pad_maximum_fusion.3), calls=%async_computation.6 | async-start | bytes 655360 | tf_op jit(solution)/shard_map/all_to_all | solution.py:189
  144.7 24.5 %all-to-all-done.6 = bf16[16,16,640]{2,1,0:T(8,128)(2,1)S(1)} async-done(((bf16[16,16,640]{2,1,0:T(8,128)(2,1)}), bf16[16,16,640]{2,1,0:T(8,128)(2,1)S(1)}, u32[]{:S(2)}, u32[]{:S(2)}) %all-to-all-start.6) | async-done | bytes 327712 | tf_op jit(solution)/shard_map/all_to_all | solution.py:189
  169.9 1.1 reshape.194
  171.5 1.6 fusion.5
  173.1 0.9 broadcast_in_dim.151
  174.0 3.6 %all-to-all-start.7 = ((bf16[16,8,16,128]{3,2,1,0:T(8,128)(2,1)}), bf16[16,8,16,128]{3,2,1,0:T(8,128)(2,1)S(1)}, u32[]{:S(2)}, u32[]{:S(2)}) async-start(bf16[16,8,16,128]{3,2,1,0:T(8,128)(2,1)} %bitcast.29), calls=%async_computation.7 | async-start | bytes 1048576 | tf_op jit(solution)/shard_map/all_to_all | solution.py:205
  177.6 1.6 fusion.2
  179.2 1.6 fusion.1
  180.8 3.8 %collective-permute-start = (bf16[2,8,16,128]{3,1,2,0:T(8,128)(2,1)S(1)}, bf16[2,8,16,128]{3,1,2,0:T(8,128)(2,1)S(1)}, u32[]{:S(2)}, u32[]{:S(2)}) collective-permute-start(bf16[2,8,16,128]{3,1,2,0:T(8,128)(2,1)S(1)} %select_convert_fusion), channel_id=1, source_target_pairs={{0,128},{128,0},{256,384},{384,256},{1,129},{129,1},{257,385},{385... | collective-permute-start | bytes 196616 | tf_op jit(solution)/shard_map/ppermute | solution.py:45
  184.6 4.2 %collective-permute-done = bf16[2,8,16,128]{3,1,2,0:T(8,128)(2,1)S(1)} collective-permute-done((bf16[2,8,16,128]{3,1,2,0:T(8,128)(2,1)S(1)}, bf16[2,8,16,128]{3,1,2,0:T(8,128)(2,1)S(1)}, u32[]{:S(2)}, u32[]{:S(2)}) %collective-permute-start) | collective-permute-done | bytes 65568 | tf_op jit(solution)/shard_map/ppermute | solution.py:45
  190.2 1.6 fusion.8
  191.8 1.6 fusion.47
  194.2 3.4 all-to-all-start.8
  197.6 1.6 fusion.17
  199.2 5.8 %all-to-all-done.8 = bf16[8,8,16,128]{3,2,1,0:T(8,128)(2,1)S(1)} async-done(((bf16[8,8,16,128]{3,2,1,0:T(8,128)(2,1)}), bf16[8,8,16,128]{3,2,1,0:T(8,128)(2,1)S(1)}, u32[]{:S(2)}, u32[]{:S(2)}) %all-to-all-start.8) | async-done | bytes 262176 | tf_op jit(solution)/shard_map/all_to_all | solution.py:9
  205.7 1.5 fusion.9
  207.2 1.6 fusion.45
  208.9 9.9 %all_to_all.86 = bf16[8,8,16,128]{3,2,1,0:T(8,128)(2,1)S(1)} all-to-all(bf16[8,8,16,128]{3,2,1,0:T(8,128)(2,1)S(1)} %broadcast_in_dim.153), channel_id=1, replica_groups=mesh['layer'=4,'prow'=16,'pcol'=8] {'pcol'}, dimensions={0} | all-to-all | bytes 524288 | tf_op jit(solution)/shard_map/all_to_all | solution.py:9
  218.9 1.5 fusion.11
  221.1 7.2 %all-to-all-start.10 = ((bf16[16,40,256]{2,1,0:T(8,128)(2,1)}), bf16[16,40,256]{2,1,0:T(8,128)(2,1)S(1)}, u32[]{:S(2)}, u32[]{:S(2)}) async-start(bf16[16,40,256]{2,1,0:T(8,128)(2,1)} %broadcast_in_dim.154), calls=%async_computation.10 | async-start | bytes 655360 | tf_op jit(solution)/shard_map/all_to_all | solution.py:9
  229.2 1.7 slice.237
  231.9 20.9 %all-to-all-done.10 = bf16[16,40,256]{2,1,0:T(8,128)(2,1)S(1)} async-done(((bf16[16,40,256]{2,1,0:T(8,128)(2,1)}), bf16[16,40,256]{2,1,0:T(8,128)(2,1)S(1)}, u32[]{:S(2)}, u32[]{:S(2)}) %all-to-all-start.10) | async-done | bytes 327712 | tf_op jit(solution)/shard_map/all_to_all | solution.py:9
  253.6 1.2 convolution_subtract_fusion.2
  255.1 26.4 %all_to_all.87 = bf16[64,4,3,128]{3,1,2,0:T(4,128)(2,1)S(1)} all-to-all(bf16[64,4,3,128]{3,1,2,0:T(4,128)(2,1)S(1)} %copy.223), channel_id=1, replica_groups=mesh['layer'=4,'prow'=16,'pcol'=8] {'layer','prow'}, dimensions={0} | all-to-all | bytes 393216 | tf_op jit(solution)/shard_map/all_to_all | solution.py:238
  281.8 9.0 %all_to_all.88 = bf16[8,4,16,128]{3,2,1,0:T(8,128)(2,1)S(1)} all-to-all(bf16[8,4,16,128]{3,2,1,0:T(8,128)(2,1)S(1)} %broadcast_in_dim.162), channel_id=1, replica_groups=mesh['layer'=4,'prow'=16,'pcol'=8] {'pcol'}, dimensions={0} | all-to-all | bytes 262144 | tf_op jit(solution)/shard_map/all_to_all | solution.py:9
  290.8 1.5 fusion.12
  292.2 1.6 fusion.6
  294.6 3.4 all-to-all-start.13
  297.9 1.6 convolution_subtract_fusion.7
  299.5 4.5 %all-to-all-done.13 = bf16[8,4,16,128]{3,2,1,0:T(8,128)(2,1)S(1)} async-done(((bf16[8,4,16,128]{3,2,1,0:T(8,128)(2,1)}), bf16[8,4,16,128]{3,2,1,0:T(8,128)(2,1)S(1)}, u32[]{:S(2)}, u32[]{:S(2)}) %all-to-all-start.13) | async-done | bytes 131104 | tf_op jit(solution)/shard_map/all_to_all | solution.py:9
  304.0 1.5 fusion.13
  305.5 1.6 fusion.7
  307.1 8.5 %all_to_all.89 = bf16[8,4,16,128]{3,2,1,0:T(8,128)(2,1)S(1)} all-to-all(bf16[8,4,16,128]{3,2,1,0:T(8,128)(2,1)S(1)} %broadcast_in_dim.164), channel_id=1, replica_groups=mesh['layer'=4,'prow'=16,'pcol'=8] {'pcol'}, dimensions={0} | all-to-all | bytes 262144 | tf_op jit(solution)/shard_map/all_to_all | solution.py:9
  315.7 1.5 fusion.15
  317.9 5.8 %all-to-all-start.15 = ((bf16[16,3,4,256]{3,2,1,0:T(4,128)(2,1)}), bf16[16,3,4,256]{3,2,1,0:T(4,128)(2,1)S(1)}, u32[]{:S(2)}, u32[]{:S(2)}) async-start(bf16[16,3,4,256]{3,2,1,0:T(4,128)(2,1)} %broadcast_in_dim.165), calls=%async_computation.15 | async-start | bytes 196608 | tf_op jit(solution)/shard_map/all_to_all | solution.py:9
  323.7 2.7 collective-permute-start.1
  326.4 10.0 %all-to-all-done.15 = bf16[16,3,4,256]{3,2,1,0:T(4,128)(2,1)S(1)} async-done(((bf16[16,3,4,256]{3,2,1,0:T(4,128)(2,1)}), bf16[16,3,4,256]{3,2,1,0:T(4,128)(2,1)S(1)}, u32[]{:S(2)}, u32[]{:S(2)}) %all-to-all-start.15) | async-done | bytes 98336 | tf_op jit(solution)/shard_map/all_to_all | solution.py:9
  337.3 3.6 %all-to-all-start.16 = ((bf16[4,16,3,4,256]{4,3,1,2,0:T(4,128)(2,1)}), bf16[4,16,3,4,256]{4,3,1,2,0:T(4,128)(2,1)S(1)}, u32[]{:S(2)}, u32[]{:S(2)}) async-start(bf16[4,16,3,4,256]{4,3,1,2,0:T(4,128)(2,1)} %broadcast_in_dim.166), calls=%async_computation.16 | async-start | bytes 786432 | tf_op jit(solution)/shard_map/all_to_all | solution.py:9
  341.8 0.9 copy.249
  342.7 5.5 %all-to-all-done.16 = bf16[4,16,3,4,256]{4,3,1,2,0:T(4,128)(2,1)S(1)} async-done(((bf16[4,16,3,4,256]{4,3,1,2,0:T(4,128)(2,1)}), bf16[4,16,3,4,256]{4,3,1,2,0:T(4,128)(2,1)S(1)}, u32[]{:S(2)}, u32[]{:S(2)}) %all-to-all-start.16) | async-done | bytes 393248 | tf_op jit(solution)/shard_map/all_to_all | solution.py:9
  348.5 0.9 copy.250
  (107 shorter events, 22.0 us)
Async XLA Ops:
  7.2 63.7 %copy-start.2 = (bf16[1,3,1,128,2,1,128]{6,4,5,3,2,1,0:T(2,128)(2,1)S(1)}, bf16[1,3,1,128,2,1,128]{6,4,5,3,2,1,0:T(2,128)(2,1)}, u32[]{:S(2)}) copy-start(bf16[1,3,1,128,2,1,128]{6,4,5,3,2,1,0:T(2,128)(2,1)} %param.11) | copy-start | bytes 589828
  7.2 27.1 %copy-start.3 = (s32[1,21,1,2,1]{1,4,3,2,0:T(1,128)S(1)}, s32[1,21,1,2,1]{1,4,3,2,0:T(1,128)}, u32[]{:S(2)}) copy-start(s32[1,21,1,2,1]{1,4,3,2,0:T(1,128)} %param.10) | copy-start | bytes 508
  7.2 43.4 %copy-start = (bf16[1,21,1,128,2,1,128]{6,4,5,3,2,1,0:T(2,128)(2,1)S(1)}, bf16[1,21,1,128,2,1,128]{6,4,5,3,2,1,0:T(2,128)(2,1)}, u32[]{:S(2)}) copy-start(bf16[1,21,1,128,2,1,128]{6,4,5,3,2,1,0:T(2,128)(2,1)} %param.9) | copy-start | bytes 4128772
  7.2 164.3 %all-gather.5.cloned.1.call-start = ((), (), s32[]{:S(2)}) async-start(), calls=%async_computation.17 | async-start | bytes 10027008 | tf_op jit(solution)/shard_map/all_gather | solution.py:148
  16.1 29.5 %all-to-all-start = ((bf16[16,16,256]{2,1,0:T(8,128)(2,1)}), bf16[16,16,256]{2,1,0:T(8,128)(2,1)S(1)}, u32[]{:S(2)}, u32[]{:S(2)}) async-start(bf16[16,16,256]{2,1,0:T(8,128)(2,1)} %bitcast.1), calls=%async_computation | async-start | bytes 262144 | tf_op jit(solution)/shard_map/all_to_all | solution.py:30
  31.3 259.5 %all-gather.7.cloned.1.call-start = ((), (), s32[]{:S(2)}) async-start(), calls=%async_computation.18 | async-start | bytes 6684672 | tf_op jit(solution)/shard_map/all_gather | solution.py:151
  46.3 19.3 %all-to-all-start.1 = ((bf16[16,16,256]{2,1,0:T(8,128)(2,1)}), bf16[16,16,256]{2,1,0:T(8,128)(2,1)S(1)}, u32[]{:S(2)}, u32[]{:S(2)}) async-start(bf16[16,16,256]{2,1,0:T(8,128)(2,1)} %broadcast_in_dim.139), calls=%async_computation.1 | async-start | bytes 262144 | tf_op jit(solution)/shard_map/all_to_all | solution.py:9
  66.6 14.6 %all-to-all-start.2 = ((bf16[8,128,256]{2,1,0:T(8,128)(2,1)}), bf16[8,128,256]{2,1,0:T(8,128)(2,1)S(1)}, u32[]{:S(2)}, u32[]{:S(2)}) async-start(bf16[8,128,256]{2,1,0:T(8,128)(2,1)} %broadcast_in_dim.142), calls=%async_computation.2 | async-start | bytes 1048576 | tf_op jit(solution)/shard_map/all_to_all | solution.py:9
  102.9 20.1 %all-to-all-start.4 = ((bf16[16,16,256]{2,1,0:T(8,128)(2,1)}), bf16[16,16,256]{2,1,0:T(8,128)(2,1)S(1)}, u32[]{:S(2)}, u32[]{:S(2)}) async-start(bf16[16,16,256]{2,1,0:T(8,128)(2,1)} %broadcast_in_dim.143), calls=%async_computation.4 | async-start | bytes 262144 | tf_op jit(solution)/shard_map/all_to_all | solution.py:9
  124.0 13.8 %all-to-all-start.5 = ((bf16[8,128,256]{2,1,0:T(8,128)(2,1)}), bf16[8,128,256]{2,1,0:T(8,128)(2,1)S(1)}, u32[]{:S(2)}, u32[]{:S(2)}) async-start(bf16[8,128,256]{2,1,0:T(8,128)(2,1)} %broadcast_in_dim.144), calls=%async_computation.5 | async-start | bytes 1048576 | tf_op jit(solution)/shard_map/all_to_all | solution.py:9
  139.7 29.4 %all-to-all-start.6 = ((bf16[16,16,640]{2,1,0:T(8,128)(2,1)}), bf16[16,16,640]{2,1,0:T(8,128)(2,1)S(1)}, u32[]{:S(2)}, u32[]{:S(2)}) async-start(bf16[16,16,640]{2,1,0:T(8,128)(2,1)} %pad_maximum_fusion.3), calls=%async_computation.6 | async-start | bytes 655360 | tf_op jit(solution)/shard_map/all_to_all | solution.py:189
  174.0 15.5 %all-to-all-start.7 = ((bf16[16,8,16,128]{3,2,1,0:T(8,128)(2,1)}), bf16[16,8,16,128]{3,2,1,0:T(8,128)(2,1)S(1)}, u32[]{:S(2)}, u32[]{:S(2)}) async-start(bf16[16,8,16,128]{3,2,1,0:T(8,128)(2,1)} %bitcast.29), calls=%async_computation.7 | async-start | bytes 1048576 | tf_op jit(solution)/shard_map/all_to_all | solution.py:205
  180.8 8.0 %collective-permute-start = (bf16[2,8,16,128]{3,1,2,0:T(8,128)(2,1)S(1)}, bf16[2,8,16,128]{3,1,2,0:T(8,128)(2,1)S(1)}, u32[]{:S(2)}, u32[]{:S(2)}) collective-permute-start(bf16[2,8,16,128]{3,1,2,0:T(8,128)(2,1)S(1)} %select_convert_fusion), channel_id=1, source_target_pairs={{0,128},{128,0},{256,384},{384,256},{1,129},{129,1},{257,385},{385... | collective-permute-start | bytes 196616 | tf_op jit(solution)/shard_map/ppermute | solution.py:45
  190.2 40.7 %copy-start.1 = (bf16[1,12,1,128,2,1,128]{6,4,5,3,2,1,0:T(2,128)(2,1)S(1)}, bf16[1,12,1,128,2,1,128]{6,4,5,3,2,1,0:T(2,128)(2,1)}, u32[]{:S(2)}) copy-start(bf16[1,12,1,128,2,1,128]{6,4,5,3,2,1,0:T(2,128)(2,1)} %param.12) | copy-start | bytes 2359300
  194.2 10.9 %all-to-all-start.8 = ((bf16[8,8,16,128]{3,2,1,0:T(8,128)(2,1)}), bf16[8,8,16,128]{3,2,1,0:T(8,128)(2,1)S(1)}, u32[]{:S(2)}, u32[]{:S(2)}) async-start(bf16[8,8,16,128]{3,2,1,0:T(8,128)(2,1)} %broadcast_in_dim.152), calls=%async_computation.8 | async-start | bytes 524288 | tf_op jit(solution)/shard_map/all_to_all | solution.py:9
  221.1 31.6 %all-to-all-start.10 = ((bf16[16,40,256]{2,1,0:T(8,128)(2,1)}), bf16[16,40,256]{2,1,0:T(8,128)(2,1)S(1)}, u32[]{:S(2)}, u32[]{:S(2)}) async-start(bf16[16,40,256]{2,1,0:T(8,128)(2,1)} %broadcast_in_dim.154), calls=%async_computation.10 | async-start | bytes 655360 | tf_op jit(solution)/shard_map/all_to_all | solution.py:9
  294.6 9.4 %all-to-all-start.13 = ((bf16[8,4,16,128]{3,2,1,0:T(8,128)(2,1)}), bf16[8,4,16,128]{3,2,1,0:T(8,128)(2,1)S(1)}, u32[]{:S(2)}, u32[]{:S(2)}) async-start(bf16[8,4,16,128]{3,2,1,0:T(8,128)(2,1)} %broadcast_in_dim.163), calls=%async_computation.13 | async-start | bytes 262144 | tf_op jit(solution)/shard_map/all_to_all | solution.py:9
  317.9 18.5 %all-to-all-start.15 = ((bf16[16,3,4,256]{3,2,1,0:T(4,128)(2,1)}), bf16[16,3,4,256]{3,2,1,0:T(4,128)(2,1)S(1)}, u32[]{:S(2)}, u32[]{:S(2)}) async-start(bf16[16,3,4,256]{3,2,1,0:T(4,128)(2,1)} %broadcast_in_dim.165), calls=%async_computation.15 | async-start | bytes 196608 | tf_op jit(solution)/shard_map/all_to_all | solution.py:9
  323.7 18.1 %collective-permute-start.1 = (bf16[16,24,256]{2,1,0:T(8,128)(2,1)S(1)}, bf16[16,24,256]{2,1,0:T(8,128)(2,1)S(1)}, u32[]{:S(2)}, u32[]{:S(2)}) collective-permute-start(bf16[16,24,256]{2,1,0:T(8,128)(2,1)S(1)} %get-tuple-element.49), channel_id=1, source_target_pairs={{0,128},{128,0},{256,384},{384,256},{1,129},{129,1},{257,385},{385... | collective-permute-start | bytes 589832 | tf_op jit(solution)/shard_map/ppermute | solution.py:45
  337.3 10.9 %all-to-all-start.16 = ((bf16[4,16,3,4,256]{4,3,1,2,0:T(4,128)(2,1)}), bf16[4,16,3,4,256]{4,3,1,2,0:T(4,128)(2,1)S(1)}, u32[]{:S(2)}, u32[]{:S(2)}) async-start(bf16[4,16,3,4,256]{4,3,1,2,0:T(4,128)(2,1)} %broadcast_in_dim.166), calls=%async_computation.16 | async-start | bytes 786432 | tf_op jit(solution)/shard_map/all_to_all | solution.py:9
Sparse Core Ops, SparseCore 0:
  16.2 150.4 all-gather.4
  169.4 103.6 all-gather.6

commit v6 on v5

--- a/solution.py
+++ b/solution.py
@@ -1,7 +1,14 @@
+import functools
+
 import jax
 import jax.numpy as jnp
 from jax import lax
+from jax.experimental import pallas as pl
+from jax.experimental.pallas import tpu as pltpu
 from jax.sharding import PartitionSpec as P
+
+VMEM = pl.BlockSpec(memory_space=pltpu.VMEM)
+ANY = pl.BlockSpec(memory_space=pl.ANY)
 
 
 def shared_with_all(value, axis):
@@ -61,24 +68,171 @@
     return inside, outside
 
 
-def slice_solve(first, sums, gathered, panels):
-    sums = [first] + sums
+def as_rows(tiles):
+    return tiles.reshape(tiles.shape[0] * tiles.shape[1], tiles.shape[2])
+
+
+def times_rows(solved, tiles):
+    return lax.dot_general(
+        solved, as_rows(tiles), (((1,), (1,)), ((), ())), preferred_element_type=jnp.float32
+    )
+
+
+def fetch(gathered, block, buffer, arrived):
+    copies = []
+    for p in range(buffer.shape[0]):
+        copies.append(
+            pltpu.make_async_copy(gathered.at[p, block], buffer.at[p], arrived.at[p])
+        )
+        copies[-1].start()
+    return copies
+
+
+def wait_all(copies):
+    for copy in copies:
+        copy.wait()
+
+
+def total_of(received):
+    total = received[0].astype(jnp.float32)
+    for w in range(1, received.shape[0]):
+        total = total + received[w].astype(jnp.float32)
+    return total
+
+
+def step_kernel(panel, block, received, gathered, sums, solved, copies, inverse, tiles, first, then):
+    stored = fetch(gathered, panel, inverse, first)
+    wanted = fetch(gathered, block, tiles, then)
+    total = total_of(received).astype(jnp.bfloat16)
+    wait_all(stored)
+    result = jnp.dot(total, as_rows(inverse[...]), preferred_element_type=jnp.float32)
+    result = result.astype(jnp.bfloat16)
+    solved[...] = result
+    wait_all(wanted)
+    left = (sums[...] - times_rows(result, tiles[...])).astype(jnp.bfloat16)
+    for w in range(copies.shape[0]):
+        copies[w] = left
+
+
+def last_kernel(panel, received, gathered, solved, inverse, first):
+    stored = fetch(gathered, panel, inverse, first)
+    total = total_of(received).astype(jnp.bfloat16)
+    wait_all(stored)
+    result = jnp.dot(total, as_rows(inverse[...]), preferred_element_type=jnp.float32)
+    solved[...] = result.astype(jnp.bfloat16)
+
+
+def update_kernel(block, solved, gathered, sums, left, tiles, then):
+    wait_all(fetch(gathered, block, tiles, then))
+    left[...] = sums[...] - times_rows(solved[...], tiles[...])
+
+
+def take_off(received, product, target, line):
+    ways, _, width = received.shape
+    tile_rows = product.shape[1] // ways
+    start = width - (3 - target) * tile_rows
+    for p in range(ways):
+        here = slice(p * tile_rows, (p + 1) * tile_rows)
+        part = received[p, :, start : start + tile_rows].astype(jnp.float32)
+        line[:, here] = part - product[:, here]
+
+
+def open_kernel(block, received, gathered, solved, copies, tiles, line, then):
+    wanted = fetch(gathered, block, tiles, then)
+    total = received[0, :, : solved.shape[1]].astype(jnp.float32)
+    for w in range(1, received.shape[0]):
+        total = total + received[w, :, : solved.shape[1]].astype(jnp.float32)
+    result = total.astype(jnp.bfloat16)
+    solved[...] = result
+    wait_all(wanted)
+    take_off(received, times_rows(result, tiles[...]), 0, line)
+    half = copies.shape[1]
+    for h in range(2):
+        part = line[h * half : (h + 1) * half, :].astype(jnp.bfloat16)
+        for w in range(copies.shape[0] // 2):
+            copies[h * (copies.shape[0] // 2) + w] = part
+
+
+def later_kernel(block, received, solved, gathered, sums, tiles, more, line, first, then):
+    wanted = fetch(gathered, block, tiles, first)
+    beside = fetch(gathered, block + 1, more, then)
+    wait_all(wanted)
+    take_off(received, times_rows(solved[...], tiles[...]), 1, line)
+    sums[0] = line[...]
+    wait_all(beside)
+    take_off(received, times_rows(solved[...], more[...]), 2, line)
+    sums[1] = line[...]
+
+
+def call(kernel, shapes, specs, buffers, blocks, columns, gathered, *operands):
+    tile = gathered.shape[:1] + gathered.shape[2:]
+    size = tile[0] * tile[1] * tile[2]
+    scratch = [pltpu.VMEM(tile, jnp.bfloat16)] * blocks + buffers
+    scratch += [pltpu.SemaphoreType.DMA((tile[0],))] * blocks
+    return pl.pallas_call(
+        kernel,
+        out_shape=shapes,
+        in_specs=specs,
+        out_specs=tuple(VMEM for _ in shapes) if isinstance(shapes, tuple) else VMEM,
+        scratch_shapes=scratch,
+        compiler_params=pltpu.CompilerParams(vmem_limit_bytes=59 * 2**20),
+        cost_estimate=pl.CostEstimate(
+            flops=2 * columns * size * blocks, bytes_accessed=2 * size * blocks, transcendentals=0
+        ),
+    )(*operands)
+
+
+def slice_solve(received, sums, gathered, panels):
+    columns, rows = received.shape[1:]
+    col_width = gathered.shape[-1]
+    ways = lax.axis_size("pcol")
+    solved_shape = jax.ShapeDtypeStruct((columns, col_width), jnp.bfloat16)
+    copies_shape = jax.ShapeDtypeStruct((ways, columns, rows), jnp.bfloat16)
+    sums_shape = jax.ShapeDtypeStruct((columns, rows), jnp.float32)
+    sums = [None] + list(sums)
     solved = []
     offset = panels
-    for step in range(panels):
-        residual = (first if step == 0 else row_total(sums[step])).astype(jnp.bfloat16)
-        result = lax.dot_general(
-            residual,
-            gathered[:, step],
-            (((1, 2), (0, 1)), ((), ())),
-            preferred_element_type=jnp.float32,
-        ).astype(jnp.bfloat16)
+    for step in range(panels - 1):
+        result, copies = call(
+            functools.partial(step_kernel, step, offset),
+            (solved_shape, copies_shape),
+            [VMEM, ANY, VMEM],
+            [],
+            2,
+            columns,
+            gathered,
+            received,
+            gathered,
+            sums[step + 1],
+        )
         solved.append(result)
-        for target in range(step + 1, panels):
-            sums[target] = sums[target] - transposed_product(
-                result, gathered[:, offset + target - step - 1]
+        received = lax.all_to_all(copies, "pcol", 0, 0)
+        for target in range(step + 2, panels):
+            sums[target] = call(
+                functools.partial(update_kernel, offset + target - step - 1),
+                sums_shape,
+                [VMEM, ANY, VMEM],
+                [],
+                1,
+                columns,
+                gathered,
+                result,
+                gathered,
+                sums[target],
             )
         offset += panels - 1 - step
+    result = call(
+        functools.partial(last_kernel, panels - 1),
+        solved_shape,
+        [VMEM, ANY],
+        [],
+        1,
+        columns,
+        gathered,
+        received,
+        gathered,
+    )
+    solved.append(result)
     return jnp.stack(solved)
 
 
@@ -141,13 +295,13 @@
     ahead = slice(own_tiles.shape[0] - 2 * panels, own_tiles.shape[0] - panels)
     early_tiles = own_blocks[0, ahead, 0].reshape(-1, tile_rows, cycles, tile_rows)
     early_kept = own_pattern[0, ahead].reshape(-1, 1, cycles, 1) > 0
-    early_cols = jnp.where(early_kept, early_tiles, jnp.zeros((), own_tiles.dtype)).reshape(
-        -1, tile_rows, col_width
-    )
-    pair_in, pair_out = by_column(as_blocks(pair_blocks), panels, 2 * panels)
-    pair_all = lax.all_gather(
-        jnp.concatenate([as_blocks(pair_inverse)] + pair_in + [early_cols]), "prow"
-    )
+    early_tiles = jnp.where(early_kept, early_tiles, jnp.zeros((), own_tiles.dtype))
+    _, pair_out = by_column(as_blocks(pair_blocks), panels, 2 * panels)
+    pair_tiles = pair_blocks[0, :, 0].reshape(-1, tile_rows, cycles, tile_rows)
+    tiles_in, _ = by_column(pair_tiles, panels, 2 * panels)
+    first_tiles = pair_inverse.reshape(-1, tile_rows, cycles, tile_rows)
+    ready = lax.optimization_barrier(jnp.concatenate([first_tiles] + tiles_in + [early_tiles]))
+    pair_all = lax.all_gather(ready.reshape(-1, tile_rows, col_width), "prow")
     root_all = lax.all_gather(
         jnp.concatenate([as_blocks(root_inverse), as_blocks(root_blocks)]), "prow"
     )
@@ -186,36 +340,48 @@
         ],
         axis=-1,
     )
-    received = lax.all_to_all(pieces, "prow", 0, 0).astype(jnp.float32)
-    last_own = jnp.sum(received[:, :, :col_width], axis=0).astype(jnp.bfloat16)
-    parts = received[:, :, col_width:].reshape(prows, wide, panels, tile_rows)
-    ancestors = [
-        parts[:, :, t].transpose(1, 0, 2)
-        - transposed_product(last_own, pair_all[:, t - panels])
-        for t in range(panels)
-    ]
-
+    received = lax.all_to_all(pieces, "prow", 0, 0)
     pcols = lax.axis_size("pcol")
-    halves = ancestors[0].astype(jnp.bfloat16).reshape(2, 1, half, prows, tile_rows)
-    pieces = jnp.broadcast_to(halves, (2, pcols, half, prows, tile_rows))
+    rows = prows * tile_rows
+    count = pair_all.shape[1]
+    line = pltpu.VMEM((wide, rows), jnp.float32)
+    last_own, copies = call(
+        functools.partial(open_kernel, count - panels),
+        (
+            jax.ShapeDtypeStruct((wide, col_width), jnp.bfloat16),
+            jax.ShapeDtypeStruct((2 * pcols, half, rows), jnp.bfloat16),
+        ),
+        [VMEM, ANY],
+        [line],
+        1,
+        wide,
+        pair_all,
+        received,
+        pair_all,
+    )
+
     groups = [
         [layer * pcols + c for layer in (low, low + 1) for c in range(pcols)]
         for low in range(0, layers, 2)
     ]
-    partials = lax.all_to_all(
-        pieces.reshape((2 * pcols,) + halves.shape[2:]),
-        ("layer", "pcol"),
-        0,
-        0,
-        axis_index_groups=groups,
-    )
-    first = jnp.sum(partials.astype(jnp.float32), axis=0)
-    later = jnp.stack(ancestors[1:])
+    partials = lax.all_to_all(copies, ("layer", "pcol"), 0, 0, axis_index_groups=groups)
+    later = call(
+        functools.partial(later_kernel, count - panels + 1),
+        jax.ShapeDtypeStruct((panels - 1, wide, rows), jnp.float32),
+        [VMEM, VMEM, ANY],
+        [line],
+        2,
+        wide,
+        pair_all,
+        received,
+        last_own,
+        pair_all,
+    )
     low, high = later[:, :half], later[:, half:]
     kept = jnp.where(second == 0, low, high)
     given = jnp.where(second == 0, high, low)
     later = kept + layer_swap(given.astype(jnp.bfloat16), 1).astype(jnp.float32)
-    pair_solved = slice_solve(first, list(later), pair_all, panels)
+    pair_solved = slice_solve(partials, list(later), pair_all, panels)
     payload = jnp.concatenate([pair_solved.reshape(panels * half, col_width), last_own])
     everywhere = shared_with_all(payload, "prow")
     last_turned = everywhere[:, panels * half :].reshape(rhs_width, col_width)
@@ -237,9 +403,10 @@
     pieces = pieces.transpose(1, 0, 2, 3, 4).reshape(layers * prows, narrow, panels, tile_rows)
     received = lax.all_to_all(pieces, ("layer", "prow"), 0, 0)
     received = received.reshape(layers, prows, narrow, panels, tile_rows)
-    sums = jnp.sum(received.astype(jnp.float32), axis=0).transpose(1, 0, 2, 3)
-    sums = [sums[:, :, t] for t in range(panels)]
-    root_solved = slice_solve(row_total(sums[0]), sums[1:], root_all, panels)
+    sums = jnp.sum(received.astype(jnp.float32), axis=0).transpose(2, 1, 0, 3)
+    sums = sums.reshape(panels, narrow, rows)
+    received = shared_with_all(sums[0].astype(jnp.bfloat16), "pcol")
+    root_solved = slice_solve(received, list(sums[1:]), root_all, panels)
     by_layer = shared_with_all(shared_with_all(root_solved, "prow"), "layer")
     root_turned = by_layer.transpose(2, 1, 0, 3, 4).reshape(panels, rhs_width, col_width)
 

time: 359 us -> 382 us (1.064)
  Pallas kernels: 0 us -> 38.1 us
  matrix products: 30.2 us -> 5.8 us
  waiting for transfers between devices: 131 us -> 143 us
  blocking collectives: 73.7 us -> 68.5 us
    pallas_call x0 -> x10, Pallas kernels: none -> 38.1 us  [call(): pl.pallas_call(kernel, out_shape=shapes, in_specs=specs, out_specs=tuple(...]
    all_to_all x2 -> x4, waiting for transfers between devices: 24.5 us -> 41.1 us  [the longest x1 24.5 us: local(): received = lax.all_to_all(pieces, 'prow', 0, 0)]
    dot_general x13 -> x4, matrix products: 16.3 us -> 0.9 us  [transposed_product(): lax.dot_general(solved, blocks, (((solved.ndim - 1,), (blocks.ndim - 1,))...]
    dot_general x6 -> x0, matrix products: 9.01 us -> none  [slice_solve(): lax.dot_general(residual, gathered[:, step], (((1, 2), (0, 1)), ((), ()))...]
    all_to_all x2 -> x4, starting transfers between devices: 8.54 us -> 15.4 us  [the longest x2 6.81 us: slice_solve(): received = lax.all_to_all(copies, 'pcol', 0, 0)]
    all_to_all x3 -> x2, blocking collectives: 27.4 us -> 21.7 us  [slice_solve(): received = lax.all_to_all(copies, 'pcol', 0, 0)]
    unnamed x10 -> x46, local copies, waits for them, and re-layouts: 1.86 us -> 6.91 us
    ppermute x2, waiting for transfers between devices: 4.2 us -> 0.01 us  [layer_swap(): lax.ppermute(value, 'layer', [(i, i ^ apart) for i in range(lax.axis_size...]
  transfers between devices with their start and end apart: 16 -> 17, of which waited for: 12 -> 13; matrix products, arithmetic and copies ran while one was open for 13% -> 6% of each run, Pallas kernels for 0% -> 7%
where the time goes in v6:
time: 382 us; the launch traced here: 379 us
  waiting for transfers between devices  143 us (37%)
  starting transfers between devices  73.6 us (19%)
  blocking collectives  68.5 us (18%)
  Pallas kernels  38.1 us (10%)
  local copies, waits for them, and re-layouts  24.3 us (6%)
  between operations  14.7 us (4%)
  other arithmetic  10.3 us (3%)
  matrix products  5.8 us (2%)
    all_to_all x8, waiting for transfers between devices, shared_with_all(): return lax.all_to_all(copies, axis, 0, 0)  88 us
    pallas_call x10, Pallas kernels, call(): pl.pallas_call(kernel, out_shape=shapes, in_specs=specs, out_specs=tuple(...  38.1 us
    all_to_all x8, starting transfers between devices, shared_with_all(): return lax.all_to_all(copies, axis, 0, 0)  37.1 us
    all_to_all x1, blocking collectives, local(): received = lax.all_to_all(pieces, ('layer', 'prow'), 0, 0)  26.6 us
    all_to_all x1, waiting for transfers between devices, local(): received = lax.all_to_all(pieces, 'prow', 0, 0)  24.5 us
    all_to_all x2, blocking collectives, slice_solve(): received = lax.all_to_all(copies, 'pcol', 0, 0)  21.7 us
    all_to_all x1, blocking collectives, column_total(): received = lax.all_to_all(pieces, 'prow', 0, 0)  20.2 us
    all_to_all x1, starting transfers between devices, column_total(): received = lax.all_to_all(pieces, 'prow', 0, 0)  15.2 us
  transfers between devices with their start and end apart: 17, of which 13 were waited for; matrix products, arithmetic and copies ran while one was open for 6% of the time, Pallas kernels for 7%

profile of v6, /device:TPU:32, one launch (start us, length us, event | category | flops | bytes accessed | tf_op | source)
XLA Modules:
  0.0 378.6 jit_solution(15045442812088851291)
XLA Ops:
  7.2 0.9 slice.138
  8.1 1.7 convolution_convert_fusion.2
  10.7 1.0 slice_bitcast_fusion.1
  11.7 0.9 slice_bitcast_fusion.10
  12.6 1.2 broadcast_select_fusion.1
  13.8 1.9 pad_maximum_fusion
  15.6 1.2 all_gather_reshape.3
  17.2 0.8 pad_maximum_fusion.2
  18.0 15.2 %all-to-all-start = ((bf16[16,16,256]{2,1,0:T(8,128)(2,1)}), bf16[16,16,256]{2,1,0:T(8,128)(2,1)S(1)}, u32[]{:S(2)}, u32[]{:S(2)}) async-start(bf16[16,16,256]{2,1,0:T(8,128)(2,1)} %bitcast.1), calls=%async_computation | async-start | bytes 262144 | tf_op jit(solution)/shard_map/all_to_all | solution.py:37
  33.3 14.1 %all-to-all-done = bf16[16,16,256]{2,1,0:T(8,128)(2,1)S(1)} async-done(((bf16[16,16,256]{2,1,0:T(8,128)(2,1)}), bf16[16,16,256]{2,1,0:T(8,128)(2,1)S(1)}, u32[]{:S(2)}, u32[]{:S(2)}) %all-to-all-start) | async-done | bytes 131104 | tf_op jit(solution)/shard_map/all_to_all | solution.py:37
  48.2 5.0 %all-to-all-start.1 = ((bf16[16,16,256]{2,1,0:T(8,128)(2,1)}), bf16[16,16,256]{2,1,0:T(8,128)(2,1)S(1)}, u32[]{:S(2)}, u32[]{:S(2)}) async-start(bf16[16,16,256]{2,1,0:T(8,128)(2,1)} %broadcast_in_dim.104), calls=%async_computation.1 | async-start | bytes 262144 | tf_op jit(solution)/shard_map/all_to_all | solution.py:16
  53.2 1.2 broadcast_select_fusion
  54.6 13.0 %all-to-all-done.1 = bf16[16,16,256]{2,1,0:T(8,128)(2,1)S(1)} async-done(((bf16[16,16,256]{2,1,0:T(8,128)(2,1)}), bf16[16,16,256]{2,1,0:T(8,128)(2,1)S(1)}, u32[]{:S(2)}, u32[]{:S(2)}) %all-to-all-start.1) | async-done | bytes 131104 | tf_op jit(solution)/shard_map/all_to_all | solution.py:16
  67.8 0.8 broadcast_in_dim.107
  68.6 4.3 %all-to-all-start.2 = ((bf16[8,128,256]{2,1,0:T(8,128)(2,1)}), bf16[8,128,256]{2,1,0:T(8,128)(2,1)S(1)}, u32[]{:S(2)}, u32[]{:S(2)}) async-start(bf16[8,128,256]{2,1,0:T(8,128)(2,1)} %broadcast_in_dim.107), calls=%async_computation.2 | async-start | bytes 1048576 | tf_op jit(solution)/shard_map/all_to_all | solution.py:16
  73.0 10.2 %all-to-all-done.2 = bf16[8,128,256]{2,1,0:T(8,128)(2,1)S(1)} async-done(((bf16[8,128,256]{2,1,0:T(8,128)(2,1)}), bf16[8,128,256]{2,1,0:T(8,128)(2,1)S(1)}, u32[]{:S(2)}, u32[]{:S(2)}) %all-to-all-start.2) | async-done | bytes 524320 | tf_op jit(solution)/shard_map/all_to_all | solution.py:16
  83.3 1.0 convolution_convert_fusion.1
  84.4 20.2 %all_to_all.85 = bf16[16,16,256]{2,1,0:T(8,128)(2,1)S(1)} all-to-all(bf16[16,16,256]{2,1,0:T(8,128)(2,1)S(1)} %bitcast.224), channel_id=1, replica_groups=mesh['layer'=4,'prow'=16,'pcol'=8] {'prow'}, dimensions={0} | all-to-all | bytes 262144 | tf_op jit(solution)/shard_map/all_to_all | solution.py:37
  105.3 5.0 %all-to-all-start.4 = ((bf16[16,16,256]{2,1,0:T(8,128)(2,1)}), bf16[16,16,256]{2,1,0:T(8,128)(2,1)S(1)}, u32[]{:S(2)}, u32[]{:S(2)}) async-start(bf16[16,16,256]{2,1,0:T(8,128)(2,1)} %broadcast_in_dim.108), calls=%async_computation.4 | async-start | bytes 262144 | tf_op jit(solution)/shard_map/all_to_all | solution.py:16
  111.8 13.5 %all-to-all-done.4 = bf16[16,16,256]{2,1,0:T(8,128)(2,1)S(1)} async-done(((bf16[16,16,256]{2,1,0:T(8,128)(2,1)}), bf16[16,16,256]{2,1,0:T(8,128)(2,1)S(1)}, u32[]{:S(2)}, u32[]{:S(2)}) %all-to-all-start.4) | async-done | bytes 131104 | tf_op jit(solution)/shard_map/all_to_all | solution.py:16
  125.4 0.8 broadcast_in_dim.109
  126.3 3.5 all-to-all-start.5
  130.8 9.2 %all-to-all-done.5 = bf16[8,128,256]{2,1,0:T(8,128)(2,1)S(1)} async-done(((bf16[8,128,256]{2,1,0:T(8,128)(2,1)}), bf16[8,128,256]{2,1,0:T(8,128)(2,1)S(1)}, u32[]{:S(2)}, u32[]{:S(2)}) %all-to-all-start.5) | async-done | bytes 524320 | tf_op jit(solution)/shard_map/all_to_all | solution.py:16
  140.1 1.0 convolution_convert_fusion
  141.9 5.0 %all-to-all-start.6 = ((bf16[16,16,640]{2,1,0:T(8,128)(2,1)}), bf16[16,16,640]{2,1,0:T(8,128)(2,1)S(1)}, u32[]{:S(2)}, u32[]{:S(2)}) async-start(bf16[16,16,640]{2,1,0:T(8,128)(2,1)} %pad_maximum_fusion.3), calls=%async_computation.6 | async-start | bytes 655360 | tf_op jit(solution)/shard_map/all_to_all | solution.py:343
  146.9 24.5 %all-to-all-done.6.received = bf16[16,16,640]{2,1,0:T(8,128)(2,1)S(1)} async-done(((bf16[16,16,640]{2,1,0:T(8,128)(2,1)}), bf16[16,16,640]{2,1,0:T(8,128)(2,1)S(1)}, u32[]{:S(2)}, u32[]{:S(2)}) %all-to-all-start.6) | async-done | bytes 327712 | tf_op jit(solution)/shard_map/all_to_all | solution.py:343
  172.1 3.6 shard_map.112
  175.7 4.3 %shard_map.113 = f32[2,16,2048]{2,1,0:T(8,128)} custom-call(bf16[16,16,640]{2,1,0:T(8,128)(2,1)} %copy-done, bf16[16,256]{1,0:T(8,128)(2,1)} %get-tuple-element.30.solved, bf16[16,9,128,256]{3,2,1,0:T(8,128)(2,1)} %all-gather.4.cloned.1.call-done.gathered), custom_call_target="tpu_custom_call" | custom-call | flops 33554432 | bytes 2097152 | tf_op jit(solution)/shard_map/pallas_call | solution.py:172
  180.0 1.0 select_convert_fusion
  181.0 3.5 collective-permute-start
  184.5 3.6 all-to-all-start.7
  188.8 10.1 %all-to-all-done.7.received = bf16[16,8,2048]{2,1,0:T(8,128)(2,1)S(1)} async-done(((bf16[16,8,2048]{2,1,0:T(8,128)(2,1)}), bf16[16,8,2048]{2,1,0:T(8,128)(2,1)S(1)}, u32[]{:S(2)}, u32[]{:S(2)}) %all-to-all-start.7) | async-done | bytes 524320 | tf_op jit(solution)/shard_map/all_to_all | solution.py:367
  198.9 0.8 copy-done.1
  199.7 4.5 %shard_map.114 = (bf16[8,256]{1,0:T(8,128)(2,1)}, bf16[8,8,2048]{2,1,0:T(8,128)(2,1)}) custom-call(bf16[16,8,2048]{2,1,0:T(8,128)(2,1)} %copy-done.1, bf16[16,9,128,256]{3,2,1,0:T(8,128)(2,1)} %all-gather.4.cloned.1.call-done.gathered, f32[8,2048]{1,0:T(8,128)} %get-tuple-element.70.sums), custom_call_target="tpu_custom_call" | custom-call | flops 16777216 | bytes 2097152 | tf_op jit(solution)/shard_map/pallas_call | solution.py:172
  204.3 3.4 all-to-all-start.8
  207.7 3.2 shard_map.115.sums
  210.9 4.2 %all-to-all-done.8.received = bf16[8,8,2048]{2,1,0:T(8,128)(2,1)S(1)} async-done(((bf16[8,8,2048]{2,1,0:T(8,128)(2,1)}), bf16[8,8,2048]{2,1,0:T(8,128)(2,1)S(1)}, u32[]{:S(2)}, u32[]{:S(2)}) %all-to-all-start.8) | async-done | bytes 262176 | tf_op jit(solution)/shard_map/all_to_all | solution.py:209
  215.9 4.4 %shard_map.116 = (bf16[8,256]{1,0:T(8,128)(2,1)}, bf16[8,8,2048]{2,1,0:T(8,128)(2,1)}) custom-call(bf16[8,8,2048]{2,1,0:T(8,128)(2,1)} %copy-done.4, bf16[16,9,128,256]{3,2,1,0:T(8,128)(2,1)} %all-gather.4.cloned.1.call-done.gathered, f32[8,2048]{1,0:T(8,128)} %shard_map.115.sums), custom_call_target="tpu_custom_call" | custom-call | flops 16777216 | bytes 2097152 | tf_op jit(solution)/shard_map/pallas_call | solution.py:172
  220.3 11.6 %all_to_all.86.received = bf16[8,8,2048]{2,1,0:T(8,128)(2,1)} all-to-all(bf16[8,8,2048]{2,1,0:T(8,128)(2,1)} %get-tuple-element.34), channel_id=1, replica_groups=mesh['layer'=4,'prow'=16,'pcol'=8] {'pcol'}, dimensions={0} | all-to-all | bytes 524288 | tf_op jit(solution)/shard_map/all_to_all | solution.py:209
  231.9 3.2 shard_map.117
  235.1 0.8 maximum_bitcast_fusion
  236.6 7.2 %all-to-all-start.10 = ((bf16[16,40,256]{2,1,0:T(8,128)(2,1)}), bf16[16,40,256]{2,1,0:T(8,128)(2,1)S(1)}, u32[]{:S(2)}, u32[]{:S(2)}) async-start(bf16[16,40,256]{2,1,0:T(8,128)(2,1)} %broadcast_in_dim.113), calls=%async_computation.10 | async-start | bytes 655360 | tf_op jit(solution)/shard_map/all_to_all | solution.py:16
  243.8 0.8 slice.189
  244.6 1.8 slice.164
  247.4 20.9 %all-to-all-done.10 = bf16[16,40,256]{2,1,0:T(8,128)(2,1)S(1)} async-done(((bf16[16,40,256]{2,1,0:T(8,128)(2,1)}), bf16[16,40,256]{2,1,0:T(8,128)(2,1)S(1)}, u32[]{:S(2)}, u32[]{:S(2)}) %all-to-all-start.10) | async-done | bytes 327712 | tf_op jit(solution)/shard_map/all_to_all | solution.py:16
  270.0 26.6 %all_to_all.87 = bf16[64,4,3,128]{3,1,2,0:T(4,128)(2,1)S(1)} all-to-all(bf16[64,4,3,128]{3,1,2,0:T(4,128)(2,1)S(1)} %copy.124), channel_id=1, replica_groups=mesh['layer'=4,'prow'=16,'pcol'=8] {'layer','prow'}, dimensions={0} | all-to-all | bytes 393216 | tf_op jit(solution)/shard_map/all_to_all | solution.py:404
  297.4 3.4 all-to-all-start.12
  301.4 5.4 %all-to-all-done.12.received = bf16[8,4,2048]{2,1,0:T(4,128)(2,1)S(1)} async-done(((bf16[8,4,2048]{2,1,0:T(4,128)(2,1)}), bf16[8,4,2048]{2,1,0:T(4,128)(2,1)S(1)}, u32[]{:S(2)}, u32[]{:S(2)}) %all-to-all-start.12) | async-done | bytes 131104 | tf_op jit(solution)/shard_map/all_to_all | solution.py:16
  307.5 4.3 %shard_map.118 = (bf16[4,256]{1,0:T(4,128)(2,1)}, bf16[8,4,2048]{2,1,0:T(4,128)(2,1)}) custom-call(bf16[8,4,2048]{2,1,0:T(4,128)(2,1)} %copy-done.7, bf16[16,6,128,256]{3,2,1,0:T(8,128)(2,1)} %bitcast.197, f32[4,2048]{1,0:T(4,128)} %bitcast.238), custom_call_target="tpu_custom_call" | custom-call | flops 8388608 | bytes 2097152 | tf_op jit(solution)/shard_map/pallas_call | solution.py:172
  311.8 3.4 all-to-all-start.13
  315.8 3.1 shard_map.119.sums
  319.0 2.3 all-to-all-done.13.received
  321.9 4.3 %shard_map.120 = (bf16[4,256]{1,0:T(4,128)(2,1)}, bf16[8,4,2048]{2,1,0:T(4,128)(2,1)}) custom-call(bf16[8,4,2048]{2,1,0:T(4,128)(2,1)} %copy-done.8, bf16[16,6,128,256]{3,2,1,0:T(8,128)(2,1)} %bitcast.199, f32[4,2048]{1,0:T(4,128)} %shard_map.119.sums), custom_call_target="tpu_custom_call" | custom-call | flops 8388608 | bytes 2097152 | tf_op jit(solution)/shard_map/pallas_call | solution.py:172
  326.2 10.1 %all_to_all.88.received = bf16[8,4,2048]{2,1,0:T(4,128)(2,1)} all-to-all(bf16[8,4,2048]{2,1,0:T(4,128)(2,1)} %get-tuple-element.40), channel_id=1, replica_groups=mesh['layer'=4,'prow'=16,'pcol'=8] {'pcol'}, dimensions={0} | all-to-all | bytes 262144 | tf_op jit(solution)/shard_map/all_to_all | solution.py:209
  336.3 3.1 shard_map.121
  340.8 5.3 %all-to-all-start.15 = ((bf16[16,3,4,256]{3,2,1,0:T(4,128)(2,1)}), bf16[16,3,4,256]{3,2,1,0:T(4,128)(2,1)S(1)}, u32[]{:S(2)}, u32[]{:S(2)}) async-start(bf16[16,3,4,256]{3,2,1,0:T(4,128)(2,1)} %broadcast_in_dim.122), calls=%async_computation.15 | async-start | bytes 196608 | tf_op jit(solution)/shard_map/all_to_all | solution.py:16
  346.2 2.3 collective-permute-start.1
  348.5 10.3 %all-to-all-done.15 = bf16[16,3,4,256]{3,2,1,0:T(4,128)(2,1)S(1)} async-done(((bf16[16,3,4,256]{3,2,1,0:T(4,128)(2,1)}), bf16[16,3,4,256]{3,2,1,0:T(4,128)(2,1)S(1)}, u32[]{:S(2)}, u32[]{:S(2)}) %all-to-all-start.15) | async-done | bytes 98336 | tf_op jit(solution)/shard_map/all_to_all | solution.py:16
  358.9 0.9 broadcast_in_dim.123
  359.8 3.5 all-to-all-start.16
  363.4 0.8 pad_maximum_fusion.1
  364.2 0.9 copy.136
  365.2 5.5 %all-to-all-done.16 = bf16[4,16,3,4,256]{4,3,1,2,0:T(4,128)(2,1)S(1)} async-done(((bf16[4,16,3,4,256]{4,3,1,2,0:T(4,128)(2,1)}), bf16[4,16,3,4,256]{4,3,1,2,0:T(4,128)(2,1)S(1)}, u32[]{:S(2)}, u32[]{:S(2)}) %all-to-all-start.16) | async-done | bytes 393248 | tf_op jit(solution)/shard_map/all_to_all | solution.py:16
  370.9 0.9 copy.137
  (111 shorter events, 17.4 us)
Async XLA Ops:
  7.2 164.2 %all-gather.4.cloned.1.call-start = ((), (), s32[]{:S(2)}) async-start(), calls=%async_computation.17 | async-start | bytes 10027008 | tf_op jit(solution)/shard_map/all_gather | solution.py:304
  13.7 3.2 copy-start.10
  15.6 1.4 copy-start.11
  16.8 16.4 %copy-start.16 = (s32[1,21,1,2,1]{1,4,3,2,0:T(1,128)S(1)}, s32[1,21,1,2,1]{1,4,3,2,0:T(1,128)}, u32[]{:S(2)}) copy-start(s32[1,21,1,2,1]{1,4,3,2,0:T(1,128)} %param.10) | copy-start | bytes 508
  16.8 36.4 %copy-start.2 = (bf16[1,21,1,128,2,1,128]{6,4,5,3,2,1,0:T(2,128)(2,1)S(1)}, bf16[1,21,1,128,2,1,128]{6,4,5,3,2,1,0:T(2,128)(2,1)}, u32[]{:S(2)}) copy-start(bf16[1,21,1,128,2,1,128]{6,4,5,3,2,1,0:T(2,128)(2,1)} %param.9) | copy-start | bytes 4128772
  16.8 284.6 %all-gather.6.cloned.1.call-start = ((), (), s32[]{:S(2)}) async-start(), calls=%async_computation.18 | async-start | bytes 6684672 | tf_op jit(solution)/shard_map/all_gather | solution.py:305
  18.0 29.5 %all-to-all-start = ((bf16[16,16,256]{2,1,0:T(8,128)(2,1)}), bf16[16,16,256]{2,1,0:T(8,128)(2,1)S(1)}, u32[]{:S(2)}, u32[]{:S(2)}) async-start(bf16[16,16,256]{2,1,0:T(8,128)(2,1)} %bitcast.1), calls=%async_computation | async-start | bytes 262144 | tf_op jit(solution)/shard_map/all_to_all | solution.py:37
  48.2 19.4 %all-to-all-start.1 = ((bf16[16,16,256]{2,1,0:T(8,128)(2,1)}), bf16[16,16,256]{2,1,0:T(8,128)(2,1)S(1)}, u32[]{:S(2)}, u32[]{:S(2)}) async-start(bf16[16,16,256]{2,1,0:T(8,128)(2,1)} %broadcast_in_dim.104), calls=%async_computation.1 | async-start | bytes 262144 | tf_op jit(solution)/shard_map/all_to_all | solution.py:16
  54.4 18.5 %copy-start.12 = (bf16[1,3,1,128,2,1,128]{6,4,5,3,2,1,0:T(2,128)(2,1)S(1)}, bf16[1,3,1,128,2,1,128]{6,4,5,3,2,1,0:T(2,128)(2,1)}, u32[]{:S(2)}) copy-start(bf16[1,3,1,128,2,1,128]{6,4,5,3,2,1,0:T(2,128)(2,1)} %param.11) | copy-start | bytes 589828
  68.6 14.6 %all-to-all-start.2 = ((bf16[8,128,256]{2,1,0:T(8,128)(2,1)}), bf16[8,128,256]{2,1,0:T(8,128)(2,1)S(1)}, u32[]{:S(2)}, u32[]{:S(2)}) async-start(bf16[8,128,256]{2,1,0:T(8,128)(2,1)} %broadcast_in_dim.107), calls=%async_computation.2 | async-start | bytes 1048576 | tf_op jit(solution)/shard_map/all_to_all | solution.py:16
  104.6 6.6 %copy-start.9 = (bf16[1,6,1,128,256]{4,3,2,1,0:T(8,128)(2,1)S(1)}, bf16[1,6,1,128,256]{4,3,2,1,0:T(8,128)(2,1)}, u32[]{:S(2)}) copy-start(bf16[1,6,1,128,256]{4,3,2,1,0:T(8,128)(2,1)} %param.17) | copy-start | bytes 1179652
  105.3 20.0 %all-to-all-start.4 = ((bf16[16,16,256]{2,1,0:T(8,128)(2,1)}), bf16[16,16,256]{2,1,0:T(8,128)(2,1)S(1)}, u32[]{:S(2)}, u32[]{:S(2)}) async-start(bf16[16,16,256]{2,1,0:T(8,128)(2,1)} %broadcast_in_dim.108), calls=%async_computation.4 | async-start | bytes 262144 | tf_op jit(solution)/shard_map/all_to_all | solution.py:16
  126.3 13.8 %all-to-all-start.5 = ((bf16[8,128,256]{2,1,0:T(8,128)(2,1)}), bf16[8,128,256]{2,1,0:T(8,128)(2,1)S(1)}, u32[]{:S(2)}, u32[]{:S(2)}) async-start(bf16[8,128,256]{2,1,0:T(8,128)(2,1)} %broadcast_in_dim.109), calls=%async_computation.5 | async-start | bytes 1048576 | tf_op jit(solution)/shard_map/all_to_all | solution.py:16
  141.9 29.5 %all-to-all-start.6 = ((bf16[16,16,640]{2,1,0:T(8,128)(2,1)}), bf16[16,16,640]{2,1,0:T(8,128)(2,1)S(1)}, u32[]{:S(2)}, u32[]{:S(2)}) async-start(bf16[16,16,640]{2,1,0:T(8,128)(2,1)} %pad_maximum_fusion.3), calls=%async_computation.6 | async-start | bytes 655360 | tf_op jit(solution)/shard_map/all_to_all | solution.py:343
  171.4 0.7 copy-start
  180.0 8.1 %copy-start.3 = (f32[2,16,2048]{2,1,0:T(8,128)S(1)}, f32[2,16,2048]{2,1,0:T(8,128)}, u32[]{:S(2)}) copy-start(f32[2,16,2048]{2,1,0:T(8,128)} %shard_map.113) | copy-start | bytes 786436
  181.0 7.1 %collective-permute-start = (bf16[2,8,2048]{2,1,0:T(8,128)(2,1)S(1)}, bf16[2,8,2048]{2,1,0:T(8,128)(2,1)S(1)}, u32[]{:S(2)}, u32[]{:S(2)}) collective-permute-start(bf16[2,8,2048]{2,1,0:T(8,128)(2,1)S(1)} %select_convert_fusion), channel_id=1, source_target_pairs={{0,128},{128,0},{256,384},{384,256},{1,129},{129,1},{257,385},{385... | collective-permute-start | bytes 196616 | tf_op jit(solution)/shard_map/ppermute | solution.py:52
  184.5 14.4 %all-to-all-start.7 = ((bf16[16,8,2048]{2,1,0:T(8,128)(2,1)}), bf16[16,8,2048]{2,1,0:T(8,128)(2,1)S(1)}, u32[]{:S(2)}, u32[]{:S(2)}) async-start(bf16[16,8,2048]{2,1,0:T(8,128)(2,1)} %get-tuple-element.29), calls=%async_computation.7 | async-start | bytes 1048576 | tf_op jit(solution)/shard_map/all_to_all | solution.py:367
  198.9 0.8 copy-start.1
  204.3 10.9 %all-to-all-start.8 = ((bf16[8,8,2048]{2,1,0:T(8,128)(2,1)}), bf16[8,8,2048]{2,1,0:T(8,128)(2,1)S(1)}, u32[]{:S(2)}, u32[]{:S(2)}) async-start(bf16[8,8,2048]{2,1,0:T(8,128)(2,1)} %get-tuple-element.32), calls=%async_computation.8 | async-start | bytes 524288 | tf_op jit(solution)/shard_map/all_to_all | solution.py:209
  215.2 0.7 copy-start.4
  231.9 3.2 copy-start.14
  231.9 3.2 copy-start.17
  231.9 4.0 %copy-start.13 = (bf16[16,256]{1,0:T(8,128)(2,1)S(1)}, bf16[16,256]{1,0:T(8,128)(2,1)}, u32[]{:S(2)}) copy-start(bf16[16,256]{1,0:T(8,128)(2,1)} %get-tuple-element.30.solved) | copy-start | bytes 24580
  235.1 11.3 %copy-start.5 = (bf16[1,12,1,128,2,1,128]{6,4,5,3,2,1,0:T(2,128)(2,1)S(1)}, bf16[1,12,1,128,2,1,128]{6,4,5,3,2,1,0:T(2,128)(2,1)}, u32[]{:S(2)}) copy-start(bf16[1,12,1,128,2,1,128]{6,4,5,3,2,1,0:T(2,128)(2,1)} %param.12) | copy-start | bytes 2359300
  236.6 31.7 %all-to-all-start.10 = ((bf16[16,40,256]{2,1,0:T(8,128)(2,1)}), bf16[16,40,256]{2,1,0:T(8,128)(2,1)S(1)}, u32[]{:S(2)}, u32[]{:S(2)}) async-start(bf16[16,40,256]{2,1,0:T(8,128)(2,1)} %broadcast_in_dim.113), calls=%async_computation.10 | async-start | bytes 655360 | tf_op jit(solution)/shard_map/all_to_all | solution.py:16
  268.4 0.9 copy-start.6
  297.4 9.4 %all-to-all-start.12 = ((bf16[8,4,2048]{2,1,0:T(4,128)(2,1)}), bf16[8,4,2048]{2,1,0:T(4,128)(2,1)S(1)}, u32[]{:S(2)}, u32[]{:S(2)}) async-start(bf16[8,4,2048]{2,1,0:T(4,128)(2,1)} %broadcast_in_dim.121), calls=%async_computation.12 | async-start | bytes 262144 | tf_op jit(solution)/shard_map/all_to_all | solution.py:16
  306.8 0.7 copy-start.7
  311.8 9.4 %all-to-all-start.13 = ((bf16[8,4,2048]{2,1,0:T(4,128)(2,1)}), bf16[8,4,2048]{2,1,0:T(4,128)(2,1)S(1)}, u32[]{:S(2)}, u32[]{:S(2)}) async-start(bf16[8,4,2048]{2,1,0:T(4,128)(2,1)} %get-tuple-element.38), calls=%async_computation.13 | async-start | bytes 262144 | tf_op jit(solution)/shard_map/all_to_all | solution.py:209
  321.2 0.7 copy-start.8
  336.3 3.1 copy-start.15
  336.3 3.1 copy-start.18
  340.8 18.0 %all-to-all-start.15 = ((bf16[16,3,4,256]{3,2,1,0:T(4,128)(2,1)}), bf16[16,3,4,256]{3,2,1,0:T(4,128)(2,1)S(1)}, u32[]{:S(2)}, u32[]{:S(2)}) async-start(bf16[16,3,4,256]{3,2,1,0:T(4,128)(2,1)} %broadcast_in_dim.122), calls=%async_computation.15 | async-start | bytes 196608 | tf_op jit(solution)/shard_map/all_to_all | solution.py:16
  346.2 18.0 %collective-permute-start.1 = (bf16[16,24,256]{2,1,0:T(8,128)(2,1)S(1)}, bf16[16,24,256]{2,1,0:T(8,128)(2,1)S(1)}, u32[]{:S(2)}, u32[]{:S(2)}) collective-permute-start(bf16[16,24,256]{2,1,0:T(8,128)(2,1)S(1)} %get-tuple-element.66), channel_id=1, source_target_pairs={{0,128},{128,0},{256,384},{384,256},{1,129},{129,1},{257,385},{385... | collective-permute-start | bytes 589832 | tf_op jit(solution)/shard_map/ppermute | solution.py:52
  359.8 10.8 %all-to-all-start.16 = ((bf16[4,16,3,4,256]{4,3,1,2,0:T(4,128)(2,1)}), bf16[4,16,3,4,256]{4,3,1,2,0:T(4,128)(2,1)S(1)}, u32[]{:S(2)}, u32[]{:S(2)}) async-start(bf16[4,16,3,4,256]{4,3,1,2,0:T(4,128)(2,1)} %broadcast_in_dim.123), calls=%async_computation.16 | async-start | bytes 786432 | tf_op jit(solution)/shard_map/all_to_all | solution.py:16
Sparse Core Ops, SparseCore 0:
  17.0 151.1 all-gather.3
  170.8 98.7 all-gather.5

commit v7 on v5

--- a/solution.py
+++ b/solution.py
@@ -186,14 +186,14 @@
         ],
         axis=-1,
     )
-    received = lax.all_to_all(pieces, "prow", 0, 0).astype(jnp.float32)
-    last_own = jnp.sum(received[:, :, :col_width], axis=0).astype(jnp.bfloat16)
-    parts = received[:, :, col_width:].reshape(prows, wide, panels, tile_rows)
-    ancestors = [
-        parts[:, :, t].transpose(1, 0, 2)
-        - transposed_product(last_own, pair_all[:, t - panels])
-        for t in range(panels)
-    ]
+    received = lax.all_to_all(pieces, "prow", 0, 0)
+    last_own = jnp.sum(received[:, :, :col_width].astype(jnp.float32), axis=0).astype(jnp.bfloat16)
+    ancestors = []
+    for t in range(panels):
+        start = col_width + t * tile_rows
+        part = received[:, :, start : start + tile_rows].transpose(1, 0, 2)
+        product = transposed_product(last_own, pair_all[:, t - panels])
+        ancestors.append(part.astype(jnp.float32) - product)
 
     pcols = lax.axis_size("pcol")
     halves = ancestors[0].astype(jnp.bfloat16).reshape(2, 1, half, prows, tile_rows)

time: 359 us -> 359 us (level)
  transfers between devices with their start and end apart: 16 -> 16, of which waited for: 12 -> 12; matrix products, arithmetic and copies ran while one was open for 13% -> 12% of each run, Pallas kernels for 0% -> 0%
where the time goes in v7:
time: 359 us; the launch traced here: 356 us
  waiting for transfers between devices  131 us (36%)
  blocking collectives  74.8 us (21%)
  starting transfers between devices  73.3 us (20%)
  matrix products  30.2 us (8%)
  local copies, waits for them, and re-layouts  25.1 us (7%)
  between operations  14.7 us (4%)
  other arithmetic  6.69 us (2%)
    all_to_all x9, waiting for transfers between devices, shared_with_all(): return lax.all_to_all(copies, axis, 0, 0)  91.5 us
    all_to_all x9, starting transfers between devices, shared_with_all(): return lax.all_to_all(copies, axis, 0, 0)  43.1 us
    all_to_all x3, blocking collectives, shared_with_all(): return lax.all_to_all(copies, axis, 0, 0)  28.2 us
    all_to_all x1, blocking collectives, local(): received = lax.all_to_all(pieces, ('layer', 'prow'), 0, 0)  26.8 us
    all_to_all x1, waiting for transfers between devices, local(): received = lax.all_to_all(pieces, 'prow', 0, 0)  24.5 us
    all_to_all x1, blocking collectives, column_total(): received = lax.all_to_all(pieces, 'prow', 0, 0)  19.8 us
    dot_general x13, matrix products, transposed_product(): lax.dot_general(solved, blocks, (((solved.ndim - 1,), (blocks.ndim - 1,))...  16.3 us
    all_to_all x1, starting transfers between devices, column_total(): received = lax.all_to_all(pieces, 'prow', 0, 0)  15.2 us
  transfers between devices with their start and end apart: 16, of which 12 were waited for; matrix products, arithmetic and copies ran while one was open for 12% of the time, Pallas kernels for 0%

profile of v7, /device:TPU:32, one launch (start us, length us, event | category | flops | bytes accessed | tf_op | source)
XLA Modules:
  0.0 356.3 jit_solution(1652321818961741851)
XLA Ops:
  7.2 1.0 slice.194
  8.2 1.7 convolution_convert_fusion.2
  10.0 1.0 slice.210
  11.0 0.9 slice.212
  11.8 1.1 slice.215
  14.0 1.1 reshape.191
  15.1 0.9 pad_maximum_fusion
  16.1 15.2 %all-to-all-start = ((bf16[16,16,256]{2,1,0:T(8,128)(2,1)}), bf16[16,16,256]{2,1,0:T(8,128)(2,1)S(1)}, u32[]{:S(2)}, u32[]{:S(2)}) async-start(bf16[16,16,256]{2,1,0:T(8,128)(2,1)} %bitcast.1), calls=%async_computation | async-start | bytes 262144 | tf_op jit(solution)/shard_map/all_to_all | solution.py:30
  31.3 1.1 reshape.200
  32.4 1.1 reshape.201
  34.4 11.2 %all-to-all-done = bf16[16,16,256]{2,1,0:T(8,128)(2,1)S(1)} async-done(((bf16[16,16,256]{2,1,0:T(8,128)(2,1)}), bf16[16,16,256]{2,1,0:T(8,128)(2,1)S(1)}, u32[]{:S(2)}, u32[]{:S(2)}) %all-to-all-start) | async-done | bytes 131104 | tf_op jit(solution)/shard_map/all_to_all | solution.py:30
  46.3 4.3 %all-to-all-start.1 = ((bf16[16,16,256]{2,1,0:T(8,128)(2,1)}), bf16[16,16,256]{2,1,0:T(8,128)(2,1)S(1)}, u32[]{:S(2)}, u32[]{:S(2)}) async-start(bf16[16,16,256]{2,1,0:T(8,128)(2,1)} %broadcast_in_dim.139), calls=%async_computation.1 | async-start | bytes 262144 | tf_op jit(solution)/shard_map/all_to_all | solution.py:9
  50.6 1.2 broadcast_select_fusion
  51.9 13.6 %all-to-all-done.1 = bf16[16,16,256]{2,1,0:T(8,128)(2,1)S(1)} async-done(((bf16[16,16,256]{2,1,0:T(8,128)(2,1)}), bf16[16,16,256]{2,1,0:T(8,128)(2,1)S(1)}, u32[]{:S(2)}, u32[]{:S(2)}) %all-to-all-start.1) | async-done | bytes 131104 | tf_op jit(solution)/shard_map/all_to_all | solution.py:9
  66.6 4.3 %all-to-all-start.2 = ((bf16[8,128,256]{2,1,0:T(8,128)(2,1)}), bf16[8,128,256]{2,1,0:T(8,128)(2,1)S(1)}, u32[]{:S(2)}, u32[]{:S(2)}) async-start(bf16[8,128,256]{2,1,0:T(8,128)(2,1)} %broadcast_in_dim.142), calls=%async_computation.2 | async-start | bytes 1048576 | tf_op jit(solution)/shard_map/all_to_all | solution.py:9
  71.6 9.6 %all-to-all-done.2 = bf16[8,128,256]{2,1,0:T(8,128)(2,1)S(1)} async-done(((bf16[8,128,256]{2,1,0:T(8,128)(2,1)}), bf16[8,128,256]{2,1,0:T(8,128)(2,1)S(1)}, u32[]{:S(2)}, u32[]{:S(2)}) %all-to-all-start.2) | async-done | bytes 524320 | tf_op jit(solution)/shard_map/all_to_all | solution.py:9
  81.3 1.0 convolution_convert_fusion.1
  82.3 19.8 %all_to_all.85 = bf16[16,16,256]{2,1,0:T(8,128)(2,1)S(1)} all-to-all(bf16[16,16,256]{2,1,0:T(8,128)(2,1)S(1)} %bitcast.383), channel_id=1, replica_groups=mesh['layer'=4,'prow'=16,'pcol'=8] {'prow'}, dimensions={0} | all-to-all | bytes 262144 | tf_op jit(solution)/shard_map/all_to_all | solution.py:30
  102.9 5.1 %all-to-all-start.4 = ((bf16[16,16,256]{2,1,0:T(8,128)(2,1)}), bf16[16,16,256]{2,1,0:T(8,128)(2,1)S(1)}, u32[]{:S(2)}, u32[]{:S(2)}) async-start(bf16[16,16,256]{2,1,0:T(8,128)(2,1)} %broadcast_in_dim.143), calls=%async_computation.4 | async-start | bytes 262144 | tf_op jit(solution)/shard_map/all_to_all | solution.py:9
  108.9 1.2 copy.179
  110.6 12.4 %all-to-all-done.4 = bf16[16,16,256]{2,1,0:T(8,128)(2,1)S(1)} async-done(((bf16[16,16,256]{2,1,0:T(8,128)(2,1)}), bf16[16,16,256]{2,1,0:T(8,128)(2,1)S(1)}, u32[]{:S(2)}, u32[]{:S(2)}) %all-to-all-start.4) | async-done | bytes 131104 | tf_op jit(solution)/shard_map/all_to_all | solution.py:9
  124.0 3.5 all-to-all-start.5
  128.5 9.2 %all-to-all-done.5 = bf16[8,128,256]{2,1,0:T(8,128)(2,1)S(1)} async-done(((bf16[8,128,256]{2,1,0:T(8,128)(2,1)}), bf16[8,128,256]{2,1,0:T(8,128)(2,1)S(1)}, u32[]{:S(2)}, u32[]{:S(2)}) %all-to-all-start.5) | async-done | bytes 524320 | tf_op jit(solution)/shard_map/all_to_all | solution.py:9
  137.9 1.1 convolution_convert_fusion
  139.7 5.0 %all-to-all-start.6 = ((bf16[16,16,640]{2,1,0:T(8,128)(2,1)}), bf16[16,16,640]{2,1,0:T(8,128)(2,1)S(1)}, u32[]{:S(2)}, u32[]{:S(2)}) async-start(bf16[16,16,640]{2,1,0:T(8,128)(2,1)} %pad_maximum_fusion.3), calls=%async_computation.6 | async-start | bytes 655360 | tf_op jit(solution)/shard_map/all_to_all | solution.py:189
  144.7 24.5 %all-to-all-done.6 = bf16[16,16,640]{2,1,0:T(8,128)(2,1)S(1)} async-done(((bf16[16,16,640]{2,1,0:T(8,128)(2,1)}), bf16[16,16,640]{2,1,0:T(8,128)(2,1)S(1)}, u32[]{:S(2)}, u32[]{:S(2)}) %all-to-all-start.6) | async-done | bytes 327712 | tf_op jit(solution)/shard_map/all_to_all | solution.py:189
  169.2 1.6 fusion.5
  170.8 0.9 broadcast_in_dim.151
  171.8 3.6 %all-to-all-start.7 = ((bf16[16,8,16,128]{3,2,1,0:T(8,128)(2,1)}), bf16[16,8,16,128]{3,2,1,0:T(8,128)(2,1)S(1)}, u32[]{:S(2)}, u32[]{:S(2)}) async-start(bf16[16,8,16,128]{3,2,1,0:T(8,128)(2,1)} %bitcast.28), calls=%async_computation.7 | async-start | bytes 1048576 | tf_op jit(solution)/shard_map/all_to_all | solution.py:205
  175.3 1.6 fusion.2
  176.9 1.6 fusion.1
  178.6 3.8 %collective-permute-start = (bf16[2,8,16,128]{3,1,2,0:T(8,128)(2,1)S(1)}, bf16[2,8,16,128]{3,1,2,0:T(8,128)(2,1)S(1)}, u32[]{:S(2)}, u32[]{:S(2)}) collective-permute-start(bf16[2,8,16,128]{3,1,2,0:T(8,128)(2,1)S(1)} %select_convert_fusion), channel_id=1, source_target_pairs={{0,128},{128,0},{256,384},{384,256},{1,129},{129,1},{257,385},{385... | collective-permute-start | bytes 196616 | tf_op jit(solution)/shard_map/ppermute | solution.py:45
  182.4 4.2 %collective-permute-done = bf16[2,8,16,128]{3,1,2,0:T(8,128)(2,1)S(1)} collective-permute-done((bf16[2,8,16,128]{3,1,2,0:T(8,128)(2,1)S(1)}, bf16[2,8,16,128]{3,1,2,0:T(8,128)(2,1)S(1)}, u32[]{:S(2)}, u32[]{:S(2)}) %collective-permute-start) | collective-permute-done | bytes 65568 | tf_op jit(solution)/shard_map/ppermute | solution.py:45
  186.7 1.5 fusion.8
  188.3 1.6 fusion.47
  190.7 3.4 all-to-all-start.8
  194.1 1.6 fusion.17
  195.7 5.8 %all-to-all-done.8 = bf16[8,8,16,128]{3,2,1,0:T(8,128)(2,1)S(1)} async-done(((bf16[8,8,16,128]{3,2,1,0:T(8,128)(2,1)}), bf16[8,8,16,128]{3,2,1,0:T(8,128)(2,1)S(1)}, u32[]{:S(2)}, u32[]{:S(2)}) %all-to-all-start.8) | async-done | bytes 262176 | tf_op jit(solution)/shard_map/all_to_all | solution.py:9
  202.2 1.5 fusion.9
  203.7 1.6 fusion.45
  205.4 9.9 %all_to_all.86 = bf16[8,8,16,128]{3,2,1,0:T(8,128)(2,1)S(1)} all-to-all(bf16[8,8,16,128]{3,2,1,0:T(8,128)(2,1)S(1)} %broadcast_in_dim.153), channel_id=1, replica_groups=mesh['layer'=4,'prow'=16,'pcol'=8] {'pcol'}, dimensions={0} | all-to-all | bytes 524288 | tf_op jit(solution)/shard_map/all_to_all | solution.py:9
  215.4 1.5 fusion.11
  217.6 9.5 %all-to-all-start.10 = ((bf16[16,40,256]{2,1,0:T(8,128)(2,1)}), bf16[16,40,256]{2,1,0:T(8,128)(2,1)S(1)}, u32[]{:S(2)}, u32[]{:S(2)}) async-start(bf16[16,40,256]{2,1,0:T(8,128)(2,1)} %broadcast_in_dim.154), calls=%async_computation.10 | async-start | bytes 655360 | tf_op jit(solution)/shard_map/all_to_all | solution.py:9
  227.9 1.7 slice.233
  230.7 20.7 %all-to-all-done.10 = bf16[16,40,256]{2,1,0:T(8,128)(2,1)S(1)} async-done(((bf16[16,40,256]{2,1,0:T(8,128)(2,1)}), bf16[16,40,256]{2,1,0:T(8,128)(2,1)S(1)}, u32[]{:S(2)}, u32[]{:S(2)}) %all-to-all-start.10) | async-done | bytes 327712 | tf_op jit(solution)/shard_map/all_to_all | solution.py:9
  252.2 1.2 convolution_subtract_fusion.2
  253.8 26.8 %all_to_all.87 = bf16[64,4,3,128]{3,1,2,0:T(4,128)(2,1)S(1)} all-to-all(bf16[64,4,3,128]{3,1,2,0:T(4,128)(2,1)S(1)} %copy.208), channel_id=1, replica_groups=mesh['layer'=4,'prow'=16,'pcol'=8] {'layer','prow'}, dimensions={0} | all-to-all | bytes 393216 | tf_op jit(solution)/shard_map/all_to_all | solution.py:238
  280.7 9.8 %all_to_all.88 = bf16[8,4,16,128]{3,2,1,0:T(8,128)(2,1)S(1)} all-to-all(bf16[8,4,16,128]{3,2,1,0:T(8,128)(2,1)S(1)} %broadcast_in_dim.162), channel_id=1, replica_groups=mesh['layer'=4,'prow'=16,'pcol'=8] {'pcol'}, dimensions={0} | all-to-all | bytes 262144 | tf_op jit(solution)/shard_map/all_to_all | solution.py:9
  290.5 1.5 fusion.12
  292.0 1.6 fusion.6
  294.3 3.4 all-to-all-start.13
  297.7 1.6 convolution_subtract_fusion.7
  299.3 4.5 %all-to-all-done.13 = bf16[8,4,16,128]{3,2,1,0:T(8,128)(2,1)S(1)} async-done(((bf16[8,4,16,128]{3,2,1,0:T(8,128)(2,1)}), bf16[8,4,16,128]{3,2,1,0:T(8,128)(2,1)S(1)}, u32[]{:S(2)}, u32[]{:S(2)}) %all-to-all-start.13) | async-done | bytes 131104 | tf_op jit(solution)/shard_map/all_to_all | solution.py:9
  303.8 1.5 fusion.13
  305.3 1.6 fusion.7
  306.9 8.5 %all_to_all.89 = bf16[8,4,16,128]{3,2,1,0:T(8,128)(2,1)S(1)} all-to-all(bf16[8,4,16,128]{3,2,1,0:T(8,128)(2,1)S(1)} %broadcast_in_dim.164), channel_id=1, replica_groups=mesh['layer'=4,'prow'=16,'pcol'=8] {'pcol'}, dimensions={0} | all-to-all | bytes 262144 | tf_op jit(solution)/shard_map/all_to_all | solution.py:9
  315.5 1.5 fusion.15
  317.6 5.8 %all-to-all-start.15 = ((bf16[16,3,4,256]{3,2,1,0:T(4,128)(2,1)}), bf16[16,3,4,256]{3,2,1,0:T(4,128)(2,1)S(1)}, u32[]{:S(2)}, u32[]{:S(2)}) async-start(bf16[16,3,4,256]{3,2,1,0:T(4,128)(2,1)} %broadcast_in_dim.165), calls=%async_computation.15 | async-start | bytes 196608 | tf_op jit(solution)/shard_map/all_to_all | solution.py:9
  323.5 2.5 collective-permute-start.1
  326.0 10.1 %all-to-all-done.15 = bf16[16,3,4,256]{3,2,1,0:T(4,128)(2,1)S(1)} async-done(((bf16[16,3,4,256]{3,2,1,0:T(4,128)(2,1)}), bf16[16,3,4,256]{3,2,1,0:T(4,128)(2,1)S(1)}, u32[]{:S(2)}, u32[]{:S(2)}) %all-to-all-start.15) | async-done | bytes 98336 | tf_op jit(solution)/shard_map/all_to_all | solution.py:9
  337.1 3.8 %all-to-all-start.16 = ((bf16[4,16,3,4,256]{4,3,1,2,0:T(4,128)(2,1)}), bf16[4,16,3,4,256]{4,3,1,2,0:T(4,128)(2,1)S(1)}, u32[]{:S(2)}, u32[]{:S(2)}) async-start(bf16[4,16,3,4,256]{4,3,1,2,0:T(4,128)(2,1)} %broadcast_in_dim.166), calls=%async_computation.16 | async-start | bytes 786432 | tf_op jit(solution)/shard_map/all_to_all | solution.py:9
  341.9 0.9 copy.234
  342.8 5.5 %all-to-all-done.16 = bf16[4,16,3,4,256]{4,3,1,2,0:T(4,128)(2,1)S(1)} async-done(((bf16[4,16,3,4,256]{4,3,1,2,0:T(4,128)(2,1)}), bf16[4,16,3,4,256]{4,3,1,2,0:T(4,128)(2,1)S(1)}, u32[]{:S(2)}, u32[]{:S(2)}) %all-to-all-start.16) | async-done | bytes 393248 | tf_op jit(solution)/shard_map/all_to_all | solution.py:9
  348.5 0.9 copy.235
  (105 shorter events, 18.8 us)
Async XLA Ops:
  7.2 63.7 %copy-start.3 = (bf16[1,3,1,128,2,1,128]{6,4,5,3,2,1,0:T(2,128)(2,1)S(1)}, bf16[1,3,1,128,2,1,128]{6,4,5,3,2,1,0:T(2,128)(2,1)}, u32[]{:S(2)}) copy-start(bf16[1,3,1,128,2,1,128]{6,4,5,3,2,1,0:T(2,128)(2,1)} %param.11) | copy-start | bytes 589828
  7.2 27.1 %copy-start.4 = (s32[1,21,1,2,1]{1,4,3,2,0:T(1,128)S(1)}, s32[1,21,1,2,1]{1,4,3,2,0:T(1,128)}, u32[]{:S(2)}) copy-start(s32[1,21,1,2,1]{1,4,3,2,0:T(1,128)} %param.10) | copy-start | bytes 508
  7.2 43.4 %copy-start = (bf16[1,21,1,128,2,1,128]{6,4,5,3,2,1,0:T(2,128)(2,1)S(1)}, bf16[1,21,1,128,2,1,128]{6,4,5,3,2,1,0:T(2,128)(2,1)}, u32[]{:S(2)}) copy-start(bf16[1,21,1,128,2,1,128]{6,4,5,3,2,1,0:T(2,128)(2,1)} %param.9) | copy-start | bytes 4128772
  7.2 162.0 %all-gather.5.cloned.1.call-start = ((), (), s32[]{:S(2)}) async-start(), calls=%async_computation.17 | async-start | bytes 10027008 | tf_op jit(solution)/shard_map/all_gather | solution.py:148
  16.1 29.5 %all-to-all-start = ((bf16[16,16,256]{2,1,0:T(8,128)(2,1)}), bf16[16,16,256]{2,1,0:T(8,128)(2,1)S(1)}, u32[]{:S(2)}, u32[]{:S(2)}) async-start(bf16[16,16,256]{2,1,0:T(8,128)(2,1)} %bitcast.1), calls=%async_computation | async-start | bytes 262144 | tf_op jit(solution)/shard_map/all_to_all | solution.py:30
  31.3 259.2 %all-gather.7.cloned.1.call-start = ((), (), s32[]{:S(2)}) async-start(), calls=%async_computation.18 | async-start | bytes 6684672 | tf_op jit(solution)/shard_map/all_gather | solution.py:151
  46.3 19.3 %all-to-all-start.1 = ((bf16[16,16,256]{2,1,0:T(8,128)(2,1)}), bf16[16,16,256]{2,1,0:T(8,128)(2,1)S(1)}, u32[]{:S(2)}, u32[]{:S(2)}) async-start(bf16[16,16,256]{2,1,0:T(8,128)(2,1)} %broadcast_in_dim.139), calls=%async_computation.1 | async-start | bytes 262144 | tf_op jit(solution)/shard_map/all_to_all | solution.py:9
  66.6 14.6 %all-to-all-start.2 = ((bf16[8,128,256]{2,1,0:T(8,128)(2,1)}), bf16[8,128,256]{2,1,0:T(8,128)(2,1)S(1)}, u32[]{:S(2)}, u32[]{:S(2)}) async-start(bf16[8,128,256]{2,1,0:T(8,128)(2,1)} %broadcast_in_dim.142), calls=%async_computation.2 | async-start | bytes 1048576 | tf_op jit(solution)/shard_map/all_to_all | solution.py:9
  102.9 20.1 %all-to-all-start.4 = ((bf16[16,16,256]{2,1,0:T(8,128)(2,1)}), bf16[16,16,256]{2,1,0:T(8,128)(2,1)S(1)}, u32[]{:S(2)}, u32[]{:S(2)}) async-start(bf16[16,16,256]{2,1,0:T(8,128)(2,1)} %broadcast_in_dim.143), calls=%async_computation.4 | async-start | bytes 262144 | tf_op jit(solution)/shard_map/all_to_all | solution.py:9
  124.0 13.8 %all-to-all-start.5 = ((bf16[8,128,256]{2,1,0:T(8,128)(2,1)}), bf16[8,128,256]{2,1,0:T(8,128)(2,1)S(1)}, u32[]{:S(2)}, u32[]{:S(2)}) async-start(bf16[8,128,256]{2,1,0:T(8,128)(2,1)} %broadcast_in_dim.144), calls=%async_computation.5 | async-start | bytes 1048576 | tf_op jit(solution)/shard_map/all_to_all | solution.py:9
  139.7 29.4 %all-to-all-start.6 = ((bf16[16,16,640]{2,1,0:T(8,128)(2,1)}), bf16[16,16,640]{2,1,0:T(8,128)(2,1)S(1)}, u32[]{:S(2)}, u32[]{:S(2)}) async-start(bf16[16,16,640]{2,1,0:T(8,128)(2,1)} %pad_maximum_fusion.3), calls=%async_computation.6 | async-start | bytes 655360 | tf_op jit(solution)/shard_map/all_to_all | solution.py:189
  171.8 14.9 %all-to-all-start.7 = ((bf16[16,8,16,128]{3,2,1,0:T(8,128)(2,1)}), bf16[16,8,16,128]{3,2,1,0:T(8,128)(2,1)S(1)}, u32[]{:S(2)}, u32[]{:S(2)}) async-start(bf16[16,8,16,128]{3,2,1,0:T(8,128)(2,1)} %bitcast.28), calls=%async_computation.7 | async-start | bytes 1048576 | tf_op jit(solution)/shard_map/all_to_all | solution.py:205
  178.6 8.0 %collective-permute-start = (bf16[2,8,16,128]{3,1,2,0:T(8,128)(2,1)S(1)}, bf16[2,8,16,128]{3,1,2,0:T(8,128)(2,1)S(1)}, u32[]{:S(2)}, u32[]{:S(2)}) collective-permute-start(bf16[2,8,16,128]{3,1,2,0:T(8,128)(2,1)S(1)} %select_convert_fusion), channel_id=1, source_target_pairs={{0,128},{128,0},{256,384},{384,256},{1,129},{129,1},{257,385},{385... | collective-permute-start | bytes 196616 | tf_op jit(solution)/shard_map/ppermute | solution.py:45
  186.6 4.1 %copy-start.2 = (f32[2,8,16,128]{3,1,2,0:T(8,128)}, f32[2,8,16,128]{3,1,2,0:T(8,128)S(1)}, u32[]{:S(2)}) copy-start(f32[2,8,16,128]{3,1,2,0:T(8,128)S(1)} %convert_add_fusion) | copy-start | bytes 393220
  186.7 43.0 %copy-start.1 = (bf16[1,12,1,128,2,1,128]{6,4,5,3,2,1,0:T(2,128)(2,1)S(1)}, bf16[1,12,1,128,2,1,128]{6,4,5,3,2,1,0:T(2,128)(2,1)}, u32[]{:S(2)}) copy-start(bf16[1,12,1,128,2,1,128]{6,4,5,3,2,1,0:T(2,128)(2,1)} %param.12) | copy-start | bytes 2359300
  190.7 10.9 %all-to-all-start.8 = ((bf16[8,8,16,128]{3,2,1,0:T(8,128)(2,1)}), bf16[8,8,16,128]{3,2,1,0:T(8,128)(2,1)S(1)}, u32[]{:S(2)}, u32[]{:S(2)}) async-start(bf16[8,8,16,128]{3,2,1,0:T(8,128)(2,1)} %broadcast_in_dim.152), calls=%async_computation.8 | async-start | bytes 524288 | tf_op jit(solution)/shard_map/all_to_all | solution.py:9
  217.6 33.7 %all-to-all-start.10 = ((bf16[16,40,256]{2,1,0:T(8,128)(2,1)}), bf16[16,40,256]{2,1,0:T(8,128)(2,1)S(1)}, u32[]{:S(2)}, u32[]{:S(2)}) async-start(bf16[16,40,256]{2,1,0:T(8,128)(2,1)} %broadcast_in_dim.154), calls=%async_computation.10 | async-start | bytes 655360 | tf_op jit(solution)/shard_map/all_to_all | solution.py:9
  294.3 9.4 %all-to-all-start.13 = ((bf16[8,4,16,128]{3,2,1,0:T(8,128)(2,1)}), bf16[8,4,16,128]{3,2,1,0:T(8,128)(2,1)S(1)}, u32[]{:S(2)}, u32[]{:S(2)}) async-start(bf16[8,4,16,128]{3,2,1,0:T(8,128)(2,1)} %broadcast_in_dim.163), calls=%async_computation.13 | async-start | bytes 262144 | tf_op jit(solution)/shard_map/all_to_all | solution.py:9
  317.6 18.5 %all-to-all-start.15 = ((bf16[16,3,4,256]{3,2,1,0:T(4,128)(2,1)}), bf16[16,3,4,256]{3,2,1,0:T(4,128)(2,1)S(1)}, u32[]{:S(2)}, u32[]{:S(2)}) async-start(bf16[16,3,4,256]{3,2,1,0:T(4,128)(2,1)} %broadcast_in_dim.165), calls=%async_computation.15 | async-start | bytes 196608 | tf_op jit(solution)/shard_map/all_to_all | solution.py:9
  323.5 18.3 %collective-permute-start.1 = (bf16[16,24,256]{2,1,0:T(8,128)(2,1)S(1)}, bf16[16,24,256]{2,1,0:T(8,128)(2,1)S(1)}, u32[]{:S(2)}, u32[]{:S(2)}) collective-permute-start(bf16[16,24,256]{2,1,0:T(8,128)(2,1)S(1)} %get-tuple-element.46), channel_id=1, source_target_pairs={{0,128},{128,0},{256,384},{384,256},{1,129},{129,1},{257,385},{385... | collective-permute-start | bytes 589832 | tf_op jit(solution)/shard_map/ppermute | solution.py:45
  337.1 11.2 %all-to-all-start.16 = ((bf16[4,16,3,4,256]{4,3,1,2,0:T(4,128)(2,1)}), bf16[4,16,3,4,256]{4,3,1,2,0:T(4,128)(2,1)S(1)}, u32[]{:S(2)}, u32[]{:S(2)}) async-start(bf16[4,16,3,4,256]{4,3,1,2,0:T(4,128)(2,1)} %broadcast_in_dim.166), calls=%async_computation.16 | async-start | bytes 786432 | tf_op jit(solution)/shard_map/all_to_all | solution.py:9
Sparse Core Ops, SparseCore 0:
  16.2 150.4 all-gather.4
  169.4 103.9 all-gather.6

commit v8 on v7

--- a/solution.py
+++ b/solution.py
@@ -234,10 +234,11 @@
     is_mine = jnp.arange(2).reshape(1, 2, 1, 1, 1) == second
     left = left.reshape(prows, 2, half, panels, tile_rows) - jnp.where(is_mine, taken, 0.0)
     pieces = left.astype(jnp.bfloat16).reshape(prows, layers, narrow, panels, tile_rows)
-    pieces = pieces.transpose(1, 0, 2, 3, 4).reshape(layers * prows, narrow, panels, tile_rows)
-    received = lax.all_to_all(pieces, ("layer", "prow"), 0, 0)
-    received = received.reshape(layers, prows, narrow, panels, tile_rows)
-    sums = jnp.sum(received.astype(jnp.float32), axis=0).transpose(1, 0, 2, 3)
+    pieces = pieces.transpose(1, 0, 2, 3, 4)
+    by_source = lax.all_to_all(pieces, "layer", 0, 0)
+    pieces = jnp.sum(by_source.astype(jnp.float32), axis=0).astype(jnp.bfloat16)
+    received = lax.all_to_all(pieces, "prow", 0, 0)
+    sums = received.astype(jnp.float32).transpose(1, 0, 2, 3)
     sums = [sums[:, :, t] for t in range(panels)]
     root_solved = slice_solve(row_total(sums[0]), sums[1:], root_all, panels)
     by_layer = shared_with_all(shared_with_all(root_solved, "prow"), "layer")

time: 359 us -> 357 us (level)
    all_to_all x1 -> x2, blocking collectives: 26.8 us -> 28 us  [the longest x1 17.6 us: local(): received = lax.all_to_all(pieces, 'prow', 0, 0)]
where the time goes in v8:
time: 357 us; the launch traced here: 355 us
  waiting for transfers between devices  132 us (37%)
  blocking collectives  74.8 us (21%)
  starting transfers between devices  71.4 us (20%)
  matrix products  30.2 us (8%)
  local copies, waits for them, and re-layouts  25 us (7%)
  between operations  14.7 us (4%)
  other arithmetic  6.74 us (2%)
    all_to_all x9, waiting for transfers between devices, shared_with_all(): return lax.all_to_all(copies, axis, 0, 0)  92.2 us
    all_to_all x9, starting transfers between devices, shared_with_all(): return lax.all_to_all(copies, axis, 0, 0)  41.5 us
    all_to_all x3, blocking collectives, shared_with_all(): return lax.all_to_all(copies, axis, 0, 0)  27 us
    all_to_all x1, waiting for transfers between devices, local(): received = lax.all_to_all(pieces, 'prow', 0, 0)  24.5 us
    all_to_all x1, blocking collectives, column_total(): received = lax.all_to_all(pieces, 'prow', 0, 0)  19.8 us
    all_to_all x1, blocking collectives, local(): received = lax.all_to_all(pieces, 'prow', 0, 0)  17.6 us
    dot_general x13, matrix products, transposed_product(): lax.dot_general(solved, blocks, (((solved.ndim - 1,), (blocks.ndim - 1,))...  16.3 us
    all_to_all x1, starting transfers between devices, column_total(): received = lax.all_to_all(pieces, 'prow', 0, 0)  15.2 us
  transfers between devices with their start and end apart: 16, of which 12 were waited for; matrix products, arithmetic and copies ran while one was open for 12% of the time, Pallas kernels for 0%

profile of v8, /device:TPU:32, one launch (start us, length us, event | category | flops | bytes accessed | tf_op | source)
XLA Modules:
  0.0 355.1 jit_solution(7841649180956720994)
XLA Ops:
  7.2 1.0 slice.194
  8.2 1.7 convolution_convert_fusion.2
  10.0 1.0 slice.210
  11.8 1.1 slice.215
  14.0 1.1 reshape.185
  15.1 0.9 pad_maximum_fusion
  16.1 15.2 %all-to-all-start = ((bf16[16,16,256]{2,1,0:T(8,128)(2,1)}), bf16[16,16,256]{2,1,0:T(8,128)(2,1)S(1)}, u32[]{:S(2)}, u32[]{:S(2)}) async-start(bf16[16,16,256]{2,1,0:T(8,128)(2,1)} %bitcast.1), calls=%async_computation | async-start | bytes 262144 | tf_op jit(solution)/shard_map/all_to_all | solution.py:30
  31.4 1.1 reshape.193
  32.4 1.1 reshape.194
  34.4 11.2 %all-to-all-done = bf16[16,16,256]{2,1,0:T(8,128)(2,1)S(1)} async-done(((bf16[16,16,256]{2,1,0:T(8,128)(2,1)}), bf16[16,16,256]{2,1,0:T(8,128)(2,1)S(1)}, u32[]{:S(2)}, u32[]{:S(2)}) %all-to-all-start) | async-done | bytes 131104 | tf_op jit(solution)/shard_map/all_to_all | solution.py:30
  46.3 4.3 %all-to-all-start.1 = ((bf16[16,16,256]{2,1,0:T(8,128)(2,1)}), bf16[16,16,256]{2,1,0:T(8,128)(2,1)S(1)}, u32[]{:S(2)}, u32[]{:S(2)}) async-start(bf16[16,16,256]{2,1,0:T(8,128)(2,1)} %broadcast_in_dim.139), calls=%async_computation.1 | async-start | bytes 262144 | tf_op jit(solution)/shard_map/all_to_all | solution.py:9
  50.6 1.2 broadcast_select_fusion
  51.9 13.6 %all-to-all-done.1 = bf16[16,16,256]{2,1,0:T(8,128)(2,1)S(1)} async-done(((bf16[16,16,256]{2,1,0:T(8,128)(2,1)}), bf16[16,16,256]{2,1,0:T(8,128)(2,1)S(1)}, u32[]{:S(2)}, u32[]{:S(2)}) %all-to-all-start.1) | async-done | bytes 131104 | tf_op jit(solution)/shard_map/all_to_all | solution.py:9
  66.6 4.3 %all-to-all-start.2 = ((bf16[8,128,256]{2,1,0:T(8,128)(2,1)}), bf16[8,128,256]{2,1,0:T(8,128)(2,1)S(1)}, u32[]{:S(2)}, u32[]{:S(2)}) async-start(bf16[8,128,256]{2,1,0:T(8,128)(2,1)} %broadcast_in_dim.142), calls=%async_computation.2 | async-start | bytes 1048576 | tf_op jit(solution)/shard_map/all_to_all | solution.py:9
  71.6 9.6 %all-to-all-done.2 = bf16[8,128,256]{2,1,0:T(8,128)(2,1)S(1)} async-done(((bf16[8,128,256]{2,1,0:T(8,128)(2,1)}), bf16[8,128,256]{2,1,0:T(8,128)(2,1)S(1)}, u32[]{:S(2)}, u32[]{:S(2)}) %all-to-all-start.2) | async-done | bytes 524320 | tf_op jit(solution)/shard_map/all_to_all | solution.py:9
  81.3 1.1 convolution_convert_fusion.1
  82.4 19.8 %all_to_all.90 = bf16[16,16,256]{2,1,0:T(8,128)(2,1)S(1)} all-to-all(bf16[16,16,256]{2,1,0:T(8,128)(2,1)S(1)} %bitcast.379), channel_id=1, replica_groups=mesh['layer'=4,'prow'=16,'pcol'=8] {'prow'}, dimensions={0} | all-to-all | bytes 262144 | tf_op jit(solution)/shard_map/all_to_all | solution.py:30
  102.9 5.1 %all-to-all-start.4 = ((bf16[16,16,256]{2,1,0:T(8,128)(2,1)}), bf16[16,16,256]{2,1,0:T(8,128)(2,1)S(1)}, u32[]{:S(2)}, u32[]{:S(2)}) async-start(bf16[16,16,256]{2,1,0:T(8,128)(2,1)} %broadcast_in_dim.143), calls=%async_computation.4 | async-start | bytes 262144 | tf_op jit(solution)/shard_map/all_to_all | solution.py:9
  108.9 1.2 copy.211
  110.6 12.5 %all-to-all-done.4 = bf16[16,16,256]{2,1,0:T(8,128)(2,1)S(1)} async-done(((bf16[16,16,256]{2,1,0:T(8,128)(2,1)}), bf16[16,16,256]{2,1,0:T(8,128)(2,1)S(1)}, u32[]{:S(2)}, u32[]{:S(2)}) %all-to-all-start.4) | async-done | bytes 131104 | tf_op jit(solution)/shard_map/all_to_all | solution.py:9
  124.0 3.5 all-to-all-start.5
  128.6 9.2 %all-to-all-done.5 = bf16[8,128,256]{2,1,0:T(8,128)(2,1)S(1)} async-done(((bf16[8,128,256]{2,1,0:T(8,128)(2,1)}), bf16[8,128,256]{2,1,0:T(8,128)(2,1)S(1)}, u32[]{:S(2)}, u32[]{:S(2)}) %all-to-all-start.5) | async-done | bytes 524320 | tf_op jit(solution)/shard_map/all_to_all | solution.py:9
  137.9 1.1 convolution_convert_fusion
  139.7 4.9 %all-to-all-start.6 = ((bf16[16,16,640]{2,1,0:T(8,128)(2,1)}), bf16[16,16,640]{2,1,0:T(8,128)(2,1)S(1)}, u32[]{:S(2)}, u32[]{:S(2)}) async-start(bf16[16,16,640]{2,1,0:T(8,128)(2,1)} %pad_maximum_fusion.3), calls=%async_computation.6 | async-start | bytes 655360 | tf_op jit(solution)/shard_map/all_to_all | solution.py:189
  144.7 24.5 %all-to-all-done.6 = bf16[16,16,640]{2,1,0:T(8,128)(2,1)S(1)} async-done(((bf16[16,16,640]{2,1,0:T(8,128)(2,1)}), bf16[16,16,640]{2,1,0:T(8,128)(2,1)S(1)}, u32[]{:S(2)}, u32[]{:S(2)}) %all-to-all-start.6) | async-done | bytes 327712 | tf_op jit(solution)/shard_map/all_to_all | solution.py:189
  169.2 1.6 fusion.5
  170.9 0.9 broadcast_in_dim.151
  171.8 3.6 %all-to-all-start.7 = ((bf16[16,8,16,128]{3,2,1,0:T(8,128)(2,1)}), bf16[16,8,16,128]{3,2,1,0:T(8,128)(2,1)S(1)}, u32[]{:S(2)}, u32[]{:S(2)}) async-start(bf16[16,8,16,128]{3,2,1,0:T(8,128)(2,1)} %bitcast.28), calls=%async_computation.7 | async-start | bytes 1048576 | tf_op jit(solution)/shard_map/all_to_all | solution.py:205
  175.3 1.6 fusion.2
  177.0 1.6 fusion.1
  178.6 3.8 %collective-permute-start = (bf16[2,8,16,128]{3,1,2,0:T(8,128)(2,1)S(1)}, bf16[2,8,16,128]{3,1,2,0:T(8,128)(2,1)S(1)}, u32[]{:S(2)}, u32[]{:S(2)}) collective-permute-start(bf16[2,8,16,128]{3,1,2,0:T(8,128)(2,1)S(1)} %select_convert_fusion), channel_id=1, source_target_pairs={{0,128},{128,0},{256,384},{384,256},{1,129},{129,1},{257,385},{385... | collective-permute-start | bytes 196616 | tf_op jit(solution)/shard_map/ppermute | solution.py:45
  182.4 4.2 %collective-permute-done = bf16[2,8,16,128]{3,1,2,0:T(8,128)(2,1)S(1)} collective-permute-done((bf16[2,8,16,128]{3,1,2,0:T(8,128)(2,1)S(1)}, bf16[2,8,16,128]{3,1,2,0:T(8,128)(2,1)S(1)}, u32[]{:S(2)}, u32[]{:S(2)}) %collective-permute-start) | collective-permute-done | bytes 65568 | tf_op jit(solution)/shard_map/ppermute | solution.py:45
  186.7 1.5 fusion.8
  188.3 1.6 fusion.47
  190.7 3.4 all-to-all-start.8
  194.1 1.6 fusion.17
  195.7 5.8 %all-to-all-done.8 = bf16[8,8,16,128]{3,2,1,0:T(8,128)(2,1)S(1)} async-done(((bf16[8,8,16,128]{3,2,1,0:T(8,128)(2,1)}), bf16[8,8,16,128]{3,2,1,0:T(8,128)(2,1)S(1)}, u32[]{:S(2)}, u32[]{:S(2)}) %all-to-all-start.8) | async-done | bytes 262176 | tf_op jit(solution)/shard_map/all_to_all | solution.py:9
  202.2 1.5 fusion.9
  203.7 1.6 fusion.45
  205.4 9.9 %all_to_all.91 = bf16[8,8,16,128]{3,2,1,0:T(8,128)(2,1)S(1)} all-to-all(bf16[8,8,16,128]{3,2,1,0:T(8,128)(2,1)S(1)} %broadcast_in_dim.153), channel_id=1, replica_groups=mesh['layer'=4,'prow'=16,'pcol'=8] {'pcol'}, dimensions={0} | all-to-all | bytes 524288 | tf_op jit(solution)/shard_map/all_to_all | solution.py:9
  215.4 1.5 fusion.11
  217.6 9.5 %all-to-all-start.10 = ((bf16[16,40,256]{2,1,0:T(8,128)(2,1)}), bf16[16,40,256]{2,1,0:T(8,128)(2,1)S(1)}, u32[]{:S(2)}, u32[]{:S(2)}) async-start(bf16[16,40,256]{2,1,0:T(8,128)(2,1)} %broadcast_in_dim.154), calls=%async_computation.10 | async-start | bytes 655360 | tf_op jit(solution)/shard_map/all_to_all | solution.py:9
  227.9 1.7 slice.233
  230.7 20.7 %all-to-all-done.10 = bf16[16,40,256]{2,1,0:T(8,128)(2,1)S(1)} async-done(((bf16[16,40,256]{2,1,0:T(8,128)(2,1)}), bf16[16,40,256]{2,1,0:T(8,128)(2,1)S(1)}, u32[]{:S(2)}, u32[]{:S(2)}) %all-to-all-start.10) | async-done | bytes 327712 | tf_op jit(solution)/shard_map/all_to_all | solution.py:9
  252.2 1.2 convolution_subtract_fusion.2
  253.7 10.4 %all_to_all.92 = bf16[4,16,4,3,128]{4,2,1,3,0:T(4,128)(2,1)S(1)} all-to-all(bf16[4,16,4,3,128]{4,2,1,3,0:T(4,128)(2,1)S(1)} %copy.239), channel_id=1, replica_groups=mesh['layer'=4,'prow'=16,'pcol'=8] {'layer'}, dimensions={0} | all-to-all | bytes 393216 | tf_op jit(solution)/shard_map/all_to_all | solution.py:238
  264.2 17.6 %all_to_all.93 = bf16[16,4,3,128]{3,1,2,0:T(4,128)(2,1)S(1)} all-to-all(bf16[16,4,3,128]{3,1,2,0:T(4,128)(2,1)S(1)} %copy.240), channel_id=1, replica_groups=mesh['layer'=4,'prow'=16,'pcol'=8] {'prow'}, dimensions={0} | all-to-all | bytes 98304 | tf_op jit(solution)/shard_map/all_to_all | solution.py:240
  281.9 8.5 %all_to_all.94 = bf16[8,4,16,128]{3,2,1,0:T(8,128)(2,1)S(1)} all-to-all(bf16[8,4,16,128]{3,2,1,0:T(8,128)(2,1)S(1)} %broadcast_in_dim.162), channel_id=1, replica_groups=mesh['layer'=4,'prow'=16,'pcol'=8] {'pcol'}, dimensions={0} | all-to-all | bytes 262144 | tf_op jit(solution)/shard_map/all_to_all | solution.py:9
  290.5 1.5 fusion.12
  291.9 1.6 fusion.6
  294.2 3.4 all-to-all-start.14
  297.6 1.6 convolution_subtract_fusion.7
  299.2 4.5 %all-to-all-done.14 = bf16[8,4,16,128]{3,2,1,0:T(8,128)(2,1)S(1)} async-done(((bf16[8,4,16,128]{3,2,1,0:T(8,128)(2,1)}), bf16[8,4,16,128]{3,2,1,0:T(8,128)(2,1)S(1)}, u32[]{:S(2)}, u32[]{:S(2)}) %all-to-all-start.14) | async-done | bytes 131104 | tf_op jit(solution)/shard_map/all_to_all | solution.py:9
  303.7 1.5 fusion.13
  305.2 1.6 fusion.7
  306.8 8.5 %all_to_all.95 = bf16[8,4,16,128]{3,2,1,0:T(8,128)(2,1)S(1)} all-to-all(bf16[8,4,16,128]{3,2,1,0:T(8,128)(2,1)S(1)} %broadcast_in_dim.164), channel_id=1, replica_groups=mesh['layer'=4,'prow'=16,'pcol'=8] {'pcol'}, dimensions={0} | all-to-all | bytes 262144 | tf_op jit(solution)/shard_map/all_to_all | solution.py:9
  315.4 1.5 fusion.15
  317.6 4.6 %all-to-all-start.16 = ((bf16[16,3,4,256]{3,2,1,0:T(4,128)(2,1)}), bf16[16,3,4,256]{3,2,1,0:T(4,128)(2,1)S(1)}, u32[]{:S(2)}, u32[]{:S(2)}) async-start(bf16[16,3,4,256]{3,2,1,0:T(4,128)(2,1)} %broadcast_in_dim.165), calls=%async_computation.16 | async-start | bytes 196608 | tf_op jit(solution)/shard_map/all_to_all | solution.py:9
  322.1 2.3 collective-permute-start.1
  324.5 10.8 %all-to-all-done.16 = bf16[16,3,4,256]{3,2,1,0:T(4,128)(2,1)S(1)} async-done(((bf16[16,3,4,256]{3,2,1,0:T(4,128)(2,1)}), bf16[16,3,4,256]{3,2,1,0:T(4,128)(2,1)S(1)}, u32[]{:S(2)}, u32[]{:S(2)}) %all-to-all-start.16) | async-done | bytes 98336 | tf_op jit(solution)/shard_map/all_to_all | solution.py:9
  336.3 3.5 all-to-all-start.17
  340.7 0.9 copy.265
  341.6 5.4 %all-to-all-done.17 = bf16[4,16,3,4,256]{4,3,1,2,0:T(4,128)(2,1)S(1)} async-done(((bf16[4,16,3,4,256]{4,3,1,2,0:T(4,128)(2,1)}), bf16[4,16,3,4,256]{4,3,1,2,0:T(4,128)(2,1)S(1)}, u32[]{:S(2)}, u32[]{:S(2)}) %all-to-all-start.17) | async-done | bytes 393248 | tf_op jit(solution)/shard_map/all_to_all | solution.py:9
  347.3 0.9 copy.266
  (106 shorter events, 19.6 us)
Async XLA Ops:
  7.2 63.7 %copy-start.3 = (bf16[1,3,1,128,2,1,128]{6,4,5,3,2,1,0:T(2,128)(2,1)S(1)}, bf16[1,3,1,128,2,1,128]{6,4,5,3,2,1,0:T(2,128)(2,1)}, u32[]{:S(2)}) copy-start(bf16[1,3,1,128,2,1,128]{6,4,5,3,2,1,0:T(2,128)(2,1)} %param.11) | copy-start | bytes 589828
  7.2 27.1 %copy-start.4 = (s32[1,21,1,2,1]{1,4,3,2,0:T(1,128)S(1)}, s32[1,21,1,2,1]{1,4,3,2,0:T(1,128)}, u32[]{:S(2)}) copy-start(s32[1,21,1,2,1]{1,4,3,2,0:T(1,128)} %param.10) | copy-start | bytes 508
  7.2 43.4 %copy-start = (bf16[1,21,1,128,2,1,128]{6,4,5,3,2,1,0:T(2,128)(2,1)S(1)}, bf16[1,21,1,128,2,1,128]{6,4,5,3,2,1,0:T(2,128)(2,1)}, u32[]{:S(2)}) copy-start(bf16[1,21,1,128,2,1,128]{6,4,5,3,2,1,0:T(2,128)(2,1)} %param.9) | copy-start | bytes 4128772
  7.2 162.0 %all-gather.5.cloned.1.call-start = ((), (), s32[]{:S(2)}) async-start(), calls=%async_computation.18 | async-start | bytes 10027008 | tf_op jit(solution)/shard_map/all_gather | solution.py:148
  16.1 29.5 %all-to-all-start = ((bf16[16,16,256]{2,1,0:T(8,128)(2,1)}), bf16[16,16,256]{2,1,0:T(8,128)(2,1)S(1)}, u32[]{:S(2)}, u32[]{:S(2)}) async-start(bf16[16,16,256]{2,1,0:T(8,128)(2,1)} %bitcast.1), calls=%async_computation | async-start | bytes 262144 | tf_op jit(solution)/shard_map/all_to_all | solution.py:30
  31.3 259.1 %all-gather.7.cloned.1.call-start = ((), (), s32[]{:S(2)}) async-start(), calls=%async_computation.19 | async-start | bytes 6684672 | tf_op jit(solution)/shard_map/all_gather | solution.py:151
  46.3 19.3 %all-to-all-start.1 = ((bf16[16,16,256]{2,1,0:T(8,128)(2,1)}), bf16[16,16,256]{2,1,0:T(8,128)(2,1)S(1)}, u32[]{:S(2)}, u32[]{:S(2)}) async-start(bf16[16,16,256]{2,1,0:T(8,128)(2,1)} %broadcast_in_dim.139), calls=%async_computation.1 | async-start | bytes 262144 | tf_op jit(solution)/shard_map/all_to_all | solution.py:9
  66.6 14.6 %all-to-all-start.2 = ((bf16[8,128,256]{2,1,0:T(8,128)(2,1)}), bf16[8,128,256]{2,1,0:T(8,128)(2,1)S(1)}, u32[]{:S(2)}, u32[]{:S(2)}) async-start(bf16[8,128,256]{2,1,0:T(8,128)(2,1)} %broadcast_in_dim.142), calls=%async_computation.2 | async-start | bytes 1048576 | tf_op jit(solution)/shard_map/all_to_all | solution.py:9
  102.9 20.1 %all-to-all-start.4 = ((bf16[16,16,256]{2,1,0:T(8,128)(2,1)}), bf16[16,16,256]{2,1,0:T(8,128)(2,1)S(1)}, u32[]{:S(2)}, u32[]{:S(2)}) async-start(bf16[16,16,256]{2,1,0:T(8,128)(2,1)} %broadcast_in_dim.143), calls=%async_computation.4 | async-start | bytes 262144 | tf_op jit(solution)/shard_map/all_to_all | solution.py:9
  124.0 13.8 %all-to-all-start.5 = ((bf16[8,128,256]{2,1,0:T(8,128)(2,1)}), bf16[8,128,256]{2,1,0:T(8,128)(2,1)S(1)}, u32[]{:S(2)}, u32[]{:S(2)}) async-start(bf16[8,128,256]{2,1,0:T(8,128)(2,1)} %broadcast_in_dim.144), calls=%async_computation.5 | async-start | bytes 1048576 | tf_op jit(solution)/shard_map/all_to_all | solution.py:9
  139.7 29.4 %all-to-all-start.6 = ((bf16[16,16,640]{2,1,0:T(8,128)(2,1)}), bf16[16,16,640]{2,1,0:T(8,128)(2,1)S(1)}, u32[]{:S(2)}, u32[]{:S(2)}) async-start(bf16[16,16,640]{2,1,0:T(8,128)(2,1)} %pad_maximum_fusion.3), calls=%async_computation.6 | async-start | bytes 655360 | tf_op jit(solution)/shard_map/all_to_all | solution.py:189
  171.8 14.9 %all-to-all-start.7 = ((bf16[16,8,16,128]{3,2,1,0:T(8,128)(2,1)}), bf16[16,8,16,128]{3,2,1,0:T(8,128)(2,1)S(1)}, u32[]{:S(2)}, u32[]{:S(2)}) async-start(bf16[16,8,16,128]{3,2,1,0:T(8,128)(2,1)} %bitcast.28), calls=%async_computation.7 | async-start | bytes 1048576 | tf_op jit(solution)/shard_map/all_to_all | solution.py:205
  178.6 8.0 %collective-permute-start = (bf16[2,8,16,128]{3,1,2,0:T(8,128)(2,1)S(1)}, bf16[2,8,16,128]{3,1,2,0:T(8,128)(2,1)S(1)}, u32[]{:S(2)}, u32[]{:S(2)}) collective-permute-start(bf16[2,8,16,128]{3,1,2,0:T(8,128)(2,1)S(1)} %select_convert_fusion), channel_id=1, source_target_pairs={{0,128},{128,0},{256,384},{384,256},{1,129},{129,1},{257,385},{385... | collective-permute-start | bytes 196616 | tf_op jit(solution)/shard_map/ppermute | solution.py:45
  186.6 4.1 %copy-start.2 = (f32[2,8,16,128]{3,1,2,0:T(8,128)}, f32[2,8,16,128]{3,1,2,0:T(8,128)S(1)}, u32[]{:S(2)}) copy-start(f32[2,8,16,128]{3,1,2,0:T(8,128)S(1)} %convert_add_fusion) | copy-start | bytes 393220
  186.7 43.0 %copy-start.1 = (bf16[1,12,1,128,2,1,128]{6,4,5,3,2,1,0:T(2,128)(2,1)S(1)}, bf16[1,12,1,128,2,1,128]{6,4,5,3,2,1,0:T(2,128)(2,1)}, u32[]{:S(2)}) copy-start(bf16[1,12,1,128,2,1,128]{6,4,5,3,2,1,0:T(2,128)(2,1)} %param.12) | copy-start | bytes 2359300
  190.7 10.9 %all-to-all-start.8 = ((bf16[8,8,16,128]{3,2,1,0:T(8,128)(2,1)}), bf16[8,8,16,128]{3,2,1,0:T(8,128)(2,1)S(1)}, u32[]{:S(2)}, u32[]{:S(2)}) async-start(bf16[8,8,16,128]{3,2,1,0:T(8,128)(2,1)} %broadcast_in_dim.152), calls=%async_computation.8 | async-start | bytes 524288 | tf_op jit(solution)/shard_map/all_to_all | solution.py:9
  217.6 33.8 %all-to-all-start.10 = ((bf16[16,40,256]{2,1,0:T(8,128)(2,1)}), bf16[16,40,256]{2,1,0:T(8,128)(2,1)S(1)}, u32[]{:S(2)}, u32[]{:S(2)}) async-start(bf16[16,40,256]{2,1,0:T(8,128)(2,1)} %broadcast_in_dim.154), calls=%async_computation.10 | async-start | bytes 655360 | tf_op jit(solution)/shard_map/all_to_all | solution.py:9
  294.2 9.4 %all-to-all-start.14 = ((bf16[8,4,16,128]{3,2,1,0:T(8,128)(2,1)}), bf16[8,4,16,128]{3,2,1,0:T(8,128)(2,1)S(1)}, u32[]{:S(2)}, u32[]{:S(2)}) async-start(bf16[8,4,16,128]{3,2,1,0:T(8,128)(2,1)} %broadcast_in_dim.163), calls=%async_computation.14 | async-start | bytes 262144 | tf_op jit(solution)/shard_map/all_to_all | solution.py:9
  317.6 17.8 %all-to-all-start.16 = ((bf16[16,3,4,256]{3,2,1,0:T(4,128)(2,1)}), bf16[16,3,4,256]{3,2,1,0:T(4,128)(2,1)S(1)}, u32[]{:S(2)}, u32[]{:S(2)}) async-start(bf16[16,3,4,256]{3,2,1,0:T(4,128)(2,1)} %broadcast_in_dim.165), calls=%async_computation.16 | async-start | bytes 196608 | tf_op jit(solution)/shard_map/all_to_all | solution.py:9
  322.1 18.5 %collective-permute-start.1 = (bf16[16,24,256]{2,1,0:T(8,128)(2,1)S(1)}, bf16[16,24,256]{2,1,0:T(8,128)(2,1)S(1)}, u32[]{:S(2)}, u32[]{:S(2)}) collective-permute-start(bf16[16,24,256]{2,1,0:T(8,128)(2,1)S(1)} %get-tuple-element.49), channel_id=1, source_target_pairs={{0,128},{128,0},{256,384},{384,256},{1,129},{129,1},{257,385},{385... | collective-permute-start | bytes 589832 | tf_op jit(solution)/shard_map/ppermute | solution.py:45
  336.3 10.8 %all-to-all-start.17 = ((bf16[4,16,3,4,256]{4,3,1,2,0:T(4,128)(2,1)}), bf16[4,16,3,4,256]{4,3,1,2,0:T(4,128)(2,1)S(1)}, u32[]{:S(2)}, u32[]{:S(2)}) async-start(bf16[4,16,3,4,256]{4,3,1,2,0:T(4,128)(2,1)} %broadcast_in_dim.166), calls=%async_computation.17 | async-start | bytes 786432 | tf_op jit(solution)/shard_map/all_to_all | solution.py:9
Sparse Core Ops, SparseCore 0:
  16.2 150.4 all-gather.4
  169.4 98.6 all-gather.6

commit v9 on v8

--- a/solution.py
+++ b/solution.py
@@ -107,30 +107,6 @@
     own_rows = own_rhs.reshape(-1, tile_rows, rhs_width)
     first_inv = own_inverse[0, 0, 0].reshape(tile_rows, col_width)
     first_partial = inverse_product(first_inv, own_rows[0])
-    (
-        first_partial,
-        own_blocks,
-        own_pattern,
-        own_inverse,
-        pair_blocks,
-        pair_inverse,
-        root_blocks,
-        root_inverse,
-        shared_rhs,
-    ) = lax.optimization_barrier(
-        (
-            first_partial,
-            own_blocks,
-            own_pattern,
-            own_inverse,
-            pair_blocks,
-            pair_inverse,
-            root_blocks,
-            root_inverse,
-            shared_rhs,
-        )
-    )
-
     own_inv = own_inverse.reshape(-1, tile_rows, col_width)
     own_tiles = own_blocks.reshape(-1, tile_rows, cycles, tile_rows)
     kept_tiles = own_pattern.reshape(-1, 1, cycles, 1) > 0

time: 357 us -> 358 us (level)
  blocking collectives: 74.8 us -> 89.8 us
  waiting for transfers between devices: 132 us -> 122 us
  starting transfers between devices: 71.4 us -> 67.7 us
    all_to_all x3 -> x4, blocking collectives: 27 us -> 41.5 us  [shared_with_all(): return lax.all_to_all(copies, axis, 0, 0)]
    all_to_all x9 -> x8, waiting for transfers between devices: 92.2 us -> 81.7 us  [shared_with_all(): return lax.all_to_all(copies, axis, 0, 0)]
    all_to_all x9 -> x8, starting transfers between devices: 41.5 us -> 37.5 us  [shared_with_all(): return lax.all_to_all(copies, axis, 0, 0)]
  transfers between devices with their start and end apart: 16 -> 15, of which waited for: 12 -> 11; matrix products, arithmetic and copies ran while one was open for 12% -> 13% of each run, Pallas kernels for 0% -> 0%
where the time goes in v9:
time: 358 us; the launch traced here: 356 us
  waiting for transfers between devices  122 us (34%)
  blocking collectives  89.8 us (25%)
  starting transfers between devices  67.7 us (19%)
  matrix products  30.2 us (8%)
  local copies, waits for them, and re-layouts  24.3 us (7%)
  between operations  14.7 us (4%)
  other arithmetic  6.71 us (2%)
    all_to_all x8, waiting for transfers between devices, shared_with_all(): return lax.all_to_all(copies, axis, 0, 0)  81.7 us
    all_to_all x4, blocking collectives, shared_with_all(): return lax.all_to_all(copies, axis, 0, 0)  41.5 us
    all_to_all x8, starting transfers between devices, shared_with_all(): return lax.all_to_all(copies, axis, 0, 0)  37.5 us
    all_to_all x1, waiting for transfers between devices, local(): received = lax.all_to_all(pieces, 'prow', 0, 0)  24.4 us
    all_to_all x1, blocking collectives, column_total(): received = lax.all_to_all(pieces, 'prow', 0, 0)  20 us
    all_to_all x1, blocking collectives, local(): received = lax.all_to_all(pieces, 'prow', 0, 0)  17.6 us
    dot_general x13, matrix products, transposed_product(): lax.dot_general(solved, blocks, (((solved.ndim - 1,), (blocks.ndim - 1,))...  16.3 us
    all_to_all x1, starting transfers between devices, column_total(): received = lax.all_to_all(pieces, 'prow', 0, 0)  15.2 us
  transfers between devices with their start and end apart: 15, of which 11 were waited for; matrix products, arithmetic and copies ran while one was open for 13% of the time, Pallas kernels for 0%

profile of v9, /device:TPU:32, one launch (start us, length us, event | category | flops | bytes accessed | tf_op | source)
XLA Modules:
  0.0 355.5 jit_solution(13033236085779744144)
XLA Ops:
  7.2 1.1 slice.210
  8.3 0.9 slice.212
  9.2 1.1 slice.215
  11.4 1.1 reshape.185
  12.5 0.9 pad_maximum_fusion
  13.4 1.7 fusion.75
  15.1 1.7 convolution_convert_fusion.2
  16.8 15.2 %all-to-all-start = ((bf16[16,16,256]{2,1,0:T(8,128)(2,1)}), bf16[16,16,256]{2,1,0:T(8,128)(2,1)S(1)}, u32[]{:S(2)}, u32[]{:S(2)}) async-start(bf16[16,16,256]{2,1,0:T(8,128)(2,1)} %bitcast.1), calls=%async_computation | async-start | bytes 262144 | tf_op jit(solution)/shard_map/all_to_all | solution.py:30
  32.1 1.1 reshape.193
  33.1 1.1 reshape.194
  35.1 11.8 %all-to-all-done = bf16[16,16,256]{2,1,0:T(8,128)(2,1)S(1)} async-done(((bf16[16,16,256]{2,1,0:T(8,128)(2,1)}), bf16[16,16,256]{2,1,0:T(8,128)(2,1)S(1)}, u32[]{:S(2)}, u32[]{:S(2)}) %all-to-all-start) | async-done | bytes 131104 | tf_op jit(solution)/shard_map/all_to_all | solution.py:30
  47.6 4.7 %all-to-all-start.1 = ((bf16[16,16,256]{2,1,0:T(8,128)(2,1)}), bf16[16,16,256]{2,1,0:T(8,128)(2,1)S(1)}, u32[]{:S(2)}, u32[]{:S(2)}) async-start(bf16[16,16,256]{2,1,0:T(8,128)(2,1)} %broadcast_in_dim.139), calls=%async_computation.1 | async-start | bytes 262144 | tf_op jit(solution)/shard_map/all_to_all | solution.py:9
  52.4 1.2 broadcast_select_fusion
  53.7 13.0 %all-to-all-done.1 = bf16[16,16,256]{2,1,0:T(8,128)(2,1)S(1)} async-done(((bf16[16,16,256]{2,1,0:T(8,128)(2,1)}), bf16[16,16,256]{2,1,0:T(8,128)(2,1)S(1)}, u32[]{:S(2)}, u32[]{:S(2)}) %all-to-all-start.1) | async-done | bytes 131104 | tf_op jit(solution)/shard_map/all_to_all | solution.py:9
  67.0 14.6 %all_to_all.90 = bf16[8,128,256]{2,1,0:T(8,128)(2,1)S(1)} all-to-all(bf16[8,128,256]{2,1,0:T(8,128)(2,1)S(1)} %broadcast_in_dim.142), channel_id=1, replica_groups=mesh['layer'=4,'prow'=16,'pcol'=8] {'pcol'}, dimensions={0} | all-to-all | bytes 1048576 | tf_op jit(solution)/shard_map/all_to_all | solution.py:9
  81.6 1.1 convolution_convert_fusion.1
  82.7 20.0 %all_to_all.91 = bf16[16,16,256]{2,1,0:T(8,128)(2,1)S(1)} all-to-all(bf16[16,16,256]{2,1,0:T(8,128)(2,1)S(1)} %bitcast.381), channel_id=1, replica_groups=mesh['layer'=4,'prow'=16,'pcol'=8] {'prow'}, dimensions={0} | all-to-all | bytes 262144 | tf_op jit(solution)/shard_map/all_to_all | solution.py:30
  103.4 5.0 %all-to-all-start.4 = ((bf16[16,16,256]{2,1,0:T(8,128)(2,1)}), bf16[16,16,256]{2,1,0:T(8,128)(2,1)S(1)}, u32[]{:S(2)}, u32[]{:S(2)}) async-start(bf16[16,16,256]{2,1,0:T(8,128)(2,1)} %broadcast_in_dim.143), calls=%async_computation.4 | async-start | bytes 262144 | tf_op jit(solution)/shard_map/all_to_all | solution.py:9
  109.3 1.2 copy.211
  111.0 12.3 %all-to-all-done.4 = bf16[16,16,256]{2,1,0:T(8,128)(2,1)S(1)} async-done(((bf16[16,16,256]{2,1,0:T(8,128)(2,1)}), bf16[16,16,256]{2,1,0:T(8,128)(2,1)S(1)}, u32[]{:S(2)}, u32[]{:S(2)}) %all-to-all-start.4) | async-done | bytes 131104 | tf_op jit(solution)/shard_map/all_to_all | solution.py:9
  124.3 3.5 all-to-all-start.5
  128.8 9.2 %all-to-all-done.5 = bf16[8,128,256]{2,1,0:T(8,128)(2,1)S(1)} async-done(((bf16[8,128,256]{2,1,0:T(8,128)(2,1)}), bf16[8,128,256]{2,1,0:T(8,128)(2,1)S(1)}, u32[]{:S(2)}, u32[]{:S(2)}) %all-to-all-start.5) | async-done | bytes 524320 | tf_op jit(solution)/shard_map/all_to_all | solution.py:9
  138.2 1.1 convolution_convert_fusion
  140.0 5.0 %all-to-all-start.6 = ((bf16[16,16,640]{2,1,0:T(8,128)(2,1)}), bf16[16,16,640]{2,1,0:T(8,128)(2,1)S(1)}, u32[]{:S(2)}, u32[]{:S(2)}) async-start(bf16[16,16,640]{2,1,0:T(8,128)(2,1)} %pad_maximum_fusion.3), calls=%async_computation.6 | async-start | bytes 655360 | tf_op jit(solution)/shard_map/all_to_all | solution.py:165
  145.0 24.4 %all-to-all-done.6 = bf16[16,16,640]{2,1,0:T(8,128)(2,1)S(1)} async-done(((bf16[16,16,640]{2,1,0:T(8,128)(2,1)}), bf16[16,16,640]{2,1,0:T(8,128)(2,1)S(1)}, u32[]{:S(2)}, u32[]{:S(2)}) %all-to-all-start.6) | async-done | bytes 327712 | tf_op jit(solution)/shard_map/all_to_all | solution.py:165
  169.5 1.6 fusion.5
  171.1 0.9 broadcast_in_dim.151
  172.0 3.6 %all-to-all-start.7 = ((bf16[16,8,16,128]{3,2,1,0:T(8,128)(2,1)}), bf16[16,8,16,128]{3,2,1,0:T(8,128)(2,1)S(1)}, u32[]{:S(2)}, u32[]{:S(2)}) async-start(bf16[16,8,16,128]{3,2,1,0:T(8,128)(2,1)} %bitcast.29), calls=%async_computation.7 | async-start | bytes 1048576 | tf_op jit(solution)/shard_map/all_to_all | solution.py:181
  175.7 1.6 fusion.2
  177.3 1.6 fusion.1
  178.9 3.8 %collective-permute-start = (bf16[2,8,16,128]{3,1,2,0:T(8,128)(2,1)S(1)}, bf16[2,8,16,128]{3,1,2,0:T(8,128)(2,1)S(1)}, u32[]{:S(2)}, u32[]{:S(2)}) collective-permute-start(bf16[2,8,16,128]{3,1,2,0:T(8,128)(2,1)S(1)} %select_convert_fusion), channel_id=1, source_target_pairs={{0,128},{128,0},{256,384},{384,256},{1,129},{129,1},{257,385},{385... | collective-permute-start | bytes 196616 | tf_op jit(solution)/shard_map/ppermute | solution.py:45
  182.8 4.2 %collective-permute-done = bf16[2,8,16,128]{3,1,2,0:T(8,128)(2,1)S(1)} collective-permute-done((bf16[2,8,16,128]{3,1,2,0:T(8,128)(2,1)S(1)}, bf16[2,8,16,128]{3,1,2,0:T(8,128)(2,1)S(1)}, u32[]{:S(2)}, u32[]{:S(2)}) %collective-permute-start) | collective-permute-done | bytes 65568 | tf_op jit(solution)/shard_map/ppermute | solution.py:45
  187.1 1.5 fusion.8
  188.6 1.6 fusion.47
  191.0 3.4 all-to-all-start.8
  194.5 1.6 fusion.17
  196.1 5.8 %all-to-all-done.8 = bf16[8,8,16,128]{3,2,1,0:T(8,128)(2,1)S(1)} async-done(((bf16[8,8,16,128]{3,2,1,0:T(8,128)(2,1)}), bf16[8,8,16,128]{3,2,1,0:T(8,128)(2,1)S(1)}, u32[]{:S(2)}, u32[]{:S(2)}) %all-to-all-start.8) | async-done | bytes 262176 | tf_op jit(solution)/shard_map/all_to_all | solution.py:9
  202.6 1.5 fusion.9
  204.1 1.6 fusion.45
  205.7 9.9 %all_to_all.92 = bf16[8,8,16,128]{3,2,1,0:T(8,128)(2,1)S(1)} all-to-all(bf16[8,8,16,128]{3,2,1,0:T(8,128)(2,1)S(1)} %broadcast_in_dim.153), channel_id=1, replica_groups=mesh['layer'=4,'prow'=16,'pcol'=8] {'pcol'}, dimensions={0} | all-to-all | bytes 524288 | tf_op jit(solution)/shard_map/all_to_all | solution.py:9
  215.7 1.5 fusion.11
  218.0 9.5 %all-to-all-start.10 = ((bf16[16,40,256]{2,1,0:T(8,128)(2,1)}), bf16[16,40,256]{2,1,0:T(8,128)(2,1)S(1)}, u32[]{:S(2)}, u32[]{:S(2)}) async-start(bf16[16,40,256]{2,1,0:T(8,128)(2,1)} %broadcast_in_dim.154), calls=%async_computation.10 | async-start | bytes 655360 | tf_op jit(solution)/shard_map/all_to_all | solution.py:9
  228.3 1.7 slice.233
  231.1 20.7 %all-to-all-done.10 = bf16[16,40,256]{2,1,0:T(8,128)(2,1)S(1)} async-done(((bf16[16,40,256]{2,1,0:T(8,128)(2,1)}), bf16[16,40,256]{2,1,0:T(8,128)(2,1)S(1)}, u32[]{:S(2)}, u32[]{:S(2)}) %all-to-all-start.10) | async-done | bytes 327712 | tf_op jit(solution)/shard_map/all_to_all | solution.py:9
  252.6 1.2 convolution_subtract_fusion.2
  254.1 10.6 %all_to_all.93 = bf16[4,16,4,3,128]{4,2,1,3,0:T(4,128)(2,1)S(1)} all-to-all(bf16[4,16,4,3,128]{4,2,1,3,0:T(4,128)(2,1)S(1)} %copy.239), channel_id=1, replica_groups=mesh['layer'=4,'prow'=16,'pcol'=8] {'layer'}, dimensions={0} | all-to-all | bytes 393216 | tf_op jit(solution)/shard_map/all_to_all | solution.py:214
  264.8 17.6 %all_to_all.94 = bf16[16,4,3,128]{3,1,2,0:T(4,128)(2,1)S(1)} all-to-all(bf16[16,4,3,128]{3,1,2,0:T(4,128)(2,1)S(1)} %copy.240), channel_id=1, replica_groups=mesh['layer'=4,'prow'=16,'pcol'=8] {'prow'}, dimensions={0} | all-to-all | bytes 98304 | tf_op jit(solution)/shard_map/all_to_all | solution.py:216
  282.5 8.5 %all_to_all.95 = bf16[8,4,16,128]{3,2,1,0:T(8,128)(2,1)S(1)} all-to-all(bf16[8,4,16,128]{3,2,1,0:T(8,128)(2,1)S(1)} %broadcast_in_dim.162), channel_id=1, replica_groups=mesh['layer'=4,'prow'=16,'pcol'=8] {'pcol'}, dimensions={0} | all-to-all | bytes 262144 | tf_op jit(solution)/shard_map/all_to_all | solution.py:9
  291.0 1.5 fusion.12
  292.5 1.6 fusion.6
  294.8 3.4 all-to-all-start.14
  298.2 1.6 convolution_subtract_fusion.7
  299.8 4.5 %all-to-all-done.14 = bf16[8,4,16,128]{3,2,1,0:T(8,128)(2,1)S(1)} async-done(((bf16[8,4,16,128]{3,2,1,0:T(8,128)(2,1)}), bf16[8,4,16,128]{3,2,1,0:T(8,128)(2,1)S(1)}, u32[]{:S(2)}, u32[]{:S(2)}) %all-to-all-start.14) | async-done | bytes 131104 | tf_op jit(solution)/shard_map/all_to_all | solution.py:9
  304.3 1.5 fusion.13
  305.8 1.6 fusion.7
  307.4 8.5 %all_to_all.96 = bf16[8,4,16,128]{3,2,1,0:T(8,128)(2,1)S(1)} all-to-all(bf16[8,4,16,128]{3,2,1,0:T(8,128)(2,1)S(1)} %broadcast_in_dim.164), channel_id=1, replica_groups=mesh['layer'=4,'prow'=16,'pcol'=8] {'pcol'}, dimensions={0} | all-to-all | bytes 262144 | tf_op jit(solution)/shard_map/all_to_all | solution.py:9
  316.0 1.5 fusion.15
  318.1 4.5 %all-to-all-start.16 = ((bf16[16,3,4,256]{3,2,1,0:T(4,128)(2,1)}), bf16[16,3,4,256]{3,2,1,0:T(4,128)(2,1)S(1)}, u32[]{:S(2)}, u32[]{:S(2)}) async-start(bf16[16,3,4,256]{3,2,1,0:T(4,128)(2,1)} %broadcast_in_dim.165), calls=%async_computation.16 | async-start | bytes 196608 | tf_op jit(solution)/shard_map/all_to_all | solution.py:9
  322.6 2.5 collective-permute-start.1
  325.1 10.7 %all-to-all-done.16 = bf16[16,3,4,256]{3,2,1,0:T(4,128)(2,1)S(1)} async-done(((bf16[16,3,4,256]{3,2,1,0:T(4,128)(2,1)}), bf16[16,3,4,256]{3,2,1,0:T(4,128)(2,1)S(1)}, u32[]{:S(2)}, u32[]{:S(2)}) %all-to-all-start.16) | async-done | bytes 98336 | tf_op jit(solution)/shard_map/all_to_all | solution.py:9
  336.7 3.5 all-to-all-start.17
  341.2 0.9 copy.265
  342.1 5.4 %all-to-all-done.17 = bf16[4,16,3,4,256]{4,3,1,2,0:T(4,128)(2,1)S(1)} async-done(((bf16[4,16,3,4,256]{4,3,1,2,0:T(4,128)(2,1)}), bf16[4,16,3,4,256]{4,3,1,2,0:T(4,128)(2,1)S(1)}, u32[]{:S(2)}, u32[]{:S(2)}) %all-to-all-start.17) | async-done | bytes 393248 | tf_op jit(solution)/shard_map/all_to_all | solution.py:9
  347.8 0.9 copy.266
  (102 shorter events, 17.2 us)
Async XLA Ops:
  7.2 45.2 %copy-start = (bf16[1,21,1,128,2,1,128]{6,4,5,3,2,1,0:T(2,128)(2,1)S(1)}, bf16[1,21,1,128,2,1,128]{6,4,5,3,2,1,0:T(2,128)(2,1)}, u32[]{:S(2)}) copy-start(bf16[1,21,1,128,2,1,128]{6,4,5,3,2,1,0:T(2,128)(2,1)} %param.9) | copy-start | bytes 4128772
  7.2 27.8 %copy-start.3 = (s32[1,21,1,2,1]{1,4,3,2,0:T(1,128)S(1)}, s32[1,21,1,2,1]{1,4,3,2,0:T(1,128)}, u32[]{:S(2)}) copy-start(s32[1,21,1,2,1]{1,4,3,2,0:T(1,128)} %param.10) | copy-start | bytes 508
  7.2 162.3 %all-gather.5.cloned.1.call-start = ((), (), s32[]{:S(2)}) async-start(), calls=%async_computation.18 | async-start | bytes 10027008 | tf_op jit(solution)/shard_map/all_gather | solution.py:124
  16.8 30.1 %all-to-all-start = ((bf16[16,16,256]{2,1,0:T(8,128)(2,1)}), bf16[16,16,256]{2,1,0:T(8,128)(2,1)S(1)}, u32[]{:S(2)}, u32[]{:S(2)}) async-start(bf16[16,16,256]{2,1,0:T(8,128)(2,1)} %bitcast.1), calls=%async_computation | async-start | bytes 262144 | tf_op jit(solution)/shard_map/all_to_all | solution.py:30
  32.0 259.0 %all-gather.7.cloned.1.call-start = ((), (), s32[]{:S(2)}) async-start(), calls=%async_computation.19 | async-start | bytes 6684672 | tf_op jit(solution)/shard_map/all_gather | solution.py:127
  47.6 19.1 %all-to-all-start.1 = ((bf16[16,16,256]{2,1,0:T(8,128)(2,1)}), bf16[16,16,256]{2,1,0:T(8,128)(2,1)S(1)}, u32[]{:S(2)}, u32[]{:S(2)}) async-start(bf16[16,16,256]{2,1,0:T(8,128)(2,1)} %broadcast_in_dim.139), calls=%async_computation.1 | async-start | bytes 262144 | tf_op jit(solution)/shard_map/all_to_all | solution.py:9
  103.4 19.9 %all-to-all-start.4 = ((bf16[16,16,256]{2,1,0:T(8,128)(2,1)}), bf16[16,16,256]{2,1,0:T(8,128)(2,1)S(1)}, u32[]{:S(2)}, u32[]{:S(2)}) async-start(bf16[16,16,256]{2,1,0:T(8,128)(2,1)} %broadcast_in_dim.143), calls=%async_computation.4 | async-start | bytes 262144 | tf_op jit(solution)/shard_map/all_to_all | solution.py:9
  124.3 13.8 %all-to-all-start.5 = ((bf16[8,128,256]{2,1,0:T(8,128)(2,1)}), bf16[8,128,256]{2,1,0:T(8,128)(2,1)S(1)}, u32[]{:S(2)}, u32[]{:S(2)}) async-start(bf16[8,128,256]{2,1,0:T(8,128)(2,1)} %broadcast_in_dim.144), calls=%async_computation.5 | async-start | bytes 1048576 | tf_op jit(solution)/shard_map/all_to_all | solution.py:9
  140.0 29.4 %all-to-all-start.6 = ((bf16[16,16,640]{2,1,0:T(8,128)(2,1)}), bf16[16,16,640]{2,1,0:T(8,128)(2,1)S(1)}, u32[]{:S(2)}, u32[]{:S(2)}) async-start(bf16[16,16,640]{2,1,0:T(8,128)(2,1)} %pad_maximum_fusion.3), calls=%async_computation.6 | async-start | bytes 655360 | tf_op jit(solution)/shard_map/all_to_all | solution.py:165
  172.0 15.0 %all-to-all-start.7 = ((bf16[16,8,16,128]{3,2,1,0:T(8,128)(2,1)}), bf16[16,8,16,128]{3,2,1,0:T(8,128)(2,1)S(1)}, u32[]{:S(2)}, u32[]{:S(2)}) async-start(bf16[16,8,16,128]{3,2,1,0:T(8,128)(2,1)} %bitcast.29), calls=%async_computation.7 | async-start | bytes 1048576 | tf_op jit(solution)/shard_map/all_to_all | solution.py:181
  178.9 8.0 %collective-permute-start = (bf16[2,8,16,128]{3,1,2,0:T(8,128)(2,1)S(1)}, bf16[2,8,16,128]{3,1,2,0:T(8,128)(2,1)S(1)}, u32[]{:S(2)}, u32[]{:S(2)}) collective-permute-start(bf16[2,8,16,128]{3,1,2,0:T(8,128)(2,1)S(1)} %select_convert_fusion), channel_id=1, source_target_pairs={{0,128},{128,0},{256,384},{384,256},{1,129},{129,1},{257,385},{385... | collective-permute-start | bytes 196616 | tf_op jit(solution)/shard_map/ppermute | solution.py:45
  187.0 4.1 %copy-start.2 = (f32[2,8,16,128]{3,1,2,0:T(8,128)}, f32[2,8,16,128]{3,1,2,0:T(8,128)S(1)}, u32[]{:S(2)}) copy-start(f32[2,8,16,128]{3,1,2,0:T(8,128)S(1)} %convert_add_fusion) | copy-start | bytes 393220
  187.1 43.0 %copy-start.1 = (bf16[1,12,1,128,2,1,128]{6,4,5,3,2,1,0:T(2,128)(2,1)S(1)}, bf16[1,12,1,128,2,1,128]{6,4,5,3,2,1,0:T(2,128)(2,1)}, u32[]{:S(2)}) copy-start(bf16[1,12,1,128,2,1,128]{6,4,5,3,2,1,0:T(2,128)(2,1)} %param.12) | copy-start | bytes 2359300
  191.0 10.9 %all-to-all-start.8 = ((bf16[8,8,16,128]{3,2,1,0:T(8,128)(2,1)}), bf16[8,8,16,128]{3,2,1,0:T(8,128)(2,1)S(1)}, u32[]{:S(2)}, u32[]{:S(2)}) async-start(bf16[8,8,16,128]{3,2,1,0:T(8,128)(2,1)} %broadcast_in_dim.152), calls=%async_computation.8 | async-start | bytes 524288 | tf_op jit(solution)/shard_map/all_to_all | solution.py:9
  218.0 33.8 %all-to-all-start.10 = ((bf16[16,40,256]{2,1,0:T(8,128)(2,1)}), bf16[16,40,256]{2,1,0:T(8,128)(2,1)S(1)}, u32[]{:S(2)}, u32[]{:S(2)}) async-start(bf16[16,40,256]{2,1,0:T(8,128)(2,1)} %broadcast_in_dim.154), calls=%async_computation.10 | async-start | bytes 655360 | tf_op jit(solution)/shard_map/all_to_all | solution.py:9
  294.8 9.4 %all-to-all-start.14 = ((bf16[8,4,16,128]{3,2,1,0:T(8,128)(2,1)}), bf16[8,4,16,128]{3,2,1,0:T(8,128)(2,1)S(1)}, u32[]{:S(2)}, u32[]{:S(2)}) async-start(bf16[8,4,16,128]{3,2,1,0:T(8,128)(2,1)} %broadcast_in_dim.163), calls=%async_computation.14 | async-start | bytes 262144 | tf_op jit(solution)/shard_map/all_to_all | solution.py:9
  318.1 17.7 %all-to-all-start.16 = ((bf16[16,3,4,256]{3,2,1,0:T(4,128)(2,1)}), bf16[16,3,4,256]{3,2,1,0:T(4,128)(2,1)S(1)}, u32[]{:S(2)}, u32[]{:S(2)}) async-start(bf16[16,3,4,256]{3,2,1,0:T(4,128)(2,1)} %broadcast_in_dim.165), calls=%async_computation.16 | async-start | bytes 196608 | tf_op jit(solution)/shard_map/all_to_all | solution.py:9
  322.6 18.5 %collective-permute-start.1 = (bf16[16,24,256]{2,1,0:T(8,128)(2,1)S(1)}, bf16[16,24,256]{2,1,0:T(8,128)(2,1)S(1)}, u32[]{:S(2)}, u32[]{:S(2)}) collective-permute-start(bf16[16,24,256]{2,1,0:T(8,128)(2,1)S(1)} %get-tuple-element.31), channel_id=1, source_target_pairs={{0,128},{128,0},{256,384},{384,256},{1,129},{129,1},{257,385},{385... | collective-permute-start | bytes 589832 | tf_op jit(solution)/shard_map/ppermute | solution.py:45
  336.7 10.8 %all-to-all-start.17 = ((bf16[4,16,3,4,256]{4,3,1,2,0:T(4,128)(2,1)}), bf16[4,16,3,4,256]{4,3,1,2,0:T(4,128)(2,1)S(1)}, u32[]{:S(2)}, u32[]{:S(2)}) async-start(bf16[4,16,3,4,256]{4,3,1,2,0:T(4,128)(2,1)} %broadcast_in_dim.166), calls=%async_computation.17 | async-start | bytes 786432 | tf_op jit(solution)/shard_map/all_to_all | solution.py:9
Sparse Core Ops, SparseCore 0:
  13.5 152.4 all-gather.4
  168.7 99.7 all-gather.6
